TPU v7x, 32 devices: a whole 2x2x4 slice. The times are simulated.
32 devices in a mesh: dp: 8 (over z, x), tensor: 4 (over y, core).
Axes of the slice: x: 2, y: 2, z: 4, core: 2. Of those that a mesh axis runs over, the one named last changes fastest.
Arguments:
- inputs: bfloat16 [16384, 1536], P(('dp', 'tensor')), may hold values from -6 to 6
- cotangent: bfloat16 [16384, 1536], P(('dp', 'tensor')), may hold values from -6 to 6
- picture_start: int32 [16], P('dp'), may hold values from 0 to 768, as said below
- picture_length: int32 [16], P('dp'), may hold values from 256 to 512, as said below
- qkvg_weight: float32 [4, 1536, 1536], P(None, 'dp', 'tensor'), may hold values from -0.15625 to 0.15625
- forget_weight: float32 [1536, 24], P('dp', 'tensor'), may hold values from -0.15625 to 0.15625
- forget_bias: float32 [24], replicated, may hold values from 1 to 7
- out_weight: float32 [1536, 1536], P('tensor', 'dp'), may hold values from -0.875 to 0.875
- gate_up: float32 [2, 1536, 4096], P(None, 'dp', 'tensor'), may hold values from -0.15625 to 0.15625
- down_weight: float32 [4096, 1536], P('tensor', 'dp'), may hold values from -0.09375 to 0.09375
- attn_gain: float32 [1536], replicated, may hold values from 0.5 to 1.5
- feed_gain: float32 [1536], replicated, may hold values from 0.5 to 1.5
- qkvg_first: float32 [4, 1536, 1536], P(None, 'dp', 'tensor'), may hold values from -0.000119096316 to 0.000119096316
- qkvg_second: float32 [4, 1536, 1536], P(None, 'dp', 'tensor'), may hold values from 1.7257769e-09 to 6.8379835e-09
- forget_first: float32 [1536, 24], P('dp', 'tensor'), may hold values from -0.000119096316 to 0.000119096316
- forget_second: float32 [1536, 24], P('dp', 'tensor'), may hold values from 1.7257769e-09 to 6.8379835e-09
- bias_first: float32 [24], replicated, may hold values from -0.000119096316 to 0.000119096316
- bias_second: float32 [24], replicated, may hold values from 1.7257769e-09 to 6.8379835e-09
- out_first: float32 [1536, 1536], P('tensor', 'dp'), may hold values from -0.000119096316 to 0.000119096316
- out_second: float32 [1536, 1536], P('tensor', 'dp'), may hold values from 1.7257769e-09 to 6.8379835e-09
- gateup_first: float32 [2, 1536, 4096], P(None, 'dp', 'tensor'), may hold values from -0.000119096316 to 0.000119096316
- gateup_second: float32 [2, 1536, 4096], P(None, 'dp', 'tensor'), may hold values from 1.7257769e-09 to 6.8379835e-09
- down_first: float32 [4096, 1536], P('tensor', 'dp'), may hold values from -0.000119096316 to 0.000119096316
- down_second: float32 [4096, 1536], P('tensor', 'dp'), may hold values from 1.7257769e-09 to 6.8379835e-09
- attngain_first: float32 [1536], replicated, may hold values from -0.000119096316 to 0.000119096316
- attngain_second: float32 [1536], replicated, may hold values from 1.7257769e-09 to 6.8379835e-09
- feedgain_first: float32 [1536], replicated, may hold values from -0.000119096316 to 0.000119096316
- feedgain_second: float32 [1536], replicated, may hold values from 1.7257769e-09 to 6.8379835e-09
Outputs:
- outputs: float32 [16384, 1536], P(('dp', 'tensor'))
- input_grad: float32 [16384, 1536], P(('dp', 'tensor'))
- grad_norm: float32 [], replicated
- qkvg_update: float32 [4, 1536, 1536], P(None, 'dp', 'tensor')
- qkvg_mean: float32 [4, 1536, 1536], P(None, 'dp', 'tensor')
- qkvg_meansq: float32 [4, 1536, 1536], P(None, 'dp', 'tensor')
- forget_update: float32 [1536, 24], P('dp', 'tensor')
- forget_mean: float32 [1536, 24], P('dp', 'tensor')
- forget_meansq: float32 [1536, 24], P('dp', 'tensor')
- bias_update: float32 [24], replicated
- bias_mean: float32 [24], replicated
- bias_meansq: float32 [24], replicated
- out_update: float32 [1536, 1536], P('tensor', 'dp')
- out_mean: float32 [1536, 1536], P('tensor', 'dp')
- out_meansq: float32 [1536, 1536], P('tensor', 'dp')
- gateup_update: float32 [2, 1536, 4096], P(None, 'dp', 'tensor')
- gateup_mean: float32 [2, 1536, 4096], P(None, 'dp', 'tensor')
- gateup_meansq: float32 [2, 1536, 4096], P(None, 'dp', 'tensor')
- down_update: float32 [4096, 1536], P('tensor', 'dp')
- down_mean: float32 [4096, 1536], P('tensor', 'dp')
- down_meansq: float32 [4096, 1536], P('tensor', 'dp')
- attngain_update: float32 [1536], replicated
- attngain_mean: float32 [1536], replicated
- attngain_meansq: float32 [1536], replicated
- feedgain_update: float32 [1536], replicated
- feedgain_mean: float32 [1536], replicated
- feedgain_meansq: float32 [1536], replicated
Inputs may be any that keep to these rules, and one draw needn't show every extreme that they name: `picture_start`: a multiple of 256; picture_start + picture_length <= 1024. `picture_length`: a multiple of 256.
All inputs are finite; a program needn't handle non-finite values.
Results may differ from a plain program's by a relative error of at most 0.029.
Values may be sent and summed in bfloat16 or wider, within the bound.
No kernel may reach another device: no remote copies, remote signals or barrier semaphores. Data moves between devices by JAX's collectives and lax.ppermute only.
A program may use at most 168 MiB of HBM per device.

v0:
```python
import jax
import jax.numpy as jnp
from jax import lax
from jax.sharding import PartitionSpec as P

D = 1536
HEAD_DIM = 64


MASK_FILL = -1000000000.0
NORM_EPS = 1e-05
BETA_ONE = 0.9
BETA_TWO = 0.95
WEIGHT_DECAY = 0.1
ADAM_EPS = 1e-08
MAX_NORM = 1.0
STEP_COUNT = 10.0


def rms_scale(values):
    return lax.rsqrt(jnp.mean(values * values, axis=-1, keepdims=True) + NORM_EPS)


def norm_back(gradient, values, inv_scale, gain_row):
    normed = values * inv_scale
    scaled = gradient * gain_row
    backward = inv_scale * (scaled - normed * jnp.mean(scaled * normed, axis=-1, keepdims=True))
    return (backward, jnp.sum(gradient * normed, axis=0))


def mask_layout(pic_first, pic_size, positions):
    places = jnp.arange(positions)
    causal = places[None, :] <= places[:, None]
    inside = (places >= pic_first) & (places < pic_first + pic_size)
    allowed = causal | inside[:, None] & inside[None, :]
    return (allowed, jnp.where(causal, 1.0, -1.0).astype(jnp.float32))


def scores_of(queries, key_rows, decay_sum, pic_first, pic_size):
    allowed, orient = mask_layout(pic_first, pic_size, queries.shape[0])
    raw_scores = jnp.einsum(
        "ihe,jhe->hij", queries, key_rows, preferred_element_type=jnp.float32
    ) * HEAD_DIM ** (-0.5)
    cumulative = decay_sum.T
    shifted = raw_scores + orient[None] * (cumulative[:, :, None] - cumulative[:, None, :])
    return (jnp.where(allowed[None], shifted, MASK_FILL), orient)


def sequence_forward(members):
    queries, key_rows, values, decay_sum, pic_first, pic_size = members
    scores, orient = scores_of(queries, key_rows, decay_sum, pic_first, pic_size)
    row_peak = jnp.max(scores, axis=-1, keepdims=True)
    exponent = jnp.exp(scores - row_peak)
    row_total = jnp.sum(exponent, axis=-1, keepdims=True)
    probability = (exponent / row_total).astype(jnp.bfloat16)
    mixture = jnp.einsum("hij,jhe->ihe", probability, values, preferred_element_type=jnp.float32)
    return (mixture, (row_peak + jnp.log(row_total))[:, :, 0])


def sequence_backward(members):
    queries, key_rows, values, decay_sum, pic_first, pic_size, log_total, upstream = members
    scores, orient = scores_of(queries, key_rows, decay_sum, pic_first, pic_size)
    probability = jnp.exp(scores - log_total[:, :, None])
    grad_values = jnp.einsum(
        "hij,ihe->jhe",
        probability.astype(jnp.bfloat16),
        upstream,
        preferred_element_type=jnp.float32,
    )
    grad_probs = jnp.einsum("ihe,jhe->hij", upstream, values, preferred_element_type=jnp.float32)
    row_dot = jnp.sum(probability * grad_probs, axis=-1, keepdims=True)
    grad_scores = (probability * (grad_probs - row_dot)).astype(jnp.bfloat16)
    grad_queries = jnp.einsum(
        "hij,jhe->ihe", grad_scores, key_rows, preferred_element_type=jnp.float32
    ) * HEAD_DIM ** (-0.5)
    grad_keys = jnp.einsum(
        "hij,ihe->jhe", grad_scores, queries, preferred_element_type=jnp.float32
    ) * HEAD_DIM ** (-0.5)
    signed = grad_scores.astype(jnp.float32) * orient[None]
    grad_decay = (jnp.sum(signed, axis=2) - jnp.sum(signed, axis=1)).T
    return (grad_queries, grad_keys, grad_values, grad_decay)


def gather_rows(normed):
    return lax.all_gather(normed, "tensor", axis=0, tiled=True)


def spread_rows(partial_sum):
    return lax.psum_scatter(
        partial_sum.astype(jnp.bfloat16), "tensor", scatter_dimension=0, tiled=True
    ).astype(jnp.float32)


def fetch_back(normed, grad_low):
    return (
        lax.all_gather(normed, "tensor", axis=0, tiled=True),
        lax.all_gather(grad_low, "tensor", axis=0, tiled=True),
    )


def adam_step(weight, gradient, first_old, second_old, clip_scale, decay_rate):
    learn_rate = 0.4 / D**0.5
    scaled = gradient * clip_scale
    first_new = BETA_ONE * first_old + (1.0 - BETA_ONE) * scaled
    second_new = BETA_TWO * second_old + (1.0 - BETA_TWO) * scaled * scaled
    update = (
        first_new
        / (1.0 - BETA_ONE**STEP_COUNT)
        / (jnp.sqrt(second_new / (1.0 - BETA_TWO**STEP_COUNT)) + ADAM_EPS)
    )
    return (-learn_rate * (update + decay_rate * weight), first_new, second_new)


def body(
    inputs,
    cotangent,
    picture_start,
    picture_length,
    qkvg_weight,
    forget_weight,
    forget_bias,
    out_weight,
    gate_up,
    down_weight,
    attn_gain,
    feed_gain,
    qkvg_first,
    qkvg_second,
    forget_first,
    forget_second,
    bias_first,
    bias_second,
    out_first,
    out_second,
    gateup_first,
    gateup_second,
    down_first,
    down_second,
    attngain_first,
    attngain_second,
    feedgain_first,
    feedgain_second,
):
    qkvg_low = qkvg_weight.astype(jnp.bfloat16)
    forget_low = forget_weight.astype(jnp.bfloat16)
    out_low = out_weight.astype(jnp.bfloat16)
    gate_low = gate_up.astype(jnp.bfloat16)
    down_low = down_weight.astype(jnp.bfloat16)
    qkvg_full, forget_full, out_full, gate_full, down_full = (
        lax.all_gather(qkvg_low, "dp", axis=1, tiled=True),
        lax.all_gather(forget_low, "dp", axis=0, tiled=True),
        lax.all_gather(out_low, "dp", axis=1, tiled=True),
        lax.all_gather(gate_low, "dp", axis=1, tiled=True),
        lax.all_gather(down_low, "dp", axis=1, tiled=True),
    )
    heads_local = forget_weight.shape[1]
    width_local = qkvg_weight.shape[2]
    head_size = width_local // heads_local
    head_first = lax.axis_index("tensor") * heads_local
    bias_local = lax.dynamic_slice_in_dim(forget_bias, head_first, heads_local)
    seq_local = picture_start.shape[0]
    inputs_f = inputs.astype(jnp.float32)
    scale_one = rms_scale(inputs_f)
    normed_one = (inputs_f * scale_one * attn_gain).astype(jnp.bfloat16)
    rows_one = gather_rows(normed_one)
    rows_group = rows_one.shape[0]
    seq_len = rows_group // seq_local
    split_shape = (seq_local, seq_len, heads_local, head_size)
    projected = jnp.einsum("td,kde->kte", rows_one, qkvg_full, preferred_element_type=jnp.float32)
    forget_pre = jnp.dot(rows_one, forget_full, preferred_element_type=jnp.float32) + bias_local
    decay_sum = jnp.cumsum(
        jax.nn.log_sigmoid(forget_pre).reshape(seq_local, seq_len, heads_local), axis=1
    )
    heads_q = projected[0].astype(jnp.bfloat16).reshape(split_shape)
    heads_k = projected[1].astype(jnp.bfloat16).reshape(split_shape)
    heads_v = projected[2].astype(jnp.bfloat16).reshape(split_shape)
    gate_sig = jax.nn.sigmoid(projected[3])
    mixture, log_total = lax.map(
        sequence_forward, (heads_q, heads_k, heads_v, decay_sum, picture_start, picture_length)
    )
    core = mixture.reshape(rows_group, width_local)
    gated = (core * gate_sig).astype(jnp.bfloat16)
    middle = inputs_f + spread_rows(jnp.dot(gated, out_full, preferred_element_type=jnp.float32))
    scale_two = rms_scale(middle)
    normed_two = (middle * scale_two * feed_gain).astype(jnp.bfloat16)
    rows_two = gather_rows(normed_two)
    gate_act = jnp.einsum("td,kdf->ktf", rows_two, gate_full, preferred_element_type=jnp.float32)
    sig_gate = jax.nn.sigmoid(gate_act[0])
    silu_gate = gate_act[0] * sig_gate
    hidden = (silu_gate * gate_act[1]).astype(jnp.bfloat16)
    outputs = middle + spread_rows(jnp.dot(hidden, down_full, preferred_element_type=jnp.float32))
    qkvg_back, forget_back, out_back, gate_back, down_back = (
        lax.all_gather(qkvg_low, "dp", axis=1, tiled=True),
        lax.all_gather(forget_low, "dp", axis=0, tiled=True),
        lax.all_gather(out_low, "dp", axis=1, tiled=True),
        lax.all_gather(gate_low, "dp", axis=1, tiled=True),
        lax.all_gather(down_low, "dp", axis=1, tiled=True),
    )
    rows_two_b, feed_grad = fetch_back(normed_two, cotangent)
    grad_down = jnp.einsum("tf,td->fd", hidden, feed_grad, preferred_element_type=jnp.float32)
    grad_hidden = jnp.einsum("td,fd->tf", feed_grad, down_back, preferred_element_type=jnp.float32)
    grad_gate = grad_hidden * gate_act[1] * sig_gate * (1.0 + gate_act[0] * (1.0 - sig_gate))
    grad_upper = grad_hidden * silu_gate
    grad_act = jnp.stack([grad_gate, grad_upper]).astype(jnp.bfloat16)
    grad_in = jnp.einsum("td,ktf->kdf", rows_two_b, grad_act, preferred_element_type=jnp.float32)
    grad_two = spread_rows(
        jnp.einsum("ktf,kdf->td", grad_act, gate_back, preferred_element_type=jnp.float32)
    )
    grad_middle, gain_two_grad = norm_back(grad_two, middle, scale_two, feed_gain)
    grad_middle = grad_middle + cotangent.astype(jnp.float32)
    rows_one_b, attn_grad = fetch_back(normed_one, grad_middle.astype(jnp.bfloat16))
    grad_out = jnp.einsum("te,td->ed", gated, attn_grad, preferred_element_type=jnp.float32)
    grad_core = jnp.einsum("td,ed->te", attn_grad, out_back, preferred_element_type=jnp.float32)
    upstream = (grad_core * gate_sig).astype(jnp.bfloat16).reshape(split_shape)
    grad_gatepre = grad_core * core * gate_sig * (1.0 - gate_sig)
    grad_queries, grad_keys, grad_values, grad_decay = lax.map(
        sequence_backward,
        (heads_q, heads_k, heads_v, decay_sum, picture_start, picture_length, log_total, upstream),
    )
    grad_logf = lax.cumsum(grad_decay, axis=1, reverse=True).reshape(rows_group, heads_local)
    grad_forget_pre = (grad_logf * jax.nn.sigmoid(-forget_pre)).astype(jnp.bfloat16)
    grad_proj = jnp.stack(
        [
            grad_queries.reshape(rows_group, width_local),
            grad_keys.reshape(rows_group, width_local),
            grad_values.reshape(rows_group, width_local),
            grad_gatepre,
        ]
    ).astype(jnp.bfloat16)
    grad_attn = jnp.einsum("td,kte->kde", rows_one_b, grad_proj, preferred_element_type=jnp.float32)
    grad_forget = jnp.einsum(
        "td,th->dh", rows_one_b, grad_forget_pre, preferred_element_type=jnp.float32
    )
    bias_local_grad = jnp.sum(grad_forget_pre.astype(jnp.float32), axis=0)
    term_one = jnp.einsum("kte,kde->td", grad_proj, qkvg_back, preferred_element_type=jnp.float32)
    term_one = term_one + jnp.einsum(
        "th,dh->td", grad_forget_pre, forget_back, preferred_element_type=jnp.float32
    )
    grad_one = spread_rows(term_one)
    grad_inputs, gain_one_grad = norm_back(grad_one, inputs_f, scale_one, attn_gain)
    input_grad = grad_inputs + grad_middle
    shard_attn, shard_forget, shard_out, shard_in, shard_down = (
        lax.psum_scatter(
            grad_attn.astype(jnp.bfloat16), "dp", scatter_dimension=1, tiled=True
        ).astype(jnp.float32),
        lax.psum_scatter(
            grad_forget.astype(jnp.bfloat16), "dp", scatter_dimension=0, tiled=True
        ).astype(jnp.float32),
        lax.psum_scatter(
            grad_out.astype(jnp.bfloat16), "dp", scatter_dimension=1, tiled=True
        ).astype(jnp.float32),
        lax.psum_scatter(
            grad_in.astype(jnp.bfloat16), "dp", scatter_dimension=1, tiled=True
        ).astype(jnp.float32),
        lax.psum_scatter(
            grad_down.astype(jnp.bfloat16), "dp", scatter_dimension=1, tiled=True
        ).astype(jnp.float32),
    )
    bias_full = lax.dynamic_update_slice(
        jnp.zeros(forget_bias.shape, jnp.float32), bias_local_grad, (head_first,)
    )
    local_square = (
        jnp.sum(shard_attn * shard_attn)
        + jnp.sum(shard_forget * shard_forget)
        + jnp.sum(shard_out * shard_out)
        + jnp.sum(shard_in * shard_in)
        + jnp.sum(shard_down * shard_down)
    )
    gain_one_sum, gain_two_sum, bias_sum, square_sum = lax.psum(
        (gain_one_grad, gain_two_grad, bias_full, local_square), ("dp", "tensor")
    )
    total = (
        square_sum
        + jnp.sum(gain_one_sum * gain_one_sum)
        + jnp.sum(gain_two_sum * gain_two_sum)
        + jnp.sum(bias_sum * bias_sum)
    )
    grad_norm = jnp.sqrt(total)
    clip_scale = jnp.minimum(1.0, MAX_NORM / (grad_norm + 1e-06))
    qkvg_update, qkvg_mean, qkvg_meansq = adam_step(
        qkvg_weight, shard_attn, qkvg_first, qkvg_second, clip_scale, WEIGHT_DECAY
    )
    forget_update, forget_mean, forget_meansq = adam_step(
        forget_weight, shard_forget, forget_first, forget_second, clip_scale, WEIGHT_DECAY
    )
    bias_update, bias_mean, bias_meansq = adam_step(
        forget_bias, bias_sum, bias_first, bias_second, clip_scale, 0.0
    )
    out_update, out_mean, out_meansq = adam_step(
        out_weight, shard_out, out_first, out_second, clip_scale, WEIGHT_DECAY
    )
    gateup_update, gateup_mean, gateup_meansq = adam_step(
        gate_up, shard_in, gateup_first, gateup_second, clip_scale, WEIGHT_DECAY
    )
    down_update, down_mean, down_meansq = adam_step(
        down_weight, shard_down, down_first, down_second, clip_scale, WEIGHT_DECAY
    )
    attngain_update, attngain_mean, attngain_meansq = adam_step(
        attn_gain, gain_one_sum, attngain_first, attngain_second, clip_scale, 0.0
    )
    feedgain_update, feedgain_mean, feedgain_meansq = adam_step(
        feed_gain, gain_two_sum, feedgain_first, feedgain_second, clip_scale, 0.0
    )
    return (
        outputs,
        input_grad,
        grad_norm,
        qkvg_update,
        qkvg_mean,
        qkvg_meansq,
        forget_update,
        forget_mean,
        forget_meansq,
        bias_update,
        bias_mean,
        bias_meansq,
        out_update,
        out_mean,
        out_meansq,
        gateup_update,
        gateup_mean,
        gateup_meansq,
        down_update,
        down_mean,
        down_meansq,
        attngain_update,
        attngain_mean,
        attngain_meansq,
        feedgain_update,
        feedgain_mean,
        feedgain_meansq,
    )


def solution(mesh):
    return jax.shard_map(
        body,
        mesh=mesh,
        in_specs=(
            P(("dp", "tensor"), None),
            P(("dp", "tensor"), None),
            P("dp"),
            P("dp"),
            P(None, "dp", "tensor"),
            P("dp", "tensor"),
            P(),
            P("tensor", "dp"),
            P(None, "dp", "tensor"),
            P("tensor", "dp"),
            P(),
            P(),
            P(None, "dp", "tensor"),
            P(None, "dp", "tensor"),
            P("dp", "tensor"),
            P("dp", "tensor"),
            P(),
            P(),
            P("tensor", "dp"),
            P("tensor", "dp"),
            P(None, "dp", "tensor"),
            P(None, "dp", "tensor"),
            P("tensor", "dp"),
            P("tensor", "dp"),
            P(),
            P(),
            P(),
            P(),
        ),
        out_specs=(
            P(("dp", "tensor"), None),
            P(("dp", "tensor"), None),
            P(),
            P(None, "dp", "tensor"),
            P(None, "dp", "tensor"),
            P(None, "dp", "tensor"),
            P("dp", "tensor"),
            P("dp", "tensor"),
            P("dp", "tensor"),
            P(),
            P(),
            P(),
            P("tensor", "dp"),
            P("tensor", "dp"),
            P("tensor", "dp"),
            P(None, "dp", "tensor"),
            P(None, "dp", "tensor"),
            P(None, "dp", "tensor"),
            P("tensor", "dp"),
            P("tensor", "dp"),
            P("tensor", "dp"),
            P(),
            P(),
            P(),
            P(),
            P(),
            P(),
        ),
        check_vma=False,
    )
```

profile of v0, /device:TPU:0, one launch (start us, length us, event | category | flops | bytes accessed | tf_op | source)
XLA Modules:
  0.0 1633.1 jit_solution(10041894976050384758)
XLA Ops:
  14.6 32.2 %all-gather = bf16[8,192,6]{1,2,0:T(8,128)(2,1)S(1)} all-gather(bf16[1,192,6]{1,2,0:T(8,128)(2,1)S(1)} %convert_bitcast_fusion.2), channel_id=1, replica_groups=mesh['dp'=8,'tensor'=4] {'dp'}, dimensions={0}, use_global_device_ids=true | all-gather | bytes 20736 | tf_op jit(solution)/shard_map/all_gather | solution.py:151
  72.1 72.6 %all-gather.12.cloned.1.call-done = bf16[4,1536,384]{2,1,0:T(8,128)(2,1)} async-done(((bf16[4,192,384]{2,1,0:T(8,128)(2,1)}), bf16[4,1536,384]{2,1,0:T(8,128)(2,1)}) %all-gather.12.cloned.1.call-update) | async-done | bytes 4718608 | tf_op jit(solution)/shard_map/all_gather | solution.py:150
  185.3 134.1 %while.28 = (s32[]{:T(128)}, f32[2,1024,6,64]{1,0,3,2:T(2,128)}, f32[2,6,1024]{2,1,0:T(8,128)S(1)}, bf16[2,1024,6,64]{1,3,2,0:T(8,128)(2,1)}, s32[2]{0:T(128)S(1...) while((s32[]{:T(128)}, f32[2,1024,6,64]{1,0,3,2:T(2,128)}, ...), condition=%wide.region_6.7_spmd, body=%wide.region_3.6_spmd.sunk | while | flops 1685058560 | bytes 96545968 | solution.py:178
  224.8 27.7 %dynamic_update_slice.37 = f32[2,1024,6,64]{1,0,3,2:T(2,128)} dynamic-update-slice(f32[2,1024,6,64]{1,0,3,2:T(2,128)} %get-tuple-element.633, f32[1,1024,6,64]{1,0,3,2:T(1,128)S(1)} %copy.326, s32[]{:T(128)S(6)} %copy.336, s32[]{:T(128)} %constant.59.clone.1..sunk, s32[]{:T(128)} %constant.59.clone.1..sunk, s32[]{:T(128)} %constant.59.clone.1..sunk) | dynamic-update-slice | bytes 3145732 | tf_op jit(solution)/shard_map/while/body/jit(dynamic_update_index_in_dim)/dynamic_update_slice | solution.py:178
  291.7 27.7 %dynamic_update_slice.37 = f32[2,1024,6,64]{1,0,3,2:T(2,128)} dynamic-update-slice(f32[2,1024,6,64]{1,0,3,2:T(2,128)} %get-tuple-element.633, f32[1,1024,6,64]{1,0,3,2:T(1,128)S(1)} %copy.326, s32[]{:T(128)S(6)} %copy.336, s32[]{:T(128)} %constant.59.clone.1..sunk, s32[]{:T(128)} %constant.59.clone.1..sunk, s32[]{:T(128)} %constant.59.clone.1..sunk) | dynamic-update-slice | bytes 3145732 | tf_op jit(solution)/shard_map/while/body/jit(dynamic_update_index_in_dim)/dynamic_update_slice | solution.py:178
  341.8 53.6 %reduce-scatter.10.cloned.1.call-done = bf16[512,1536]{1,0:T(8,128)(2,1)} async-done(((bf16[2048,1536]{1,0:T(8,128)(2,1)}), bf16[512,1536]{1,0:T(8,128)(2,1)}) %reduce-scatter.10.cloned.1.call-update) | async-done | bytes 1572880 | tf_op jit(solution)/shard_map/reduce_scatter | solution.py:89
  402.2 95.2 %all-gather.18.cloned.1.call-done = bf16[2,1536,1024]{2,1,0:T(8,128)(2,1)} async-done(((bf16[2,192,1024]{2,1,0:T(8,128)(2,1)}), bf16[2,1536,1024]{2,1,0:T(8,128)(2,1)}) %all-gather.18.cloned.1.call-update) | async-done | bytes 6291472 | tf_op jit(solution)/shard_map/all_gather | solution.py:153
  497.4 46.7 %all-gather.16.cloned.1.call-done = bf16[2048,1536]{1,0:T(8,128)(2,1)} async-done(((bf16[512,1536]{1,0:T(8,128)(2,1)}), bf16[2048,1536]{1,0:T(8,128)(2,1)}) %all-gather.16.cloned.1.call-update) | async-done | bytes 6291472 | tf_op jit(solution)/shard_map/all_gather | solution.py:85
  544.0 19.4 %convolution_bitcast_fusion = f32[2,2048,1024]{2,1,0:T(8,128)} fusion(bf16[2,1536,1024]{2,1,0:T(8,128)(2,1)} %all-gather.18.cloned.1.call-done, bf16[2048,1536]{1,0:T(8,128)(2,1)} %all-gather.16.cloned.1.call-done), kind=kOutput, calls=%fused_computation.75 | convolution fusion | flops 12884901888 | bytes 29360128 | tf_op jit(solution)/shard_map/td,kdf->ktf/dot_general | solution.py:187
  563.4 44.1 %all-gather.20.cloned.1.call-done = bf16[1024,1536]{0,1:T(8,128)(2,1)} async-done(((bf16[1024,192]{0,1:T(8,128)(2,1)}), bf16[1024,1536]{0,1:T(8,128)(2,1)}) %all-gather.20.cloned.1.call-update) | async-done | bytes 3145744 | tf_op jit(solution)/shard_map/all_gather | solution.py:154
  607.5 46.7 %all-gather.22.cloned.1.call-done = bf16[2048,1536]{1,0:T(8,128)(2,1)} async-done(((bf16[512,1536]{1,0:T(8,128)(2,1)}), bf16[2048,1536]{1,0:T(8,128)(2,1)}) %all-gather.22.cloned.1.call-update) | async-done | bytes 6291472 | tf_op jit(solution)/shard_map/all_gather | solution.py:97
  654.2 18.1 %fusion.64 = (bf16[1,2048,1024]{2,1,0:T(8,128)(2,1)S(1)}, bf16[1,2048,1024]{2,1,0:T(8,128)(2,1)}, bf16[2048,1024]{1,0:T(8,128)(2,1)}) fusion(f32[2,2048,1024]{2,1,0:T(8,128)} %convolution_bitcast_fusion, bf16[2048,1536]{1,0:T(8,128)(2,1)} %all-gather.22.cloned.1.call-done, bf16[1024,1536]{0,1:T(8,128)(2,1)} %all-gather.20.cloned.1.call-done), kind=kOutput, calls=%fused_computation.95 | convolution fusion | flops 6473908224 | bytes 38797312 | tf_op jit(solution)/shard_map/td,fd->tf/dot_general | solution.py:201
  674.4 18.0 %bitcast_convert_fusion = bf16[2048,1536]{1,0:T(8,128)(2,1)} fusion(bf16[2,1536,1024]{2,1,0:T(8,128)(2,1)} %all-gather.18.cloned.1.call-done, bf16[1,2048,1024]{2,1,0:T(8,128)(2,1)} %get-tuple-element.457, bf16[1,2048,1024]{2,1,0:T(8,128)(2,1)S(1)} %get-tuple-element.456), kind=kOutput, calls=%fused_computation.64 | convolution fusion | flops 12892241920 | bytes 20971520 | tf_op jit(solution)/shard_map/ktf,kdf->td/dot_general | solution.py:207
  692.7 58.3 %reduce-scatter.14.cloned.1.call-done = bf16[512,1536]{1,0:T(8,128)(2,1)} async-done(((bf16[2048,1536]{1,0:T(8,128)(2,1)}), bf16[512,1536]{1,0:T(8,128)(2,1)}) %reduce-scatter.14.cloned.1.call-update) | async-done | bytes 1572880 | tf_op jit(solution)/shard_map/reduce_scatter | solution.py:89
  769.4 35.1 %all-gather.24.cloned.1.call-done = bf16[2048,1536]{1,0:T(8,128)(2,1)} async-done(((bf16[512,1536]{1,0:T(8,128)(2,1)}), bf16[2048,1536]{1,0:T(8,128)(2,1)}) %all-gather.24.cloned.1.call-update) | async-done | bytes 6291472 | tf_op jit(solution)/shard_map/all_gather | solution.py:97
  822.4 176.8 %while.29 = (s32[]{:T(128)}, bf16[2,1024,6,64]{1,3,2,0:T(8,128)(2,1)}, bf16[2,1024,6,64]{1,3,2,0:T(8,128)(2,1)}, bf16[2,1024,6,64]{1,3,2,0:T(8,128)(2,1)}, f32[2...) while((s32[]{:T(128)}, ...), condition=%wide.region_16.17_spmd, body=%wide.region_12.16_spmd.sunk | while | flops 4133215232 | bytes 264379616 | solution.py:216
  840.6 22.3 %multiply_reduce_fusion.6 = (f32[6,1024]{1,0:T(8,128)S(1)}, f32[6,1024,1024]{1,2,0:T(8,128)}) fusion(f32[6,1024,1024]{1,2,0:T(8,128)} %fusion.190, f32[6,1024]{1,0:T(8,128)S(1)} %dynamic-slice_bitcast_fusion.7, f32[6,1024]{1,0:T(8,128)S(1)} %dynamic-slice_bitcast_fusion.8, f32[1024,1024]{0,1:T(8,128)S(1)} %fusion.189, ...), kind=kOutput, calls=%fused_computation.26.clone.1 | convolution fusion | flops 855631872 | bytes 57271296 | tf_op jit(solution)/shard_map/while/body/eval_jaxpr/ihe,jhe->hij/dot_general | solution.py:41
  862.9 22.6 %fusion.193 = (f32[6,1024]{1,0:T(8,128)S(1)}, f32[6,1024]{1,0:T(8,128)S(1)}, bf16[6,1024,1024]{1,2,0:T(8,128)(2,1)}) fusion(f32[1024,1024]{0,1:T(8,128)S(1)} %fusion.189, f32[6,1024,1024]{1,2,0:T(8,128)} %get-tuple-element.616, f32[6,1024,1024]{1,2,0:T(8,128)} %fusion.190, f32[6,1024]{1,0:T(8,128)S(1)} %get-tuple-element.617), kind=kLoop, calls=%fused_computation.23.clone.1 | loop fusion | flops 44027904 | bytes 67182592 | tf_op jit(solution)/shard_map/while/body/eval_jaxpr/reduce_sum | solution.py:80
  929.1 22.2 %multiply_reduce_fusion.6 = (f32[6,1024]{1,0:T(8,128)S(1)}, f32[6,1024,1024]{1,2,0:T(8,128)}) fusion(f32[6,1024,1024]{1,2,0:T(8,128)} %fusion.190, f32[6,1024]{1,0:T(8,128)S(1)} %dynamic-slice_bitcast_fusion.7, f32[6,1024]{1,0:T(8,128)S(1)} %dynamic-slice_bitcast_fusion.8, f32[1024,1024]{0,1:T(8,128)S(1)} %fusion.189, ...), kind=kOutput, calls=%fused_computation.26.clone.1 | convolution fusion | flops 855631872 | bytes 57271296 | tf_op jit(solution)/shard_map/while/body/eval_jaxpr/ihe,jhe->hij/dot_general | solution.py:41
  951.4 21.4 %fusion.193 = (f32[6,1024]{1,0:T(8,128)S(1)}, f32[6,1024]{1,0:T(8,128)S(1)}, bf16[6,1024,1024]{1,2,0:T(8,128)(2,1)}) fusion(f32[1024,1024]{0,1:T(8,128)S(1)} %fusion.189, f32[6,1024,1024]{1,2,0:T(8,128)} %get-tuple-element.616, f32[6,1024,1024]{1,2,0:T(8,128)} %fusion.190, f32[6,1024]{1,0:T(8,128)S(1)} %get-tuple-element.617), kind=kLoop, calls=%fused_computation.23.clone.1 | loop fusion | flops 44027904 | bytes 67182592 | tf_op jit(solution)/shard_map/while/body/eval_jaxpr/reduce_sum | solution.py:80
  1027.9 19.2 %convert_bitcast_fusion = bf16[2,1536,1024]{1,2,0:T(8,128)(2,1)} fusion(bf16[2048,1536]{1,0:T(8,128)(2,1)} %all-gather.16.cloned.1.call-done, bf16[1,2048,1024]{2,1,0:T(8,128)(2,1)} %get-tuple-element.457, bf16[1,2048,1024]{2,1,0:T(8,128)(2,1)} %copy-done.48), kind=kOutput, calls=%fused_computation.84 | convolution fusion | flops 12892241920 | bytes 20971520 | tf_op jit(solution)/shard_map/td,ktf->kdf/dot_general | solution.py:205
  1150.9 343.0 %all-reduce.6.cloned.1.call-done = (bf16[4,1536,384]{2,0,1:T(4,128)(2,1)}, bf16[2,1536,1024]{2,0,1:T(2,128)(2,1)}) async-done(((bf16[4,1536,384]{2,0,1:T(4,128)(2,1)}, bf16[2,1536,1024]{2,0,1:T(2,128)(2,1)}), (bf16[4,1536,384]{2,0,1:T(4,128)(2,1)}, bf16[2,1536,1024]{2,0,1:T(2,128)(2,1)})) %all-reduce.6.cloned.1.call-update) | async-done | bytes 11010064
  1502.9 50.7 %reduce-scatter.16.cloned.1.call-done = bf16[512,1536]{1,0:T(8,128)(2,1)} async-done(((bf16[2048,1536]{1,0:T(8,128)(2,1)}), bf16[512,1536]{1,0:T(8,128)(2,1)}) %reduce-scatter.16.cloned.1.call-update) | async-done | bytes 1572880 | tf_op jit(solution)/shard_map/reduce_scatter | solution.py:89
  1556.6 40.2 %all-reduce.2 = (f32[]{:T(128)}, f32[1536]{0:T(1024)S(1)}, f32[1536]{0:T(1024)S(1)}, f32[24]{0:T(128)}) all-reduce(f32[]{:T(128)S(6)} %add.273, f32[1536]{0:T(1024)S(1)} %get-tuple-element.373, f32[1536]{0:T(1024)S(1)} %copy-done.34, f32[24]{0:T(128)} %copy-done.41), channel_id=1, replica_groups=mesh['dp'=8,'tensor'=4] {'dp','tensor'}, use_global_device_ids=true, to_apply=%region_31.32 | all-reduce | flops 3097 | bytes 24776 | tf_op jit(solution)/shard_map/psum | solution.py:269
  (293 shorter events, 467.5 us)
Async XLA Ops:
  7.2 54.8 %all-gather.10.cloned.1.call-start = ((), (), s32[]{:S(2)}) async-start(), calls=%async_computation.7 | async-start | bytes 7864320 | tf_op jit(solution)/shard_map/all_gather | solution.py:85
  12.8 132.0 %all-gather.12.cloned.1.call-start = ((), (), s32[]{:S(2)}) async-start(), calls=%async_computation.8 | async-start | bytes 5308416 | tf_op jit(solution)/shard_map/all_gather | solution.py:150
  13.7 317.8 %all-gather.14.cloned.1.call-start = ((), (), s32[]{:S(2)}) async-start(), calls=%async_computation.9 | async-start | bytes 1327104 | tf_op jit(solution)/shard_map/all_gather | solution.py:152
  14.5 380.9 %reduce-scatter.10.cloned.1.call-start = ((), (), s32[]{:S(2)}) async-start(), calls=%async_computation.10 | async-start | bytes 7864320 | tf_op jit(solution)/shard_map/reduce_scatter | solution.py:89
  338.8 158.6 %all-gather.18.cloned.1.call-start = ((), (), s32[]{:S(2)}) async-start(), calls=%async_computation.12 | async-start | bytes 7077888 | tf_op jit(solution)/shard_map/all_gather | solution.py:153
  341.4 202.7 %all-gather.16.cloned.1.call-start = ((), (), s32[]{:S(2)}) async-start(), calls=%async_computation.11 | async-start | bytes 7864320 | tf_op jit(solution)/shard_map/all_gather | solution.py:85
  397.6 357.3 %copy-start.32 = (f32[512]{0:T(512)}, f32[512]{0:T(512)S(1)}, u32[]{:S(2)}) copy-start(f32[512]{0:T(512)S(1)} %add_rsqrt_fusion) | copy-start | bytes 6148
  399.4 208.1 %all-gather.20.cloned.1.call-start = ((), (), s32[]{:S(2)}) async-start(), calls=%async_computation.13 | async-start | bytes 3538944 | tf_op jit(solution)/shard_map/all_gather | solution.py:154
  401.4 252.8 %all-gather.22.cloned.1.call-start = ((), (), s32[]{:S(2)}) async-start(), calls=%async_computation.15 | async-start | bytes 7864320 | tf_op jit(solution)/shard_map/all_gather | solution.py:97
  402.1 348.9 %reduce-scatter.14.cloned.1.call-start = ((), (), s32[]{:S(2)}) async-start(), calls=%async_computation.16 | async-start | bytes 7864320 | tf_op jit(solution)/shard_map/reduce_scatter | solution.py:89
  692.5 112.0 %all-gather.24.cloned.1.call-start = ((), (), s32[]{:S(2)}) async-start(), calls=%async_computation.17 | async-start | bytes 7864320 | tf_op jit(solution)/shard_map/all_gather | solution.py:97
  757.9 380.4 %reduce-scatter.20.cloned.1.call-start = ((), (), s32[]{:S(2)}) async-start(), calls=%async_computation.20 | async-start | bytes 3538944 | tf_op jit(solution)/shard_map/reduce_scatter | solution.py:255
  769.3 371.0 %reduce-scatter.22.cloned.1.call-start = ((), (), s32[]{:S(2)}) async-start(), calls=%async_computation.21 | async-start | bytes 442368
  822.4 193.1 %copy-start.26 = (f32[2048,6]{0,1:T(8,128)S(1)}, f32[2048,6]{0,1:T(8,128)}, u32[]{:S(2)}) copy-start(f32[2048,6]{0,1:T(8,128)} %get-tuple-element.469) | copy-start | bytes 147460
  1020.5 128.8 %reduce-scatter.18.cloned.1.call-start = ((), (), s32[]{:S(2)}) async-start(), calls=%async_computation.19 | async-start | bytes 1327104 | tf_op jit(solution)/shard_map/reduce_scatter | solution.py:249
  1027.8 466.0 %all-reduce.6.cloned.1.call-start = ((), (), s32[]{:S(2)}) async-start(), calls=%async_computation.22 | async-start | bytes 22020096
  1104.1 449.5 %reduce-scatter.16.cloned.1.call-start = ((), (), s32[]{:S(2)}) async-start(), calls=%async_computation.18 | async-start | bytes 7864320 | tf_op jit(solution)/shard_map/reduce_scatter | solution.py:89
  1123.5 495.7 %reduce-scatter.12.cloned.1.call-start = ((), (), s32[]{:S(2)}) async-start(), calls=%async_computation.14 | async-start | bytes 7864320 | tf_op jit(solution)/shard_map/reduce_scatter | solution.py:89
  1136.4 417.2 %copy-start.2 = (bf16[512,1536]{1,0:T(8,128)(2,1)S(1)}, bf16[512,1536]{1,0:T(8,128)(2,1)}, u32[]{:S(2)}) copy-start(bf16[512,1536]{1,0:T(8,128)(2,1)} %param.32) | copy-start | bytes 4718596
  1136.4 417.2 %copy-start.31 = (f32[1536]{0:T(1024)S(1)}, f32[1536]{0:T(1024)}, u32[]{:S(2)}) copy-start(f32[1536]{0:T(1024)} %param.42) | copy-start | bytes 18436
  1136.4 417.2 %copy-start.38 = (f32[512]{0:T(512)S(1)}, f32[512]{0:T(512)}, u32[]{:S(2)}) copy-start(f32[512]{0:T(512)} %copy-done.37) | copy-start | bytes 6148
  1140.3 353.6 %copy-start.41 = (f32[24]{0:T(128)}, f32[24]{0:T(128)S(1)}, u32[]{:S(2)}) copy-start(f32[24]{0:T(128)S(1)} %dynamic_update_slice.24) | copy-start | bytes 292
  1495.1 110.1 %copy-start.30 = (f32[1536]{0:T(1024)S(1)}, f32[1536]{0:T(1024)}, u32[]{:S(2)}) copy-start(f32[1536]{0:T(1024)} %param.43) | copy-start | bytes 18436
  1495.2 111.5 %copy-start.25 = (bf16[384,192]{0,1:T(8,128)(2,1)S(1)}, bf16[384,192]{0,1:T(8,128)(2,1)}, u32[]{:S(2)}) copy-start(bf16[384,192]{0,1:T(8,128)(2,1)} %reduce-scatter.18.cloned.1.call-done) | copy-start | bytes 442372
  (42 other events, 745.2 us)
Sparse Core Ops, SparseCore 0:
  12.9 49.0 all-gather.9
  64.8 79.9 all-gather.11
  147.5 39.1 all-gather.13
  338.9 56.5 reduce-scatter.9
  398.3 99.0 all-gather.17
  499.4 44.5 all-gather.15
  547.0 60.4 all-gather.19
  609.1 44.9 all-gather.21
  692.6 58.3 reduce-scatter.13
  758.0 46.3 all-gather.23
  808.6 74.4 reduce-scatter.19
  1020.6 61.5 reduce-scatter.21
  1086.1 63.0 reduce-scatter.17
  1153.1 340.6 all-reduce.5
  1496.2 57.3 reduce-scatter.15
  1556.1 59.0 reduce-scatter.11
where the time goes:
time: 1650 us; the launch traced here: 1630 us
  waiting for transfers between devices  869 us (53%)
  matrix products  351 us (21%)
  local copies, waits for them, and re-layouts  161 us (10%)
  other arithmetic  150 us (9%)
  blocking collectives  72.4 us (4%)
  between operations  22.5 us (1%)
    unnamed x18, waiting for transfers between devices  344 us
    reduce_scatter x4, waiting for transfers between devices, spread_rows(): lax.psum_scatter(partial_sum.astype(jnp.bfloat16), 'tensor', scatter_dime...  163 us
    all_gather x1, waiting for transfers between devices, body(): lax.all_gather(gate_low, 'dp', axis=1, tiled=True)  95.2 us
    all_gather x2, waiting for transfers between devices, fetch_back(): lax.all_gather(grad_low, 'tensor', axis=0, tiled=True)  81.8 us
    all_gather x1, waiting for transfers between devices, body(): lax.all_gather(qkvg_low, 'dp', axis=1, tiled=True)  72.6 us
    dot_general x4, matrix products, scores_of(): jnp.einsum('ihe,jhe->hij', queries, key_rows, preferred_element_type=jnp....  69.6 us
    all_gather x2, waiting for transfers between devices, gather_rows(): return lax.all_gather(normed, 'tensor', axis=0, tiled=True)  61.7 us
    dynamic_update_slice x4, local copies, waits for them, and re-layouts, body(): lax.map(sequence_forward, (heads_q, heads_k, heads_v, decay_sum, picture_...  58.6 us
  transfers between devices with their start and end apart: 16, of which 12 were waited for; matrix products, arithmetic and copies ran while one was open for 36% of the time, Pallas kernels for 0%

commit v1 on v0

v1 whole, which is shorter than its diff:
```python
import functools

import jax
import jax.numpy as jnp
from jax import lax
from jax.experimental import pallas as pl
from jax.experimental.pallas import tpu as pltpu

HEAD_DIM = 64
PIECE = 256
LOG2E = 1.4426950408889634
LOW = jnp.bfloat16
F32 = jnp.float32
HIDE = -1e30
NT = (((1,), (1,)), ((), ()))
TN = (((0,), (0,)), ((), ()))


def mm(a, b, dims=(((1,), (0,)), ((), ()))):
    return lax.dot_general(a, b, dims, preferred_element_type=F32)


def split_three(x):
    hi = x.astype(LOW)
    rest = x - hi.astype(F32)
    mid = rest.astype(LOW)
    return hi, mid, (rest - mid.astype(F32)).astype(LOW)


def scan_rows(x, reverse):
    length = x.shape[1]
    row = lax.broadcasted_iota(jnp.int32, (PIECE, PIECE), 0)
    col = lax.broadcasted_iota(jnp.int32, (PIECE, PIECE), 1)
    tri = jnp.where(row >= col if reverse else row <= col, 1.0, 0.0).astype(LOW)
    count = length // PIECE
    out = [None] * count
    carry = None
    for b in reversed(range(count)) if reverse else range(count):
        part = x[:, b * PIECE:(b + 1) * PIECE]
        done = sum(mm(t, tri) for t in split_three(part))
        if carry is not None:
            done = done + carry
        out[b] = done
        carry = done[:, :1] if reverse else done[:, PIECE - 1:]
    return jnp.concatenate(out, axis=1)


def log_gate(zf):
    return jnp.minimum(zf, 0.0) - jnp.log1p(jnp.exp(-jnp.abs(zf)))


def attn_fwd_kernel(start, size, q_ref, k_ref, v_ref, zf_ref, o_ref, lse_ref, *, hb):
    s_at = pl.program_id(0)
    length, width = q_ref.shape
    count = length // PIECE
    first, extent = start[s_at], size[s_at]
    c_rows = scan_rows(log_gate(zf_ref[...]), False) * LOG2E
    c_cols = c_rows.T
    row = lax.broadcasted_iota(jnp.int32, (PIECE, PIECE), 0)
    col = lax.broadcasted_iota(jnp.int32, (PIECE, PIECE), 1)
    causal = col <= row
    lane = lax.broadcasted_iota(jnp.int32, (1, width), 1)
    mine = [(lane >= h * HEAD_DIM) & (lane < (h + 1) * HEAD_DIM) for h in range(hb)]
    spare = [((h + 1) % hb) * HEAD_DIM for h in range(hb)]
    if lse_ref.shape[0] > hb:
        lse_ref[...] = jnp.zeros(lse_ref.shape, F32)

    def block(i, wide):
        lo, hi = i * PIECE, (i + 1) * PIECE
        in_pic = (lo >= first) & (lo < first + extent)
        out, lse = None, None
        for h in range(hb):
            q = jnp.where(mine[h], q_ref[lo:hi, :], jnp.zeros((), LOW))
            c_row = c_rows[h:h + 1, :]
            c_col = c_cols[lo:hi, h:h + 1]
            base = c_row[:, lo:lo + 1]
            parts, spans = [], []
            if i:
                parts.append(mm(q, k_ref[0:lo, :], NT) + (base - c_row[:, :lo]))
                spans.append((0, lo))
            back = base - 2.0 * c_col
            other = jnp.where(in_pic, back + c_row[:, lo:hi], HIDE)
            parts.append(mm(q, k_ref[lo:hi, :], NT) + jnp.where(causal, base - c_row[:, lo:hi], other))
            spans.append((lo, hi))
            if wide:
                parts.append(mm(q, k_ref[hi:hi + PIECE, :], NT) + (back + c_row[:, hi:hi + PIECE]))
                spans.append((hi, hi + PIECE))
            peak = functools.reduce(jnp.maximum, [jnp.max(p, axis=1, keepdims=True) for p in parts])
            acc = None
            for p, (a, b) in zip(parts, spans):
                v = jnp.where(mine[h], v_ref[a:b, :], jnp.ones((), LOW))
                t = mm(jnp.exp2(p - peak).astype(LOW), v)
                acc = t if acc is None else acc + t
            total = acc[:, spare[h]:spare[h] + 1]
            o_h = acc / total
            l_h = jnp.broadcast_to(peak + jnp.log2(total), o_h.shape)
            out = o_h if out is None else jnp.where(mine[h], o_h, out)
            lse = l_h if lse is None else jnp.where(mine[h], l_h, lse)
        o_ref[lo:hi, :] = out
        turned = lse.T
        for h in range(hb):
            lse_ref[h:h + 1, lo:hi] = turned[h * HEAD_DIM:h * HEAD_DIM + 1, :]

    for i in range(count):
        if i + 1 < count:
            wide = (first == i * PIECE) & (extent > PIECE)
            pl.when(wide)(functools.partial(block, i, True))
            pl.when(jnp.logical_not(wide))(functools.partial(block, i, False))
        else:
            block(i, False)


def attn_bwd_kernel(start, size, q_ref, k_ref, v_ref, zf_ref, lse_ref, o_ref, do_ref,
                    dq_ref, dk_ref, dv_ref, dzf_ref, dk_acc, dv_acc, dc_acc, *, hb):
    s_at = pl.program_id(0)
    length, width = q_ref.shape
    count = length // PIECE
    first, extent = start[s_at], size[s_at]
    zf = zf_ref[...]
    c_rows = scan_rows(log_gate(zf), False) * LOG2E
    c_cols = c_rows.T
    row = lax.broadcasted_iota(jnp.int32, (PIECE, PIECE), 0)
    col = lax.broadcasted_iota(jnp.int32, (PIECE, PIECE), 1)
    causal = row <= col
    lane = lax.broadcasted_iota(jnp.int32, (1, width), 1)
    mine = [(lane >= h * HEAD_DIM) & (lane < (h + 1) * HEAD_DIM) for h in range(hb)]
    spare = [((h + 1) % hb) * HEAD_DIM for h in range(hb)]
    zero, one = jnp.zeros((), LOW), jnp.ones((), LOW)
    dk_acc[...] = jnp.zeros(dk_acc.shape, F32)
    dv_acc[...] = jnp.zeros(dv_acc.shape, F32)
    prod = do_ref[...].astype(F32) * o_ref[...].astype(F32)
    head_row = lax.broadcasted_iota(jnp.int32, (8, width), 0)
    head_lane = lax.broadcasted_iota(jnp.int32, (8, width), 1)
    pick = jnp.where((head_lane >= head_row * HEAD_DIM) & (head_lane < (head_row + 1) * HEAD_DIM), 1.0, 0.0).astype(LOW)
    p_hi = prod.astype(LOW)
    p_lo = (prod - p_hi.astype(F32)).astype(LOW)
    delta = mm(pick, p_hi, NT) + mm(pick, p_lo, NT)

    def block(i, wide):
        lo, hi = i * PIECE, (i + 1) * PIECE
        in_pic = (lo >= first) & (lo < first + extent)
        out = None
        for h in range(hb):
            q_all = q_ref[lo:hi, :]
            q = jnp.where(mine[h], q_all, zero)
            q_one = jnp.where(mine[h], q_all, one)
            do = jnp.where(mine[h], do_ref[lo:hi, :], zero)
            c_row = c_rows[h:h + 1, lo:hi]
            base = c_row[:, :1]
            lse = lse_ref[h:h + 1, lo:hi]
            dl = delta[h:h + 1, lo:hi]
            back = base - 2.0 * c_row - lse
            acc = None
            todo = ([(0, lo, 0)] if i else []) + [(lo, hi, 1)] + ([(hi, hi + PIECE, 2)] if wide else [])
            for a, b, kind in todo:
                c_col = c_cols[a:b, h:h + 1]
                st = mm(k_ref[a:b, :], q, NT)
                if kind == 0:
                    st = st + (base - c_col) - lse
                elif kind == 1:
                    other = jnp.where(in_pic, back + c_col, HIDE)
                    st = st + jnp.where(causal, (base - c_col) - lse, other)
                else:
                    st = st + (back + c_col)
                p = jnp.exp2(st)
                ds = p * (mm(v_ref[a:b, :], do, NT) - dl)
                ds = ds.astype(LOW)
                dv_acc[a:b, :] += mm(p.astype(LOW), do)
                k_one = jnp.where(mine[h], k_ref[a:b, :], one)
                if kind == 2:
                    q_one = jnp.where(mine[h], q_all, -one)
                    k_one = jnp.where(mine[h], k_ref[a:b, :], -one)
                dk_acc[h, a:b, :] += mm(ds, q_one)
                t = mm(ds, k_one, TN)
                acc = t if acc is None else acc + t
                if kind == 1:
                    def signs(ds=ds, lo=lo, hi=hi, h=h):
                        minus = jnp.where(causal, zero, ds)
                        m2 = jnp.where(mine[h], zero, jnp.full((), -2.0, LOW))
                        m2 = jnp.broadcast_to(m2, (PIECE, width))
                        dk_acc[h, lo:hi, :] += mm(minus, m2)
                        dc_acc[h] = mm(minus, m2, TN)
                    def none(h=h):
                        dc_acc[h] = jnp.zeros((PIECE, width), F32)
                    pl.when(in_pic)(signs)
                    pl.when(jnp.logical_not(in_pic))(none)
                    acc = acc + dc_acc[h]
            out = acc if out is None else jnp.where(mine[h], acc, out)
            dc_row = acc.T[spare[h]:spare[h] + 1, :]
            dzf_ref[h:h + 1, lo:hi] = dc_row
        dq_ref[lo:hi, :] = (out * HEAD_DIM ** -0.5).astype(LOW)

    if dzf_ref.shape[0] > hb:
        dzf_ref[...] = jnp.zeros(dzf_ref.shape, F32)
    for i in range(count):
        if i + 1 < count:
            wide = (first == i * PIECE) & (extent > PIECE)
            pl.when(wide)(functools.partial(block, i, True))
            pl.when(jnp.logical_not(wide))(functools.partial(block, i, False))
        else:
            block(i, False)
    dv_ref[...] = dv_acc[...].astype(LOW)
    dk = dk_acc[0]
    for h in range(1, hb):
        dk = jnp.where(mine[h], dk_acc[h], dk)
    dk_ref[...] = (dk * (1.0 / LOG2E)).astype(LOW)
    for h in range(hb):
        turned = dk_acc[h].T
        dzf_ref[h:h + 1, :] -= turned[spare[h]:spare[h] + 1, :]
    dlog = scan_rows(dzf_ref[...], True)
    dzf_ref[...] = (dlog * jax.nn.sigmoid(-zf)).astype(LOW).astype(F32)


def attn_calls(q_like, seqs, heads):
    width = heads * HEAD_DIM
    hb = 2 if heads % 2 == 0 else heads
    return hb, heads // hb, hb * HEAD_DIM, width


def attend(start, size, qkv, zf, seqs):
    tokens, width3 = qkv.shape
    width, length = width3 // 3, tokens // seqs
    heads = width // HEAD_DIM
    hb, pairs, bw, _ = attn_calls(qkv, seqs, heads)
    col = lambda off: pl.BlockSpec((length, bw), lambda s, p, *_: (s, off * pairs + p))
    rows = pl.BlockSpec((None, None, 8, length), lambda s, p, *_: (s, p, 0, 0))
    if bw % 128:
        three, cols = [qkv[:, j * width:(j + 1) * width] for j in range(3)], [col(0)] * 3
    else:
        three, cols = [qkv] * 3, [col(0), col(1), col(2)]
    return pl.pallas_call(
        functools.partial(attn_fwd_kernel, hb=hb),
        grid_spec=pltpu.PrefetchScalarGridSpec(
            num_scalar_prefetch=2,
            grid=(seqs, pairs),
            in_specs=cols + [rows],
            out_specs=[col(0), rows],
        ),
        out_shape=[
            jax.ShapeDtypeStruct((tokens, width), F32),
            jax.ShapeDtypeStruct((seqs, pairs, 8, length), F32),
        ],
        compiler_params=pltpu.CompilerParams(vmem_limit_bytes=50 * 2**20),
        cost_estimate=pl.CostEstimate(flops=2 * 2 * 256 * length * length * seqs * heads * 5 // 8, bytes_accessed=tokens * width * 10, transcendentals=length * length * seqs * heads),
        name="attend",
    )(start, size, *three, zf)


def attend_back(start, size, qkv, zf, lse, core, up, seqs):
    tokens, width3 = qkv.shape
    width, length = width3 // 3, tokens // seqs
    heads = width // HEAD_DIM
    hb, pairs, bw, _ = attn_calls(qkv, seqs, heads)
    col = lambda off: pl.BlockSpec((length, bw), lambda s, p, *_: (s, off * pairs + p))
    rows = pl.BlockSpec((None, None, 8, length), lambda s, p, *_: (s, p, 0, 0))
    if bw % 128:
        three, cols = [qkv[:, j * width:(j + 1) * width] for j in range(3)], [col(0)] * 3
    else:
        three, cols = [qkv] * 3, [col(0), col(1), col(2)]
    return pl.pallas_call(
        functools.partial(attn_bwd_kernel, hb=hb),
        grid_spec=pltpu.PrefetchScalarGridSpec(
            num_scalar_prefetch=2,
            grid=(seqs, pairs),
            in_specs=cols + [rows, rows, col(0), col(0)],
            out_specs=[col(0), col(0), col(0), rows],
            scratch_shapes=[
                pltpu.VMEM((hb, length, bw), F32),
                pltpu.VMEM((length, bw), F32),
                pltpu.VMEM((hb, PIECE, bw), F32),
            ],
        ),
        out_shape=[jax.ShapeDtypeStruct((tokens, width), LOW)] * 3
        + [jax.ShapeDtypeStruct((seqs, pairs, 8, length), F32)],
        compiler_params=pltpu.CompilerParams(vmem_limit_bytes=50 * 2**20),
        cost_estimate=pl.CostEstimate(flops=5 * 2 * 256 * length * length * seqs * heads * 5 // 8, bytes_accessed=tokens * width * 20, transcendentals=length * length * seqs * heads),
        name="attend_back",
    )(start, size, *three, zf, lse, core, up)


from jax.sharding import PartitionSpec as P

NORM_EPS = 1e-05
BETA_ONE = 0.9
BETA_TWO = 0.95
WEIGHT_DECAY = 0.1
ADAM_EPS = 1e-08
MAX_NORM = 1.0
STEP_COUNT = 10.0


def rms_scale(values):
    return lax.rsqrt(jnp.mean(values * values, axis=-1, keepdims=True) + NORM_EPS)


def norm_back(gradient, values, inv_scale, gain_row):
    normed = values * inv_scale
    scaled = gradient * gain_row
    backward = inv_scale * (scaled - normed * jnp.mean(scaled * normed, axis=-1, keepdims=True))
    return (backward, jnp.sum(gradient * normed, axis=0))


def adam_step(weight, gradient, first_old, second_old, clip_scale, decay_rate, width):
    learn_rate = 0.4 / width**0.5
    scaled = gradient * clip_scale
    first_new = BETA_ONE * first_old + (1.0 - BETA_ONE) * scaled
    second_new = BETA_TWO * second_old + (1.0 - BETA_TWO) * scaled * scaled
    update = (
        first_new
        / (1.0 - BETA_ONE**STEP_COUNT)
        / (jnp.sqrt(second_new / (1.0 - BETA_TWO**STEP_COUNT)) + ADAM_EPS)
    )
    return (-learn_rate * (update + decay_rate * weight), first_new, second_new)


def after(x, *done):
    return lax.optimization_barrier((x,) + done)[0]


class Team:
    def __init__(self, axis, size):
        self.axis, self.size, self.me = axis, size, lax.axis_index(axis)

    def turn(self, x, k):
        return lax.ppermute(x, self.axis, [(i, (i + k) % self.size) for i in range(self.size)])

    def add(self, x):
        parts = jnp.stack([self.turn(x, k) if k else x for k in range(self.size)])
        order = lax.rem(self.me + self.size - jnp.arange(self.size, dtype=jnp.int32), self.size)
        return jnp.sum(jnp.take(parts, order, axis=0), axis=0)


class Ring:
    def __init__(self, axis, size):
        self.axis, self.size = axis, size
        if size == 8:
            self.table = list(range(0, size, 2)) + list(range(size - 1, 0, -2))
        else:
            self.table = list(range(size))
        spot = [self.table.index(i) for i in range(size)]
        me = lax.axis_index(axis)
        mine = jnp.asarray(spot, jnp.int32)[me]
        steps = jnp.arange(size, dtype=jnp.int32)
        self.ahead = jnp.asarray(self.table, jnp.int32)[lax.rem(mine + steps, size)]

    def step(self, x, way):
        n = self.size
        return lax.ppermute(x, self.axis, [(self.table[r], self.table[(r + way) % n]) for r in range(n)])

    def gather(self, x, way):
        n = self.size
        blocks = {0: x}
        a = b = x
        for k in range(1, n // 2 + 1):
            a = self.step(a, way)
            blocks[-k * way % n] = a
            if k <= (n - 1) // 2:
                b = self.step(b, -way)
                blocks[k * way % n] = b
        return [blocks[k] for k in range(n)]

    def reduce(self, x, way):
        n = self.size

        def block(k):
            return lax.dynamic_index_in_dim(x, self.ahead[k % n], 0, keepdims=False)

        arrived = []
        for w, far in ((way, n // 2), (-way, (n - 1) // 2)):
            moving = block(w * far)
            for k in range(far - 1, -1, -1):
                moving = self.step(moving, w)
                if k:
                    moving = (moving.astype(F32) + block(w * k).astype(F32)).astype(LOW)
            arrived.append(moving)
        return sum(m.astype(F32) for m in arrived) + block(0).astype(F32)


def place_kernel(where, *refs, rows, tail):
    count = (len(refs) - (3 if tail else 2))
    out, sem = refs[count], refs[-1]
    copies = []
    for i in range(count):
        at = pl.multiple_of(where[i] * rows, rows)
        copies.append(pltpu.make_async_copy(refs[i].at[pl.ds(0, rows), :], out.at[pl.ds(at, rows), :], sem.at[i]))
        if tail:
            at = pl.multiple_of(where[i] * tail, tail)
            copies.append(
                pltpu.make_async_copy(
                    refs[i].at[pl.ds(rows, tail), :], refs[count + 1].at[pl.ds(at, tail), :], sem.at[count + i]
                )
            )
    for copy in copies:
        copy.start()
    for copy in copies:
        copy.wait()


def place(blocks, where, tail=0):
    rows, n = blocks[0].shape
    rows -= tail
    count = len(blocks)
    shapes = [jax.ShapeDtypeStruct((count * r, n), blocks[0].dtype) for r in (rows, tail) if r]
    out = pl.pallas_call(
        functools.partial(place_kernel, rows=rows, tail=tail),
        in_specs=[pl.BlockSpec(memory_space=pltpu.SMEM)] + [pl.BlockSpec(memory_space=pl.ANY)] * count,
        out_specs=[pl.BlockSpec(memory_space=pltpu.VMEM)] * len(shapes),
        out_shape=shapes,
        scratch_shapes=[pltpu.SemaphoreType.DMA((2 * count,))],
        compiler_params=pltpu.CompilerParams(vmem_limit_bytes=40 * 2**20),
        cost_estimate=pl.CostEstimate(flops=0, bytes_accessed=4 * count * rows * n, transcendentals=0),
        name="place",
    )(where, *blocks)
    return out if tail else out[0]


def make_body(dp, tn):
    def body(
        inputs, cotangent, picture_start, picture_length,
        qkvg_weight, forget_weight, forget_bias, out_weight, gate_up, down_weight,
        attn_gain, feed_gain,
        qkvg_first, qkvg_second, forget_first, forget_second, bias_first, bias_second,
        out_first, out_second, gateup_first, gateup_second, down_first, down_second,
        attngain_first, attngain_second, feedgain_first, feedgain_second,
    ):
        dims = inputs.shape[1]
        local, rank_rows, width = inputs.shape[0], qkvg_weight.shape[1], qkvg_weight.shape[2]
        hidden_size = gate_up.shape[2]
        heads = forget_weight.shape[1]
        seqs = picture_start.shape[0]
        rows_group = local * tn
        length = rows_group // seqs
        data = Ring("dp", dp)
        rank = lax.axis_index("tensor")
        paired = tn == 4 and local * 2 == length
        core, side = lax.rem(rank, 2), lax.div(rank, 2)
        rows_each = dims // dp

        def swap(x, bit):
            return lax.ppermute(x, "tensor", [(i, i ^ bit) for i in range(tn)])

        def join(a, b):
            return jnp.where(core == 0, jnp.concatenate([a, b]), jnp.concatenate([b, a]))

        def half(p, which):
            return lax.dynamic_slice_in_dim(p, which * local, local, 0)

        def gather_rows(x):
            if not paired:
                return [lax.all_gather(x, "tensor", axis=0, tiled=True)]
            far = swap(x, 2)
            near = swap(x, 1)
            return [join(x, near), join(far, swap(far, 1))]

        def spread_far(part):
            if not paired:
                return lax.psum_scatter(part, "tensor", scatter_dimension=0, tiled=True)
            both = half(part, core).astype(F32) + swap(half(part, 1 - core), 1).astype(F32)
            return swap(both.astype(LOW), 2)

        def spread_near(back, part):
            if not paired:
                return back.astype(F32)
            near = half(part, core).astype(F32) + swap(half(part, 1 - core), 1).astype(F32)
            return near + back.astype(F32)

        if paired:
            order = [side, 1 - side]
            starts = [lax.dynamic_slice_in_dim(picture_start, o, 1) for o in order]
            sizes = [lax.dynamic_slice_in_dim(picture_length, o, 1) for o in order]
            seqs_each = 1
        else:
            starts, sizes, seqs_each = [picture_start], [picture_length], seqs
        chunks = len(starts)
        hb = 2 if heads % 2 == 0 else heads
        pairs = heads // hb

        def to_heads(z):
            z = z.reshape(pairs, hb, seqs_each, length).transpose(2, 0, 1, 3)
            return jnp.pad(z, ((0, 0), (0, 0), (0, 8 - hb), (0, 0)))

        def from_heads(z):
            return z[:, :, :hb].transpose(1, 2, 0, 3).reshape(heads, seqs_each * length)

        def flat(w):
            return w.transpose(1, 0, 2).reshape(w.shape[1], -1).astype(LOW)

        inputs_f = inputs.astype(F32)
        scale_one = rms_scale(inputs_f)
        normed_one = (inputs_f * scale_one * attn_gain).astype(LOW)
        tail = 16
        forget_row = forget_weight.T.astype(LOW).reshape(1, heads * rows_each)
        forget_row = jnp.pad(forget_row, ((0, tail - 1), (0, 3 * width - heads * rows_each)))
        blocks = data.gather(jnp.concatenate([flat(qkvg_weight[:3]), forget_row]), 1)
        w_qkv, w_forget = place(blocks, data.ahead, tail)
        w_forget = w_forget.reshape(dp, tail, -1)[:, 0, :heads * rows_each]
        w_forget = w_forget.reshape(dp, heads, rows_each).transpose(1, 0, 2).reshape(heads, dims)
        rows_one = gather_rows(normed_one)
        gate_out = jnp.concatenate([qkvg_weight[3].astype(LOW), out_weight.T.astype(LOW)], axis=1)
        blocks = data.gather(after(gate_out, w_qkv), -1)
        w_gate_out = place(blocks, data.ahead)
        w_gate, w_out = w_gate_out[:, :width], w_gate_out[:, width:]
        w_up = place(data.gather(after(flat(gate_up), w_qkv), 1), data.ahead)
        w_down = place(data.gather(after(down_weight.T.astype(LOW), w_gate_out), -1), data.ahead)
        feed_grad = gather_rows(after(cotangent, *rows_one))

        head_first = rank * heads
        bias_local = lax.dynamic_slice_in_dim(forget_bias, head_first, heads)
        col_scale = jnp.where(jnp.arange(3 * width) < width, HEAD_DIM**-0.5 * LOG2E, 1.0).astype(F32)

        last = ()
        qkv, zf, attended, gate_sig, gated = ([None] * chunks for _ in range(5))
        for i in range(chunks):
            r = after(rows_one[i], *last)
            qkv[i] = (mm(r, w_qkv) * col_scale).astype(LOW)
            zf[i] = to_heads(mm(w_forget, r, NT) + bias_local[:, None])
            last = (qkv[i], zf[i])
        parts = [None] * chunks
        back = None
        for i in reversed(range(chunks)):
            attended[i] = attend(starts[i], sizes[i], after(qkv[i], *last), zf[i], seqs_each)
            gate_sig[i] = jax.nn.sigmoid(mm(after(rows_one[i], attended[i][0]), w_gate))
            gated[i] = (attended[i][0] * gate_sig[i]).astype(LOW)
            parts[i] = mm(gated[i], w_out, NT).astype(LOW)
            last = (parts[i],)
            if back is None:
                back = spread_far(parts[i])
        middle = inputs_f + spread_near(back, parts[0])
        scale_two = rms_scale(middle)
        normed_two = (middle * scale_two * feed_gain).astype(LOW)
        rows_two = gather_rows(normed_two)

        hidden, grad_act = [None] * chunks, [None] * chunks
        last, back = (), None
        for i in range(chunks):
            act = mm(after(rows_two[i], *last), w_up)
            a, b = act[:, :hidden_size], act[:, hidden_size:]
            sig = jax.nn.sigmoid(a)
            silu = a * sig
            hidden[i] = (silu * b).astype(LOW)
            grad_hidden = mm(feed_grad[i], w_down)
            grad_gate = grad_hidden * b * sig * (1.0 + a * (1.0 - sig))
            grad_act[i] = jnp.concatenate([grad_gate, grad_hidden * silu], axis=1).astype(LOW)
            last = (grad_act[i],)
        back = spread_far(mm(grad_act[-1], w_up, NT).astype(LOW))
        own = mm(grad_act[0], w_up, NT).astype(LOW)
        grad_down = sum(mm(after(y, own), h, TN) for y, h in zip(feed_grad, hidden)).astype(LOW)
        shard_down = data.reduce(grad_down.reshape(dp, rows_each, -1), 1)
        grad_up = sum(mm(after(r, grad_down), g, TN) for r, g in zip(rows_two, grad_act)).astype(LOW)
        shard_up = data.reduce(after(grad_up, shard_down).reshape(dp, rows_each, -1), -1)
        grad_two = spread_near(back, own)
        grad_middle, gain_two_grad = norm_back(grad_two, middle, scale_two, feed_gain)
        grad_middle = grad_middle + cotangent.astype(F32)
        attn_grad = gather_rows(grad_middle.astype(LOW))
        out_back = spread_far(mm(after(hidden[-1], grad_up), w_down, NT).astype(LOW))
        outputs = middle + spread_near(out_back, mm(hidden[0], w_down, NT).astype(LOW))

        grad_gatepre, grad_proj, grad_zf = ([None] * chunks for _ in range(3))
        last = (grad_up,)
        for i in range(chunks):
            grad_core = mm(after(attn_grad[i], *last), w_out)
            up_stream = (grad_core * gate_sig[i]).astype(LOW)
            grad_gatepre[i] = (grad_core * attended[i][0] * gate_sig[i] * (1.0 - gate_sig[i])).astype(LOW)
            dq, dk, dv, dz = attend_back(
                starts[i], sizes[i], qkv[i], zf[i], attended[i][1], attended[i][0], up_stream, seqs_each
            )
            grad_proj[i] = jnp.concatenate([dq, dk, dv], axis=1)
            grad_zf[i] = from_heads(dz).astype(LOW)
            last = (dq,)
        grad_out = sum(mm(y, g, TN) for y, g in zip(attn_grad, gated)).astype(LOW)
        grad_gate_w = sum(mm(r, g, TN) for r, g in zip(rows_one, grad_gatepre)).astype(LOW)
        grad_go = jnp.concatenate([grad_gate_w, grad_out], axis=1)
        shard_go = data.reduce(grad_go.reshape(dp, rows_each, -1), 1)
        shard_gate, shard_out = shard_go[:, :width], shard_go[:, width:]
        grad_qkv = sum(mm(r, g, TN) for r, g in zip(rows_one, grad_proj)).astype(LOW)
        grad_forget = sum(mm(z, r) for r, z in zip(rows_one, grad_zf)).astype(LOW)
        grad_forget = grad_forget.reshape(heads, dp, rows_each).transpose(1, 0, 2).reshape(dp, 1, heads * rows_each)
        grad_forget = jnp.pad(grad_forget, ((0, 0), (0, tail - 1), (0, 3 * width - heads * rows_each)))
        packed = jnp.concatenate([grad_qkv.reshape(dp, rows_each, -1), grad_forget], axis=1)
        shard_qkv = data.reduce(packed, -1)
        shard_forget = shard_qkv[rows_each, :heads * rows_each].reshape(heads, rows_each).T
        shard_qkv = shard_qkv[:rows_each]
        bias_local_grad = sum(jnp.sum(z.astype(F32), axis=1) for z in grad_zf)
        terms = [None] * chunks
        back, last = None, (grad_qkv,)
        for i in reversed(range(chunks)):
            t = mm(after(grad_proj[i], *last), w_qkv, NT) + mm(grad_gatepre[i], w_gate, NT)
            terms[i] = (t + mm(grad_zf[i], w_forget, TN)).astype(LOW)
            last = (terms[i],)
            if back is None:
                back = spread_far(terms[i])
        grad_one = spread_near(back, terms[0])
        grad_inputs, gain_one_grad = norm_back(grad_one, inputs_f, scale_one, attn_gain)
        input_grad = grad_inputs + grad_middle

        bias_full = lax.dynamic_update_slice(jnp.zeros(forget_bias.shape, F32), bias_local_grad, (head_first,))
        shards = (shard_qkv, shard_gate, shard_forget, shard_out, shard_up, shard_down)
        square = sum(jnp.sum(s * s) for s in shards)
        pad = 128 - forget_bias.shape[0] - 1
        packed = jnp.concatenate([gain_one_grad, gain_two_grad, bias_full, square[None], jnp.zeros((pad,), F32)])
        packed = Team("dp", dp).add(Team("tensor", tn).add(packed.reshape(-1, 128))).reshape(-1)
        gain_one_sum, gain_two_sum = packed[:dims], packed[dims:2 * dims]
        bias_sum = packed[2 * dims:2 * dims + forget_bias.shape[0]]
        total = (
            packed[2 * dims + forget_bias.shape[0]]
            + jnp.sum(gain_one_sum * gain_one_sum)
            + jnp.sum(gain_two_sum * gain_two_sum)
            + jnp.sum(bias_sum * bias_sum)
        )
        grad_norm = jnp.sqrt(total)
        clip_scale = jnp.minimum(1.0, MAX_NORM / (grad_norm + 1e-06))

        def unflat(s, parts):
            return s.reshape(s.shape[0], parts, -1).transpose(1, 0, 2)

        def adam(weight, gradient, first_old, second_old, decay):
            return adam_step(weight, gradient, first_old, second_old, clip_scale, decay, dims)

        grad_attn = unflat(jnp.concatenate([shard_qkv, shard_gate], axis=1), 4)
        return (
            (outputs, input_grad, grad_norm)
            + adam(qkvg_weight, grad_attn, qkvg_first, qkvg_second, WEIGHT_DECAY)
            + adam(forget_weight, shard_forget, forget_first, forget_second, WEIGHT_DECAY)
            + adam(forget_bias, bias_sum, bias_first, bias_second, 0.0)
            + adam(out_weight, shard_out.T, out_first, out_second, WEIGHT_DECAY)
            + adam(gate_up, unflat(shard_up, 2), gateup_first, gateup_second, WEIGHT_DECAY)
            + adam(down_weight, shard_down.T, down_first, down_second, WEIGHT_DECAY)
            + adam(attn_gain, gain_one_sum, attngain_first, attngain_second, 0.0)
            + adam(feed_gain, gain_two_sum, feedgain_first, feedgain_second, 0.0)
        )

    return body


def solution(mesh):
    tokens = P(("dp", "tensor"), None)
    stack, tall, wide = P(None, "dp", "tensor"), P("dp", "tensor"), P("tensor", "dp")
    return jax.shard_map(
        make_body(mesh.shape["dp"], mesh.shape["tensor"]),
        mesh=mesh,
        in_specs=(tokens, tokens, P("dp"), P("dp"), stack, tall, P(), wide, stack, wide, P(), P())
        + (stack, stack, tall, tall, P(), P(), wide, wide, stack, stack, wide, wide, P(), P(), P(), P()),
        out_specs=(tokens, tokens, P())
        + (stack,) * 3 + (tall,) * 3 + (P(),) * 3 + (wide,) * 3 + (stack,) * 3 + (wide,) * 3 + (P(),) * 6,
        check_vma=False,
    )
```

time: 1650 us -> 834 us (0.51)
  waiting for transfers between devices: 869 us -> 256 us
  matrix products: 351 us -> 182 us
  Pallas kernels: 0 us -> 110 us
  local copies, waits for them, and re-layouts: 161 us -> 58.3 us
  starting transfers between devices: 1.42 us -> 85.6 us
  blocking collectives: 72.4 us -> 0 us
  other arithmetic: 150 us -> 109 us
    all_gather x8 -> x0, waiting for transfers between devices: 355 us -> none  [the longest x1 95.2 us: body(): lax.all_gather(gate_low, 'dp', axis=1, tiled=True)]
    unnamed x18 -> x0, waiting for transfers between devices: 344 us -> none
    ppermute x0 -> x90, waiting for transfers between devices: none -> 256 us  [the longest x56 192 us: step(): lax.ppermute(x, self.axis, [(self.table[r], self.table[(r + way) % n]) fo...]
    reduce_scatter x6 -> x0, waiting for transfers between devices: 170 us -> none  [the longest x4 163 us: spread_rows(): lax.psum_scatter(partial_sum.astype(jnp.bfloat16), 'tensor', scatter_dime...]
    dot_general x29 -> x36, matrix products: 351 us -> 182 us  [mm(): return lax.dot_general(a, b, dims, preferred_element_type=F32)]
    pallas_call x0 -> x8, Pallas kernels: none -> 110 us  [the longest x2 63.3 us: attend_back(): pl.pallas_call(functools.partial(attn_bwd_kernel, hb=hb), grid_spec=pltpu...]
    ppermute x0 -> x90, starting transfers between devices: none -> 85.6 us  [the longest x56 61.8 us: step(): lax.ppermute(x, self.axis, [(self.table[r], self.table[(r + way) % n]) fo...]
    reduce_sum x11 -> x8, other arithmetic: 71 us -> 7.91 us  [the longest x4 6.4 us: body(): square = sum((jnp.sum(s * s) for s in shards))]
  transfers between devices with their start and end apart: 16 -> 90, of which waited for: 12 -> 40; matrix products, arithmetic and copies ran while one was open for 36% -> 32% of each run, Pallas kernels for 0% -> 10%
where the time goes in v1:
time: 834 us; the launch traced here: 826 us
  waiting for transfers between devices  256 us (31%)
  matrix products  182 us (22%)
  Pallas kernels  110 us (13%)
  other arithmetic  109 us (13%)
  starting transfers between devices  85.6 us (10%)
  local copies, waits for them, and re-layouts  58.3 us (7%)
  between operations  25.9 us (3%)
    ppermute x56, waiting for transfers between devices, step(): lax.ppermute(x, self.axis, [(self.table[r], self.table[(r + way) % n]) fo...  192 us
    dot_general x36, matrix products, mm(): return lax.dot_general(a, b, dims, preferred_element_type=F32)  182 us
    pallas_call x2, Pallas kernels, attend_back(): pl.pallas_call(functools.partial(attn_bwd_kernel, hb=hb), grid_spec=pltpu...  63.3 us
    ppermute x24, waiting for transfers between devices, swap(): return lax.ppermute(x, 'tensor', [(i, i ^ bit) for i in range(tn)])  62.7 us
    ppermute x56, starting transfers between devices, step(): lax.ppermute(x, self.axis, [(self.table[r], self.table[(r + way) % n]) fo...  61.8 us
    pallas_call x2, Pallas kernels, attend(): pl.pallas_call(functools.partial(attn_fwd_kernel, hb=hb), grid_spec=pltpu...  36.4 us
    unnamed x293, local copies, waits for them, and re-layouts  30.8 us
    select_n x8, other arithmetic, join(): jnp.where(core == 0, jnp.concatenate([a, b]), jnp.concatenate([b, a]))  24.6 us
  transfers between devices with their start and end apart: 90, of which 40 were waited for; matrix products, arithmetic and copies ran while one was open for 32% of the time, Pallas kernels for 10%

profile of v1, /device:TPU:0, one launch (start us, length us, event | category | flops | bytes accessed | tf_op | source)
XLA Modules:
  0.0 826.0 jit_solution(9155366642853087159)
XLA Ops:
  6.6 10.5 %collective-permute-done.4.refs_7_ = bf16[208,1152]{1,0:T(8,128)(2,1)S(1)} collective-permute-done((bf16[208,1152]{1,0:T(8,128)(2,1)S(1)}, bf16[208,1152]{1,0:T(8,128)(2,1)S(1)}, u32[]{:S(2)}, u32[]{:S(2)}) %collective-permute-start.4) | collective-permute-done | bytes 479264 | tf_op jit(solution)/shard_map/ppermute | solution.py:348
  82.0 12.3 %collective-permute-done.15.refs_6_ = bf16[192,768]{1,0:T(8,128)(2,1)S(1)} collective-permute-done((bf16[192,768]{1,0:T(8,128)(2,1)S(1)}, bf16[192,768]{1,0:T(8,128)(2,1)S(1)}, u32[]{:S(2)}, u32[]{:S(2)}) %collective-permute-start.15) | collective-permute-done | bytes 294944 | tf_op jit(solution)/shard_map/ppermute | solution.py:348
  121.8 17.6 %attend.2 = (f32[1024,384]{1,0:T(8,128)S(1)}, f32[1,3,8,1024]{3,2,1,0:T(8,128)S(1)}) custom-call(s32[1]{0:T(128)} %get-tuple-element.275.start, s32[1]{0:T(128)} %get-tuple-element.268.size, bf16[1024,1152]{1,0:T(8,128)(2,1)} %fusion.10.q_ref.k_ref.v_ref, bf16[1024,1152]{1,0:T(8,128)(2,1)} %fusion.10.q_ref.k_ref.v_ref, ...), custom_call_target="tpu_custom_call" | custom-call | flops 4026531840 | bytes 3932160 | tf_op jit(solution)/shard_map/attend/pallas_call | solution.py:231
  145.7 18.8 %attend.3 = (f32[1024,384]{1,0:T(8,128)S(1)}, f32[1,3,8,1024]{3,2,1,0:T(8,128)S(1)}) custom-call(s32[1]{0:T(128)} %get-tuple-element.276.start, s32[1]{0:T(128)} %get-tuple-element.267.size, bf16[1024,1152]{1,0:T(8,128)(2,1)} %fusion.9.q_ref.k_ref.v_ref, bf16[1024,1152]{1,0:T(8,128)(2,1)} %fusion.9.q_ref.k_ref.v_ref, ...), custom_call_target="tpu_custom_call" | custom-call | flops 4026531840 | bytes 3932160 | tf_op jit(solution)/shard_map/attend/pallas_call | solution.py:231
  177.3 17.7 %collective-permute-done.22.refs_2_ = bf16[192,2048]{1,0:T(8,128)(2,1)S(1)} collective-permute-done((bf16[192,2048]{1,0:T(8,128)(2,1)}, bf16[192,2048]{1,0:T(8,128)(2,1)S(1)}, u32[]{:S(2)}, u32[]{:S(2)}) %collective-permute-start.22) | collective-permute-done | bytes 786464 | tf_op jit(solution)/shard_map/ppermute | solution.py:348
  204.6 7.4 collective-permute-done.29.refs_2_
  215.4 8.9 %collective-permute-done.25.refs_6_ = bf16[192,2048]{1,0:T(8,128)(2,1)S(1)} collective-permute-done((bf16[192,2048]{1,0:T(8,128)(2,1)}, bf16[192,2048]{1,0:T(8,128)(2,1)S(1)}, u32[]{:S(2)}, u32[]{:S(2)}) %collective-permute-start.25) | collective-permute-done | bytes 786464 | tf_op jit(solution)/shard_map/ppermute | solution.py:348
  234.8 8.2 collective-permute-done.39
  295.8 8.9 %fusion.105 = f32[1024,2048]{1,0:T(8,128)} fusion(bf16[1024,1536]{1,0:T(8,128)(2,1)S(1)} %maximum_select_fusion.2, bf16[1536,2048]{1,0:T(8,128)(2,1)S(1)} %place.6), kind=kOutput, calls=%fused_computation.288 | convolution fusion | flops 6442450944 | bytes 17825792 | tf_op jit(solution)/shard_map/dot_general | solution.py:20
  304.8 8.8 %multiply_convert_fusion.4 = (bf16[1024,1024]{1,0:T(8,128)(2,1)S(1)}, bf16[1024,1024]{1,0:T(8,128)(2,1)}, bf16[1024,1024]{1,0:T(8,128)(2,1)}) fusion(f32[1024,2048]{1,0:T(8,128)} %fusion.105, bf16[1024,1536]{1,0:T(8,128)(2,1)S(1)} %maximum_select_fusion.4, bf16[1536,1024]{1,0:T(8,128)(2,1)S(1)} %place.7), kind=kOutput, calls=%fused_computation.28 | convolution fusion | flops 3236954112 | bytes 20971520 | tf_op jit(solution)/shard_map/dot_general | solution.py:20
  313.6 8.9 %convolution_convert_fusion.1 = bf16[1024,1536]{1,0:T(8,128)(2,1)S(1)} fusion(bf16[1536,2048]{1,0:T(8,128)(2,1)S(1)} %place.6, bf16[1024,1024]{1,0:T(8,128)(2,1)} %get-tuple-element.221, bf16[1024,1024]{1,0:T(8,128)(2,1)S(1)} %get-tuple-element.220), kind=kOutput, calls=%fused_computation.34 | convolution fusion | flops 6452412416 | bytes 13631488 | tf_op jit(solution)/shard_map/dot_general | solution.py:20
  337.3 8.9 %fusion.106 = f32[1024,2048]{1,0:T(8,128)} fusion(bf16[1024,1536]{1,0:T(8,128)(2,1)S(1)} %maximum_select_fusion.3, bf16[1536,2048]{1,0:T(8,128)(2,1)S(1)} %place.6), kind=kOutput, calls=%fused_computation.289 | convolution fusion | flops 6442450944 | bytes 17825792 | tf_op jit(solution)/shard_map/dot_general | solution.py:20
  346.3 8.8 %multiply_convert_fusion.1 = (bf16[1024,1024]{1,0:T(8,128)(2,1)}, bf16[1024,1024]{1,0:T(8,128)(2,1)}, bf16[1024,1024]{1,0:T(8,128)(2,1)S(1)}) fusion(f32[1024,2048]{1,0:T(8,128)} %fusion.106, bf16[1024,1536]{1,0:T(8,128)(2,1)S(1)} %maximum_select_fusion.5, bf16[1536,1024]{1,0:T(8,128)(2,1)S(1)} %place.7), kind=kOutput, calls=%fused_computation.23 | convolution fusion | flops 3236954112 | bytes 20971520 | tf_op jit(solution)/shard_map/dot_general | solution.py:20
  361.5 9.7 %convolution_convert_fusion = bf16[1024,1536]{1,0:T(8,128)(2,1)S(1)} fusion(bf16[1536,2048]{1,0:T(8,128)(2,1)S(1)} %place.6, bf16[1024,1024]{1,0:T(8,128)(2,1)} %get-tuple-element.219, bf16[1024,1024]{1,0:T(8,128)(2,1)} %get-tuple-element.218), kind=kOutput, calls=%fused_computation.33 | convolution fusion | flops 6452412416 | bytes 13631488 | tf_op jit(solution)/shard_map/dot_general | solution.py:20
  374.4 9.1 %fusion.84 = f32[1536,2048]{1,0:T(8,128)} fusion(bf16[1024,1536]{1,0:T(8,128)(2,1)S(1)} %maximum_select_fusion.2, bf16[1024,1024]{1,0:T(8,128)(2,1)S(1)} %copy-done.135, bf16[1024,1024]{1,0:T(8,128)(2,1)S(1)} %copy-done.134), kind=kOutput, calls=%fused_computation.282 | convolution fusion | flops 6450839552 | bytes 19922944 | tf_op jit(solution)/shard_map/dot_general | solution.py:20
  384.5 11.2 %add_convert_fusion = bf16[1536,2048]{1,0:T(8,128)(2,1)S(1)} fusion(f32[1536,2048]{1,0:T(8,128)} %fusion.84, bf16[1024,1536]{1,0:T(8,128)(2,1)S(1)} %copy-done.78, bf16[1024,1024]{1,0:T(8,128)(2,1)} %get-tuple-element.219, bf16[1024,1024]{1,0:T(8,128)(2,1)} %get-tuple-element.218), kind=kOutput, calls=%fused_computation.3 | convolution fusion | flops 6457131008 | bytes 26214400 | tf_op jit(solution)/shard_map/dot_general | solution.py:20
  433.9 15.8 %collective-permute-done.73 = bf16[192,2048]{1,0:T(8,128)(2,1)S(1)} collective-permute-done((bf16[192,2048]{1,0:T(8,128)(2,1)S(1)}, bf16[192,2048]{1,0:T(8,128)(2,1)S(1)}, u32[]{:S(2)}, u32[]{:S(2)}) %collective-permute-start.73) | collective-permute-done | bytes 786464 | tf_op jit(solution)/shard_map/ppermute | solution.py:348
  452.1 13.3 %collective-permute-done.45 = bf16[512,1536]{1,0:T(8,128)(2,1)S(1)} collective-permute-done((bf16[512,1536]{1,0:T(8,128)(2,1)S(1)}, bf16[512,1536]{1,0:T(8,128)(2,1)S(1)}, u32[]{:S(2)}, u32[]{:S(2)}) %collective-permute-start.45) | collective-permute-done | bytes 1572896 | tf_op jit(solution)/shard_map/ppermute | solution.py:440
  467.2 29.9 %collective-permute-done.42 = bf16[512,1536]{1,0:T(8,128)(2,1)S(1)} collective-permute-done((bf16[512,1536]{1,0:T(8,128)(2,1)S(1)}, bf16[512,1536]{1,0:T(8,128)(2,1)S(1)}, u32[]{:S(2)}, u32[]{:S(2)}) %collective-permute-start.42) | collective-permute-done | bytes 1572896 | tf_op jit(solution)/shard_map/ppermute | solution.py:440
  509.1 14.1 %collective-permute-done.75 = bf16[192,2048]{1,0:T(8,128)(2,1)S(1)} collective-permute-done((bf16[192,2048]{1,0:T(8,128)(2,1)S(1)}, bf16[192,2048]{1,0:T(8,128)(2,1)S(1)}, u32[]{:S(2)}, u32[]{:S(2)}) %collective-permute-start.75) | collective-permute-done | bytes 786464 | tf_op jit(solution)/shard_map/ppermute | solution.py:348
  535.7 33.4 %attend_back.2 = (bf16[1024,384]{1,0:T(8,128)(2,1)S(1)}, bf16[1024,384]{1,0:T(8,128)(2,1)S(1)}, bf16[1024,384]{1,0:T(8,128)(2,1)S(1)}, f32[1,3,8,1024]{3,2,1,0:T(8,128)S(1)}) custom-call(s32[1]{0:T(128)} %get-tuple-element.276.start, s32[1]{0:T(128)} %get-tuple-element.267.size, bf16[1024,1152]{1,0:T(8,128)(2,1)} %fusion.9.q_ref.k_ref.v_ref, ...), custom_call_target="tpu_custom_call" | custom-call | flops 10066329600 | bytes 7864320 | tf_op jit(solution)/shard_map/attend_back/pallas_call | solution.py:260
  603.2 29.9 %attend_back.3 = (bf16[1024,384]{1,0:T(8,128)(2,1)S(1)}, bf16[1024,384]{1,0:T(8,128)(2,1)S(1)}, bf16[1024,384]{1,0:T(8,128)(2,1)S(1)}, f32[1,3,8,1024]{3,2,1,0:T(8,128)S(1)}) custom-call(s32[1]{0:T(128)} %get-tuple-element.275.start, s32[1]{0:T(128)} %get-tuple-element.268.size, bf16[1024,1152]{1,0:T(8,128)(2,1)} %fusion.10.q_ref.k_ref.v_ref, ...), custom_call_target="tpu_custom_call" | custom-call | flops 10066329600 | bytes 7864320 | tf_op jit(solution)/shard_map/attend_back/pallas_call | solution.py:260
  693.3 8.8 %add_convert_fusion.1 = bf16[1024,1536]{1,0:T(8,128)(2,1)} fusion(f32[1024,1536]{1,0:T(8,128)} %fusion.110, f32[1024,1536]{1,0:T(8,128)} %fusion.52, bf16[1024,1152]{1,0:T(8,128)(2,1)S(1)} %copy-done.99, bf16[1536,1152]{1,0:T(8,128)(2,1)S(1)} %copy-done.38), kind=kOutput, calls=%fused_computation.8 | convolution fusion | flops 3628597248 | bytes 21626880 | tf_op jit(solution)/shard_map/dot_general | solution.py:20
  766.5 11.3 %collective-permute-done.51 = bf16[512,1536]{1,0:T(8,128)(2,1)} collective-permute-done((bf16[512,1536]{1,0:T(8,128)(2,1)}, bf16[512,1536]{1,0:T(8,128)(2,1)}, u32[]{:S(2)}, u32[]{:S(2)}) %collective-permute-start.51) | collective-permute-done | bytes 1572896 | tf_op jit(solution)/shard_map/ppermute | solution.py:440
  (620 shorter events, 467.7 us)
Async XLA Ops:
  20.5 38.4 %collective-permute-start.8 = (bf16[512,1536]{1,0:T(8,128)(2,1)}, bf16[512,1536]{1,0:T(8,128)(2,1)}, u32[]{:S(2)}, u32[]{:S(2)}) collective-permute-start(bf16[512,1536]{1,0:T(8,128)(2,1)} %fusion.11), channel_id=1, source_target_pairs={{0,2},{1,3},{2,0},{3,1},{4,6},{5,7},{6,4},{7,5},{8,10},{9,11},{10,... | collective-permute-start | bytes 4718600 | tf_op jit(solution)/shard_map/ppermute | solution.py:440
  22.0 43.5 %collective-permute-start = (bf16[512,1536]{1,0:T(8,128)(2,1)}, bf16[512,1536]{1,0:T(8,128)(2,1)}, u32[]{:S(2)}, u32[]{:S(2)}) collective-permute-start(bf16[512,1536]{1,0:T(8,128)(2,1)} %fusion.11), channel_id=1, source_target_pairs={{0,1},{1,0},{2,3},{3,2},{4,5},{5,4},{6,7},{7,6},{8,9},{9,8},{10,11... | collective-permute-start | bytes 4718600 | tf_op jit(solution)/shard_map/ppermute | solution.py:440
  58.9 51.8 %collective-permute-start.9 = (bf16[512,1536]{1,0:T(8,128)(2,1)}, bf16[512,1536]{1,0:T(8,128)(2,1)}, u32[]{:S(2)}, u32[]{:S(2)}) collective-permute-start(bf16[512,1536]{1,0:T(8,128)(2,1)} %collective-permute-done.8), channel_id=1, source_target_pairs={{0,1},{1,0},{2,3},{3,2},{4,5},{5,4},{6,7},{7,6},{8,9},{9,8},{10,11... | collective-permute-start | bytes 4718600 | tf_op jit(solution)/shard_map/ppermute | solution.py:440
  68.7 105.6 %collective-permute-start.21 = (bf16[192,2048]{1,0:T(8,128)(2,1)S(1)}, bf16[192,2048]{1,0:T(8,128)(2,1)}, u32[]{:S(2)}, u32[]{:S(2)}) collective-permute-start(bf16[192,2048]{1,0:T(8,128)(2,1)S(1)} %bitcast.293), channel_id=1, source_target_pairs={{0,4},{8,0},{16,8},{24,16},{28,24},{20,28},{12,20},{4,12},{1,5},{9... | collective-permute-start | bytes 2359304 | tf_op jit(solution)/shard_map/ppermute | solution.py:348
  70.4 105.7 %collective-permute-start.24 = (bf16[192,2048]{1,0:T(8,128)(2,1)S(1)}, bf16[192,2048]{1,0:T(8,128)(2,1)}, u32[]{:S(2)}, u32[]{:S(2)}) collective-permute-start(bf16[192,2048]{1,0:T(8,128)(2,1)S(1)} %bitcast.294), channel_id=1, source_target_pairs={{0,8},{8,16},{16,24},{24,28},{28,20},{20,12},{12,4},{4,0},{1,9},{9... | collective-permute-start | bytes 2359304 | tf_op jit(solution)/shard_map/ppermute | solution.py:348
  170.2 41.8 %collective-permute-start.17 = (bf16[512,1536]{1,0:T(8,128)(2,1)S(1)}, bf16[512,1536]{1,0:T(8,128)(2,1)S(1)}, u32[]{:S(2)}, u32[]{:S(2)}) collective-permute-start(bf16[512,1536]{1,0:T(8,128)(2,1)S(1)} %constant_dynamic-slice_fusion.7), channel_id=1, source_target_pairs={{0,1},{1,0},{2,3},{3,2},{4,5},{5,4},{6,7},{7,6},{8,9},{9,8},{10,11... | collective-permute-start | bytes 4718600 | tf_op jit(solution)/shard_map/ppermute | solution.py:440
  172.7 40.4 %collective-permute-start.19 = (bf16[512,1536]{1,0:T(8,128)(2,1)S(1)}, bf16[512,1536]{1,0:T(8,128)(2,1)S(1)}, u32[]{:S(2)}, u32[]{:S(2)}) collective-permute-start(bf16[512,1536]{1,0:T(8,128)(2,1)S(1)} %add_convert_fusion.7), channel_id=1, source_target_pairs={{0,2},{1,3},{2,0},{3,1},{4,6},{5,7},{6,4},{7,5},{8,10},{9,11},{10,... | collective-permute-start | bytes 4718600 | tf_op jit(solution)/shard_map/ppermute | solution.py:440
  175.5 67.5 %collective-permute-start.39 = (bf16[512,1536]{1,0:T(8,128)(2,1)}, bf16[512,1536]{1,0:T(8,128)(2,1)}, u32[]{:S(2)}, u32[]{:S(2)}) collective-permute-start(bf16[512,1536]{1,0:T(8,128)(2,1)} %param.31), channel_id=1, source_target_pairs={{0,2},{1,3},{2,0},{3,1},{4,6},{5,7},{6,4},{7,5},{8,10},{9,11},{10,... | collective-permute-start | bytes 4718600 | tf_op jit(solution)/shard_map/ppermute | solution.py:440
  212.1 70.1 %collective-permute-start.38 = (bf16[512,1536]{1,0:T(8,128)(2,1)}, bf16[512,1536]{1,0:T(8,128)(2,1)}, u32[]{:S(2)}, u32[]{:S(2)}) collective-permute-start(bf16[512,1536]{1,0:T(8,128)(2,1)} %param.31), channel_id=1, source_target_pairs={{0,1},{1,0},{2,3},{3,2},{4,5},{5,4},{6,7},{7,6},{8,9},{9,8},{10,11... | collective-permute-start | bytes 4718600 | tf_op jit(solution)/shard_map/ppermute | solution.py:440
  243.0 46.1 %collective-permute-start.40 = (bf16[512,1536]{1,0:T(8,128)(2,1)}, bf16[512,1536]{1,0:T(8,128)(2,1)}, u32[]{:S(2)}, u32[]{:S(2)}) collective-permute-start(bf16[512,1536]{1,0:T(8,128)(2,1)} %collective-permute-done.39), channel_id=1, source_target_pairs={{0,1},{1,0},{2,3},{3,2},{4,5},{5,4},{6,7},{7,6},{8,9},{9,8},{10,11... | collective-permute-start | bytes 4718600 | tf_op jit(solution)/shard_map/ppermute | solution.py:440
  249.7 42.7 %collective-permute-start.20 = (bf16[512,1536]{1,0:T(8,128)(2,1)}, bf16[512,1536]{1,0:T(8,128)(2,1)}, u32[]{:S(2)}, u32[]{:S(2)}) collective-permute-start(bf16[512,1536]{1,0:T(8,128)(2,1)} %multiply_convert_fusion.6), channel_id=1, source_target_pairs={{0,1},{1,0},{2,3},{3,2},{4,5},{5,4},{6,7},{7,6},{8,9},{9,8},{10,11... | collective-permute-start | bytes 4718600 | tf_op jit(solution)/shard_map/ppermute | solution.py:440
  288.5 34.1 %collective-permute-start.36 = (bf16[512,1536]{1,0:T(8,128)(2,1)}, bf16[512,1536]{1,0:T(8,128)(2,1)S(1)}, u32[]{:S(2)}, u32[]{:S(2)}) collective-permute-start(bf16[512,1536]{1,0:T(8,128)(2,1)} %multiply_convert_fusion.6), channel_id=1, source_target_pairs={{0,2},{1,3},{2,0},{3,1},{4,6},{5,7},{6,4},{7,5},{8,10},{9,11},{10,... | collective-permute-start | bytes 4718600 | tf_op jit(solution)/shard_map/ppermute | solution.py:440
  323.9 126.8 %collective-permute-start.43 = (bf16[512,1536]{1,0:T(8,128)(2,1)}, bf16[512,1536]{1,0:T(8,128)(2,1)S(1)}, u32[]{:S(2)}, u32[]{:S(2)}) collective-permute-start(bf16[512,1536]{1,0:T(8,128)(2,1)} %constant_dynamic-slice_fusion.3), channel_id=1, source_target_pairs={{0,1},{1,0},{2,3},{3,2},{4,5},{5,4},{6,7},{7,6},{8,9},{9,8},{10,11... | collective-permute-start | bytes 4718600 | tf_op jit(solution)/shard_map/ppermute | solution.py:440
  372.5 45.8 %collective-permute-start.44 = (bf16[512,1536]{1,0:T(8,128)(2,1)}, bf16[512,1536]{1,0:T(8,128)(2,1)}, u32[]{:S(2)}, u32[]{:S(2)}) collective-permute-start(bf16[512,1536]{1,0:T(8,128)(2,1)} %constant_dynamic-slice_fusion.2), channel_id=1, source_target_pairs={{0,1},{1,0},{2,3},{3,2},{4,5},{5,4},{6,7},{7,6},{8,9},{9,8},{10,11... | collective-permute-start | bytes 4718600 | tf_op jit(solution)/shard_map/ppermute | solution.py:440
  416.2 51.0 %collective-permute-start.35 = (bf16[512,1536]{1,0:T(8,128)(2,1)S(1)}, bf16[512,1536]{1,0:T(8,128)(2,1)S(1)}, u32[]{:S(2)}, u32[]{:S(2)}) collective-permute-start(bf16[512,1536]{1,0:T(8,128)(2,1)S(1)} %constant_dynamic-slice_fusion.5), channel_id=1, source_target_pairs={{0,1},{1,0},{2,3},{3,2},{4,5},{5,4},{6,7},{7,6},{8,9},{9,8},{10,11... | collective-permute-start | bytes 4718600 | tf_op jit(solution)/shard_map/ppermute | solution.py:440
  428.1 37.3 %collective-permute-start.45 = (bf16[512,1536]{1,0:T(8,128)(2,1)S(1)}, bf16[512,1536]{1,0:T(8,128)(2,1)S(1)}, u32[]{:S(2)}, u32[]{:S(2)}) collective-permute-start(bf16[512,1536]{1,0:T(8,128)(2,1)S(1)} %add_convert_fusion.5), channel_id=1, source_target_pairs={{0,2},{1,3},{2,0},{3,1},{4,6},{5,7},{6,4},{7,5},{8,10},{9,11},{10,... | collective-permute-start | bytes 4718600 | tf_op jit(solution)/shard_map/ppermute | solution.py:440
  433.1 64.0 %collective-permute-start.42 = (bf16[512,1536]{1,0:T(8,128)(2,1)S(1)}, bf16[512,1536]{1,0:T(8,128)(2,1)S(1)}, u32[]{:S(2)}, u32[]{:S(2)}) collective-permute-start(bf16[512,1536]{1,0:T(8,128)(2,1)S(1)} %add_convert_fusion.6), channel_id=1, source_target_pairs={{0,2},{1,3},{2,0},{3,1},{4,6},{5,7},{6,4},{7,5},{8,10},{9,11},{10,... | collective-permute-start | bytes 4718600 | tf_op jit(solution)/shard_map/ppermute | solution.py:440
  449.7 52.8 %collective-permute-start.77 = (bf16[192,2048]{1,0:T(8,128)(2,1)S(1)}, bf16[192,2048]{1,0:T(8,128)(2,1)S(1)}, u32[]{:S(2)}, u32[]{:S(2)}) collective-permute-start(bf16[192,2048]{1,0:T(8,128)(2,1)S(1)} %get-tuple-element.229), channel_id=1, source_target_pairs={{0,8},{8,16},{16,24},{24,28},{28,20},{20,12},{12,4},{4,0},{1,9},{9... | collective-permute-start | bytes 2359304 | tf_op jit(solution)/shard_map/ppermute | solution.py:348
  450.8 51.8 %collective-permute-start.74 = (bf16[192,2048]{1,0:T(8,128)(2,1)S(1)}, bf16[192,2048]{1,0:T(8,128)(2,1)S(1)}, u32[]{:S(2)}, u32[]{:S(2)}) collective-permute-start(bf16[192,2048]{1,0:T(8,128)(2,1)S(1)} %fusion.28), channel_id=1, source_target_pairs={{0,4},{8,0},{16,8},{24,16},{28,24},{20,28},{12,20},{4,12},{1,5},{9... | collective-permute-start | bytes 2359304 | tf_op jit(solution)/shard_map/ppermute | solution.py:348
  507.6 76.4 %collective-permute-start.47 = (bf16[512,1536]{1,0:T(8,128)(2,1)}, bf16[512,1536]{1,0:T(8,128)(2,1)}, u32[]{:S(2)}, u32[]{:S(2)}) collective-permute-start(bf16[512,1536]{1,0:T(8,128)(2,1)} %get-tuple-element.214), channel_id=1, source_target_pairs={{0,2},{1,3},{2,0},{3,1},{4,6},{5,7},{6,4},{7,5},{8,10},{9,11},{10,... | collective-permute-start | bytes 4718600 | tf_op jit(solution)/shard_map/ppermute | solution.py:440
  527.3 67.7 %collective-permute-start.79 = (bf16[192,2048]{1,0:T(8,128)(2,1)}, bf16[192,2048]{1,0:T(8,128)(2,1)}, u32[]{:S(2)}, u32[]{:S(2)}) collective-permute-start(bf16[192,2048]{1,0:T(8,128)(2,1)} %get-tuple-element.225), channel_id=1, source_target_pairs={{0,8},{8,16},{16,24},{24,28},{28,20},{20,12},{12,4},{4,0},{1,9},{9... | collective-permute-start | bytes 2359304 | tf_op jit(solution)/shard_map/ppermute | solution.py:348
  528.1 66.9 %collective-permute-start.76 = (bf16[192,2048]{1,0:T(8,128)(2,1)}, bf16[192,2048]{1,0:T(8,128)(2,1)}, u32[]{:S(2)}, u32[]{:S(2)}) collective-permute-start(bf16[192,2048]{1,0:T(8,128)(2,1)} %get-tuple-element.224), channel_id=1, source_target_pairs={{0,4},{8,0},{16,8},{24,16},{28,24},{20,28},{12,20},{4,12},{1,5},{9... | collective-permute-start | bytes 2359304 | tf_op jit(solution)/shard_map/ppermute | solution.py:348
  657.5 74.4 %collective-permute-start.50 = (bf16[512,1536]{1,0:T(8,128)(2,1)}, bf16[512,1536]{1,0:T(8,128)(2,1)}, u32[]{:S(2)}, u32[]{:S(2)}) collective-permute-start(bf16[512,1536]{1,0:T(8,128)(2,1)} %constant_dynamic-slice_fusion), channel_id=1, source_target_pairs={{0,1},{1,0},{2,3},{3,2},{4,5},{5,4},{6,7},{7,6},{8,9},{9,8},{10,11... | collective-permute-start | bytes 4718600 | tf_op jit(solution)/shard_map/ppermute | solution.py:440
  715.8 50.6 %collective-permute-start.49 = (bf16[512,1536]{1,0:T(8,128)(2,1)}, bf16[512,1536]{1,0:T(8,128)(2,1)S(1)}, u32[]{:S(2)}, u32[]{:S(2)}) collective-permute-start(bf16[512,1536]{1,0:T(8,128)(2,1)} %constant_dynamic-slice_fusion.1), channel_id=1, source_target_pairs={{0,1},{1,0},{2,3},{3,2},{4,5},{5,4},{6,7},{7,6},{8,9},{9,8},{10,11... | collective-permute-start | bytes 4718600 | tf_op jit(solution)/shard_map/ppermute | solution.py:440
  (206 other events, 2433.1 us)

commit v2 on v1

v2 whole, which is shorter than its diff:
```python
import functools

import jax
import jax.numpy as jnp
from jax import lax
from jax.experimental import pallas as pl
from jax.experimental.pallas import tpu as pltpu

HEAD_DIM = 64
PIECE = 256
LOG2E = 1.4426950408889634
LOW = jnp.bfloat16
F32 = jnp.float32
HIDE = -1e30
NT = (((1,), (1,)), ((), ()))
TN = (((0,), (0,)), ((), ()))


def mm(a, b, dims=(((1,), (0,)), ((), ()))):
    return lax.dot_general(a, b, dims, preferred_element_type=F32)


COST_SHARE = 1.0


def cost(flops, moved):
    return pl.CostEstimate(flops=int(flops * COST_SHARE), bytes_accessed=int(moved * COST_SHARE), transcendentals=0)


def split_three(x):
    hi = x.astype(LOW)
    rest = x - hi.astype(F32)
    mid = rest.astype(LOW)
    return hi, mid, (rest - mid.astype(F32)).astype(LOW)


def scan_rows(x, reverse):
    length = x.shape[1]
    row = lax.broadcasted_iota(jnp.int32, (PIECE, PIECE), 0)
    col = lax.broadcasted_iota(jnp.int32, (PIECE, PIECE), 1)
    tri = jnp.where(row >= col if reverse else row <= col, 1.0, 0.0).astype(LOW)
    count = length // PIECE
    out = [None] * count
    carry = None
    for b in reversed(range(count)) if reverse else range(count):
        part = x[:, b * PIECE:(b + 1) * PIECE]
        done = sum(mm(t, tri) for t in split_three(part))
        if carry is not None:
            done = done + carry
        out[b] = done
        carry = done[:, :1] if reverse else done[:, PIECE - 1:]
    return jnp.concatenate(out, axis=1)


def log_gate(zf):
    return jnp.minimum(zf, 0.0) - jnp.log1p(jnp.exp(-jnp.abs(zf)))


def attn_fwd_kernel(start, size, q_ref, k_ref, v_ref, zf_ref, o_ref, lse_ref, *, hb):
    s_at = pl.program_id(0)
    length, width = q_ref.shape
    count = length // PIECE
    first, extent = start[s_at], size[s_at]
    c_rows = scan_rows(log_gate(zf_ref[...]), False) * LOG2E
    c_cols = c_rows.T
    row = lax.broadcasted_iota(jnp.int32, (PIECE, PIECE), 0)
    col = lax.broadcasted_iota(jnp.int32, (PIECE, PIECE), 1)
    causal = col <= row
    lane = lax.broadcasted_iota(jnp.int32, (1, width), 1)
    mine = [(lane >= h * HEAD_DIM) & (lane < (h + 1) * HEAD_DIM) for h in range(hb)]
    spare = [((h + 1) % hb) * HEAD_DIM for h in range(hb)]
    if lse_ref.shape[0] > hb:
        lse_ref[...] = jnp.zeros(lse_ref.shape, F32)

    def block(i, wide):
        lo, hi = i * PIECE, (i + 1) * PIECE
        in_pic = (lo >= first) & (lo < first + extent)
        out, lse = None, None
        for h in range(hb):
            q = jnp.where(mine[h], q_ref[lo:hi, :], jnp.zeros((), LOW))
            c_row = c_rows[h:h + 1, :]
            c_col = c_cols[lo:hi, h:h + 1]
            base = c_row[:, lo:lo + 1]
            parts, spans = [], []
            if i:
                parts.append(mm(q, k_ref[0:lo, :], NT) + (base - c_row[:, :lo]))
                spans.append((0, lo))
            back = base - 2.0 * c_col
            other = jnp.where(in_pic, back + c_row[:, lo:hi], HIDE)
            parts.append(mm(q, k_ref[lo:hi, :], NT) + jnp.where(causal, base - c_row[:, lo:hi], other))
            spans.append((lo, hi))
            if wide:
                parts.append(mm(q, k_ref[hi:hi + PIECE, :], NT) + (back + c_row[:, hi:hi + PIECE]))
                spans.append((hi, hi + PIECE))
            peak = functools.reduce(jnp.maximum, [jnp.max(p, axis=1, keepdims=True) for p in parts])
            acc = None
            for p, (a, b) in zip(parts, spans):
                v = jnp.where(mine[h], v_ref[a:b, :], jnp.ones((), LOW))
                t = mm(jnp.exp2(p - peak).astype(LOW), v)
                acc = t if acc is None else acc + t
            total = acc[:, spare[h]:spare[h] + 1]
            o_h = acc / total
            l_h = jnp.broadcast_to(peak + jnp.log2(total), o_h.shape)
            out = o_h if out is None else jnp.where(mine[h], o_h, out)
            lse = l_h if lse is None else jnp.where(mine[h], l_h, lse)
        o_ref[lo:hi, :] = out
        turned = lse.T
        for h in range(hb):
            lse_ref[h:h + 1, lo:hi] = turned[h * HEAD_DIM:h * HEAD_DIM + 1, :]

    for i in range(count):
        if i + 1 < count:
            wide = (first == i * PIECE) & (extent > PIECE)
            pl.when(wide)(functools.partial(block, i, True))
            pl.when(jnp.logical_not(wide))(functools.partial(block, i, False))
        else:
            block(i, False)


def attn_bwd_kernel(start, size, q_ref, k_ref, v_ref, zf_ref, lse_ref, o_ref, do_ref,
                    dq_ref, dk_ref, dv_ref, dzf_ref, dk_acc, dv_acc, dc_acc, *, hb):
    s_at = pl.program_id(0)
    length, width = q_ref.shape
    count = length // PIECE
    first, extent = start[s_at], size[s_at]
    zf = zf_ref[...]
    c_rows = scan_rows(log_gate(zf), False) * LOG2E
    c_cols = c_rows.T
    row = lax.broadcasted_iota(jnp.int32, (PIECE, PIECE), 0)
    col = lax.broadcasted_iota(jnp.int32, (PIECE, PIECE), 1)
    causal = row <= col
    lane = lax.broadcasted_iota(jnp.int32, (1, width), 1)
    mine = [(lane >= h * HEAD_DIM) & (lane < (h + 1) * HEAD_DIM) for h in range(hb)]
    spare = [((h + 1) % hb) * HEAD_DIM for h in range(hb)]
    zero, one = jnp.zeros((), LOW), jnp.ones((), LOW)
    dk_acc[...] = jnp.zeros(dk_acc.shape, F32)
    dv_acc[...] = jnp.zeros(dv_acc.shape, F32)
    prod = do_ref[...].astype(F32) * o_ref[...].astype(F32)
    head_row = lax.broadcasted_iota(jnp.int32, (8, width), 0)
    head_lane = lax.broadcasted_iota(jnp.int32, (8, width), 1)
    pick = jnp.where((head_lane >= head_row * HEAD_DIM) & (head_lane < (head_row + 1) * HEAD_DIM), 1.0, 0.0).astype(LOW)
    p_hi = prod.astype(LOW)
    p_lo = (prod - p_hi.astype(F32)).astype(LOW)
    delta = mm(pick, p_hi, NT) + mm(pick, p_lo, NT)

    def block(i, wide):
        lo, hi = i * PIECE, (i + 1) * PIECE
        in_pic = (lo >= first) & (lo < first + extent)
        out = None
        for h in range(hb):
            q_all = q_ref[lo:hi, :]
            q = jnp.where(mine[h], q_all, zero)
            q_one = jnp.where(mine[h], q_all, one)
            do = jnp.where(mine[h], do_ref[lo:hi, :], zero)
            c_row = c_rows[h:h + 1, lo:hi]
            base = c_row[:, :1]
            lse = lse_ref[h:h + 1, lo:hi]
            dl = delta[h:h + 1, lo:hi]
            back = base - 2.0 * c_row - lse
            acc = None
            todo = ([(0, lo, 0)] if i else []) + [(lo, hi, 1)] + ([(hi, hi + PIECE, 2)] if wide else [])
            for a, b, kind in todo:
                c_col = c_cols[a:b, h:h + 1]
                st = mm(k_ref[a:b, :], q, NT)
                if kind == 0:
                    st = st + (base - c_col) - lse
                elif kind == 1:
                    other = jnp.where(in_pic, back + c_col, HIDE)
                    st = st + jnp.where(causal, (base - c_col) - lse, other)
                else:
                    st = st + (back + c_col)
                p = jnp.exp2(st)
                ds = p * (mm(v_ref[a:b, :], do, NT) - dl)
                ds = ds.astype(LOW)
                dv_acc[a:b, :] += mm(p.astype(LOW), do)
                k_one = jnp.where(mine[h], k_ref[a:b, :], one)
                if kind == 2:
                    q_one = jnp.where(mine[h], q_all, -one)
                    k_one = jnp.where(mine[h], k_ref[a:b, :], -one)
                dk_acc[h, a:b, :] += mm(ds, q_one)
                t = mm(ds, k_one, TN)
                acc = t if acc is None else acc + t
                if kind == 1:
                    def signs(ds=ds, lo=lo, hi=hi, h=h):
                        minus = jnp.where(causal, zero, ds)
                        m2 = jnp.where(mine[h], zero, jnp.full((), -2.0, LOW))
                        m2 = jnp.broadcast_to(m2, (PIECE, width))
                        dk_acc[h, lo:hi, :] += mm(minus, m2)
                        dc_acc[h] = mm(minus, m2, TN)
                    def none(h=h):
                        dc_acc[h] = jnp.zeros((PIECE, width), F32)
                    pl.when(in_pic)(signs)
                    pl.when(jnp.logical_not(in_pic))(none)
                    acc = acc + dc_acc[h]
            out = acc if out is None else jnp.where(mine[h], acc, out)
            dc_row = acc.T[spare[h]:spare[h] + 1, :]
            dzf_ref[h:h + 1, lo:hi] = dc_row
        dq_ref[lo:hi, :] = (out * HEAD_DIM ** -0.5).astype(LOW)

    if dzf_ref.shape[0] > hb:
        dzf_ref[...] = jnp.zeros(dzf_ref.shape, F32)
    for i in range(count):
        if i + 1 < count:
            wide = (first == i * PIECE) & (extent > PIECE)
            pl.when(wide)(functools.partial(block, i, True))
            pl.when(jnp.logical_not(wide))(functools.partial(block, i, False))
        else:
            block(i, False)
    dv_ref[...] = dv_acc[...].astype(LOW)
    dk = dk_acc[0]
    for h in range(1, hb):
        dk = jnp.where(mine[h], dk_acc[h], dk)
    dk_ref[...] = (dk * (1.0 / LOG2E)).astype(LOW)
    for h in range(hb):
        turned = dk_acc[h].T
        dzf_ref[h:h + 1, :] -= turned[spare[h]:spare[h] + 1, :]
    dlog = scan_rows(dzf_ref[...], True)
    dzf_ref[...] = (dlog * jax.nn.sigmoid(-zf)).astype(LOW).astype(F32)


def head_shapes(width):
    heads = width // HEAD_DIM
    hb = 2 if heads % 2 == 0 else heads
    return hb, heads // hb, hb * HEAD_DIM


def head_specs(qkv, seqs, first=0):
    tokens, width = qkv.shape[0], qkv.shape[1] // 3
    hb, pairs, bw = head_shapes(width)
    length = tokens // seqs

    def col(off):
        return pl.BlockSpec((length, bw), lambda s, p, *_: (s, off + p))

    def rows(off):
        return pl.BlockSpec((None, 8, length), lambda s, p, *_: (off + p, 0, s))

    if bw % 128:
        three, cols = [qkv[:, j * width:(j + 1) * width] for j in range(3)], [col(first)] * 3
    else:
        three, cols = [qkv] * 3, [col(j * pairs + first) for j in range(3)]
    return three, cols, col, rows


def attend(start, size, qkv, zf, seqs):
    tokens, width = qkv.shape[0], qkv.shape[1] // 3
    hb, pairs, bw = head_shapes(width)
    three, cols, col, rows = head_specs(qkv, seqs)
    work = tokens * tokens // seqs * width // HEAD_DIM
    return pl.pallas_call(
        functools.partial(attn_fwd_kernel, hb=hb),
        grid_spec=pltpu.PrefetchScalarGridSpec(
            num_scalar_prefetch=2,
            grid=(seqs, pairs),
            in_specs=cols + [rows(0)],
            out_specs=[col(0), rows(0)],
        ),
        out_shape=[
            jax.ShapeDtypeStruct((tokens, width), F32),
            jax.ShapeDtypeStruct((pairs, 8, tokens), F32),
        ],
        compiler_params=pltpu.CompilerParams(vmem_limit_bytes=40 * 2**20),
        cost_estimate=cost(1600 * work, tokens * width * 10),
        name="attend",
    )(start, size, *three, zf)


def attend_back(start, size, qkv, zf, lse, core, up, seqs, first, count):
    tokens, width = qkv.shape[0], qkv.shape[1] // 3
    hb, pairs, bw = head_shapes(width)
    length = tokens // seqs
    three, cols, col, rows = head_specs(qkv, seqs, first)
    work = tokens * tokens // seqs * hb * count
    return pl.pallas_call(
        functools.partial(attn_bwd_kernel, hb=hb),
        grid_spec=pltpu.PrefetchScalarGridSpec(
            num_scalar_prefetch=2,
            grid=(seqs, count),
            in_specs=cols + [rows(first), rows(first), col(first), col(first)],
            out_specs=[col(0)] * 3 + [rows(0)],
            scratch_shapes=[
                pltpu.VMEM((hb, length, bw), F32),
                pltpu.VMEM((length, bw), F32),
                pltpu.VMEM((hb, PIECE, bw), F32),
            ],
        ),
        out_shape=[jax.ShapeDtypeStruct((tokens, count * bw), LOW)] * 3
        + [jax.ShapeDtypeStruct((count, 8, tokens), F32)],
        compiler_params=pltpu.CompilerParams(vmem_limit_bytes=40 * 2**20),
        cost_estimate=cost(2600 * work, tokens * count * bw * 20),
        name="attend_back",
    )(start, size, *three, zf, lse, core, up)


BLOCK = 256


class Pieces:
    def __init__(self, half, count, rows):
        self.half, self.count, self.rows = half, count, rows
        self.block = min(BLOCK, rows)
        self.each = rows // self.block
        self.steps = count * self.each

    def first(self, p):
        return (self.count - 1 - p) * self.each

    def inside(self, p, i):
        return jnp.clip(i - self.first(p), 0, self.each - 1)

    def active(self, p, i):
        return (i >= self.first(p)) & (i < self.first(p) + self.each)

    def own_spec(self, p, n):
        return pl.BlockSpec((self.block, n), lambda i, *_: (self.inside(p, i), 0))

    def own_specs(self, n):
        return [self.own_spec(p, n) for p in range(self.count)]

    def true_at(self, i, half):
        return half[self.count - 1 - lax.div(i, self.each)] * self.each + lax.rem(i, self.each)

    def true_spec(self, n):
        return pl.BlockSpec((self.block, n), lambda i, half: (self.true_at(i, half), 0))

    def lane_spec(self, lead):
        return pl.BlockSpec(lead + (self.block,), lambda i, half: (0,) * len(lead) + (self.true_at(i, half),))

    def flat_spec(self, n):
        return pl.BlockSpec(
            (self.block, n),
            lambda i, *_: ((self.count - 1 - lax.div(i, self.each)) * self.each + lax.rem(i, self.each), 0),
        )

    def pick(self, refs, i):
        x = refs[0][...]
        for p in range(1, self.count):
            x = jnp.where(self.active(p, i), refs[p][...], x)
        return x

    def put(self, refs, i, value):
        for p in range(self.count):
            def write(p=p):
                refs[p][...] = value
            pl.when(self.active(p, i))(write)

    def shapes(self, n, dtype=LOW):
        return [jax.ShapeDtypeStruct((self.rows, n), dtype)] * self.count

    def all_rows(self):
        return self.count * self.rows

    def call(self, kernel, name, ins, in_specs, out_shapes, out_specs, flops):
        moved = sum(x.size * x.dtype.itemsize for x in ins) + sum(s.size * s.dtype.itemsize for s in out_shapes)
        return pl.pallas_call(
            kernel,
            grid_spec=pltpu.PrefetchScalarGridSpec(
                num_scalar_prefetch=1, grid=(self.steps,), in_specs=in_specs, out_specs=out_specs
            ),
            out_shape=out_shapes,
            compiler_params=pltpu.CompilerParams(vmem_limit_bytes=48 * 2**20),
            cost_estimate=cost(flops * 3 // 2, moved),
            name=name,
        )(self.half, *ins)


def whole(rows, n, at=0):
    return pl.BlockSpec((rows, n), lambda *_: (0, at), pipeline_mode=pl.Buffered(1))


def project(pc, xs, w, wf, bias):
    dims, width = w.shape[0], w.shape[1] // 3
    pairs = wf.shape[0] // 8

    def kernel(half, *refs):
        i = pl.program_id(0)
        w_ref, wf_ref, bias_ref, qkv_ref, zf_ref = refs[pc.count:]
        x = pc.pick(refs[:pc.count], i)
        q = mm(x, w_ref[:, :width]) * (HEAD_DIM**-0.5 * LOG2E)
        qkv_ref[:, :width] = q.astype(LOW)
        qkv_ref[:, width:] = mm(x, w_ref[:, width:]).astype(LOW)
        z = mm(wf_ref[...], x, NT) + bias_ref[...]
        for p in range(pairs):
            zf_ref[p] = z[8 * p:8 * p + 8, :]

    rows = pc.all_rows()
    return pc.call(
        kernel, "project",
        list(xs) + [w, wf, bias],
        pc.own_specs(dims) + [whole(dims, 3 * width), whole(8 * pairs, dims), whole(8 * pairs, 1)],
        [jax.ShapeDtypeStruct((rows, 3 * width), LOW), jax.ShapeDtypeStruct((pairs, 8, rows), F32)],
        [pc.true_spec(3 * width), pc.lane_spec((pairs, 8))],
        6 * rows * dims * width,
    )


def close(pc, xs, core, w_gate, w_out):
    dims, width = w_out.shape

    def kernel(half, *refs):
        i = pl.program_id(0)
        core_ref, wg_ref, w_ref, sig_ref, gated_ref = refs[pc.count:pc.count + 5]
        sig = jax.nn.sigmoid(mm(pc.pick(refs[:pc.count], i), wg_ref[...]))
        sig_ref[...] = sig
        g = (core_ref[...] * sig).astype(LOW)
        gated_ref[...] = g
        pc.put(refs[pc.count + 5:], i, mm(g, w_ref[...], NT).astype(LOW))

    rows = pc.all_rows()
    out = pc.call(
        kernel, "close",
        list(xs) + [core, w_gate, w_out],
        pc.own_specs(dims) + [pc.true_spec(width), whole(dims, width), whole(dims, width)],
        [jax.ShapeDtypeStruct((rows, width), F32), jax.ShapeDtypeStruct((rows, width), LOW)] + pc.shapes(dims),
        [pc.true_spec(width), pc.flat_spec(width)] + pc.own_specs(dims),
        4 * rows * dims * width,
    )
    return out[0], out[1], out[2:]


def feed(pc, xs, ys, w):
    dims, hidden = w.shape[0], w.shape[1] // 3
    n = pc.count

    def kernel(half, *refs):
        i = pl.program_id(0)
        w_ref, hidden_ref, grad_ref = refs[2 * n:2 * n + 3]
        x, y = pc.pick(refs[:n], i), pc.pick(refs[n:2 * n], i)
        a = mm(x, w_ref[:, :hidden])
        sig = jax.nn.sigmoid(a)
        silu = a * sig
        b = mm(x, w_ref[:, hidden:2 * hidden])
        hidden_ref[...] = (silu * b).astype(LOW)
        gh = mm(y, w_ref[:, 2 * hidden:])
        grad_ref[:, :hidden] = (gh * b * sig * (1.0 + a * (1.0 - sig))).astype(LOW)
        grad_ref[:, hidden:] = (gh * silu).astype(LOW)
        pc.put(refs[2 * n + 3:], i, mm(grad_ref[...], w_ref[:, :2 * hidden], NT).astype(LOW))

    rows = pc.all_rows()
    out = pc.call(
        kernel, "feed",
        list(xs) + list(ys) + [w],
        pc.own_specs(dims) * 2 + [whole(dims, 3 * hidden)],
        [jax.ShapeDtypeStruct((rows, hidden), LOW), jax.ShapeDtypeStruct((rows, 2 * hidden), LOW)] + pc.shapes(dims),
        [pc.flat_spec(hidden), pc.flat_spec(2 * hidden)] + pc.own_specs(dims),
        10 * rows * dims * hidden,
    )
    return out[0], out[1], out[2:]


def feed_out(pc, hidden, w):
    dims, n = w.shape[0], w.shape[1] // 3

    def kernel(half, hidden_ref, w_ref, *parts):
        pc.put(parts, pl.program_id(0), mm(hidden_ref[...], w_ref[...], NT).astype(LOW))

    return pc.call(
        kernel, "feed_out", [hidden, w], [pc.flat_spec(n), whole(dims, n, 2)],
        pc.shapes(dims), pc.own_specs(dims), 2 * pc.all_rows() * dims * n,
    )


def open_back(pc, ys, w_out, core, sig):
    dims, width = w_out.shape

    def kernel(half, *refs):
        w_ref, core_ref, sig_ref, up_ref, gate_ref = refs[pc.count:]
        g = mm(pc.pick(refs[:pc.count], pl.program_id(0)), w_ref[...])
        s = sig_ref[...]
        up_ref[...] = (g * s).astype(LOW)
        gate_ref[...] = (g * core_ref[...] * s * (1.0 - s)).astype(LOW)

    rows = pc.all_rows()
    return pc.call(
        kernel, "open_back",
        list(ys) + [w_out, core, sig],
        pc.own_specs(dims) + [whole(dims, width), pc.true_spec(width), pc.true_spec(width)],
        [jax.ShapeDtypeStruct((rows, width), LOW)] * 2,
        [pc.true_spec(width)] * 2,
        2 * rows * dims * width,
    )


def project_back(pc, grads, dz, w_qkv, w_gate, wf):
    dims = w_qkv.shape[0]
    pairs = dz.shape[0]
    n = len(grads)
    width = w_gate.shape[1]

    def kernel(half, *refs):
        dz_ref, w_ref, wg_ref, wf_ref = refs[n:n + 4]
        g = jnp.concatenate([r[...] for r in refs[:n - 1]], axis=1)
        total = mm(g, w_ref[...], NT) + mm(refs[n - 1][...], wg_ref[...], NT)
        z = jnp.concatenate([dz_ref[p] for p in range(pairs)], axis=0).astype(LOW)
        total = total + mm(z, wf_ref[...], TN)
        pc.put(refs[n + 4:], pl.program_id(0), total.astype(LOW))

    return pc.call(
        kernel, "project_back",
        list(grads) + [dz, w_qkv, w_gate, wf],
        [pc.true_spec(g.shape[1]) for g in grads]
        + [pc.lane_spec((pairs, 8)), whole(dims, 3 * width), whole(dims, width), whole(8 * pairs, dims)],
        pc.shapes(dims), pc.own_specs(dims), 8 * pc.all_rows() * dims * width,
    )


def weight_grads(pc, groups, name, step):
    dims = groups[0][0][0][0].shape[1]
    ins, specs, plan, at = [], [], [], 0
    flops = 0
    for group in groups:
        terms = []
        for lefts, (right, n, c), true in group:
            for p, left in enumerate(lefts):
                terms.append((len(ins), len(ins) + 1))
                ins += [left, right]
                specs.append(pl.BlockSpec((pc.rows, step), lambda i, *_: (0, i)))
                if true:
                    spec = pl.BlockSpec((pc.rows, n), lambda i, half, p=p, c=c: (half[p], c), pipeline_mode=pl.Buffered(1))
                else:
                    spec = pl.BlockSpec((pc.rows, n), lambda i, *_, p=p, c=c: (p, c), pipeline_mode=pl.Buffered(1))
                specs.append(spec)
                flops += 2 * pc.rows * dims * n
        plan.append((terms, at, n))
        at += n

    def kernel(half, *refs):
        out = refs[-1]
        for terms, at, n in plan:
            total = None
            for a, b in terms:
                t = mm(refs[a][...], refs[b][...], TN)
                total = t if total is None else total + t
            out[:, at:at + n] = total.astype(LOW)

    return pl.pallas_call(
        kernel,
        grid_spec=pltpu.PrefetchScalarGridSpec(
            num_scalar_prefetch=1, grid=(dims // step,), in_specs=specs,
            out_specs=pl.BlockSpec((step, at), lambda i, *_: (i, 0)),
        ),
        out_shape=jax.ShapeDtypeStruct((dims, at), LOW),
        compiler_params=pltpu.CompilerParams(vmem_limit_bytes=50 * 2**20),
        cost_estimate=cost(flops * 3 // 2, dims * at * 6),
        name=name,
    )(pc.half, *ins)


def project_grads(pc, chunks, size, tail, n):
    dims = chunks[0][0][0].shape[1]
    step = 384
    per = step // size
    cols = len(chunks[0][1])
    pairs = chunks[0][2].shape[0] if tail else 0
    ins, specs, plan = [], [], []
    for lefts, grads, dz in chunks:
        for p, left in enumerate(lefts):
            plan.append(len(ins))
            ins += [left] + [g for g, _ in grads]
            specs.append(pl.BlockSpec((pc.rows, step), lambda i, *_: (0, i)))
            for _, c in grads:
                specs.append(
                    pl.BlockSpec((pc.rows, n), lambda i, half, p=p, c=c: (half[p], c), pipeline_mode=pl.Buffered(1))
                )
            if tail:
                ins.append(dz)
                specs.append(pl.BlockSpec((pairs, 8, pc.rows), lambda i, half, p=p: (0, 0, half[p])))

    def kernel(half, *refs):
        out = refs[-1]
        for c in range(cols):
            total = None
            for at in plan:
                t = mm(refs[at][...], refs[at + 1 + c][...], TN)
                total = t if total is None else total + t
            total = total.astype(LOW)
            for b in range(per):
                out[b, :size, c * n:(c + 1) * n] = total[b * size:(b + 1) * size]
        if not tail:
            return
        total = None
        for at in plan:
            z = jnp.concatenate([refs[at + 1 + cols][p] for p in range(pairs)], axis=0).astype(LOW)
            t = mm(z, refs[at][...])
            total = t if total is None else total + t
        hb = tail_heads
        heads = [total[8 * p:8 * p + hb] for p in range(pairs)]
        heads.append(jnp.zeros((tail - hb * pairs, step), F32))
        total = jnp.concatenate(heads, axis=0)
        for b in range(per):
            row = total[:, b * size:(b + 1) * size]
            row = jnp.concatenate([row, jnp.zeros((tail, cols * n - size), F32)], axis=1)
            out[b, size:, :] = row.astype(LOW)

    tail_heads = head_shapes(n)[0]
    return pl.pallas_call(
        kernel,
        grid_spec=pltpu.PrefetchScalarGridSpec(
            num_scalar_prefetch=1, grid=(dims // step,), in_specs=specs,
            out_specs=pl.BlockSpec((per, size + tail, cols * n), lambda i, *_: (i, 0, 0)),
        ),
        out_shape=jax.ShapeDtypeStruct((dims // size, size + tail, cols * n), LOW),
        compiler_params=pltpu.CompilerParams(vmem_limit_bytes=50 * 2**20),
        cost_estimate=cost(12 * pc.rows * dims * cols * n, dims * cols * n * 6),
        name="project_grads",
    )(pc.half, *ins)


from jax.sharding import PartitionSpec as P

NORM_EPS = 1e-05
BETA_ONE = 0.9
BETA_TWO = 0.95
WEIGHT_DECAY = 0.1
ADAM_EPS = 1e-08
MAX_NORM = 1.0
STEP_COUNT = 10.0


def rms_scale(values):
    return lax.rsqrt(jnp.mean(values * values, axis=-1, keepdims=True) + NORM_EPS)


def norm_back(gradient, values, inv_scale, gain_row):
    normed = values * inv_scale
    scaled = gradient * gain_row
    backward = inv_scale * (scaled - normed * jnp.mean(scaled * normed, axis=-1, keepdims=True))
    return (backward, jnp.sum(gradient * normed, axis=0))


def adam_step(weight, gradient, first_old, second_old, clip_scale, decay_rate, width):
    learn_rate = 0.4 / width**0.5
    scaled = gradient * clip_scale
    first_new = BETA_ONE * first_old + (1.0 - BETA_ONE) * scaled
    second_new = BETA_TWO * second_old + (1.0 - BETA_TWO) * scaled * scaled
    update = (
        first_new
        / (1.0 - BETA_ONE**STEP_COUNT)
        / (jnp.sqrt(second_new / (1.0 - BETA_TWO**STEP_COUNT)) + ADAM_EPS)
    )
    return (-learn_rate * (update + decay_rate * weight), first_new, second_new)


def after(x, *done):
    return lax.optimization_barrier((x,) + done)[0]


def index(x, i, axis):
    return lax.dynamic_index_in_dim(x, i, axis, keepdims=False, allow_negative_indices=False)


class Ring:
    def __init__(self, axis, size):
        self.axis, self.size = axis, size
        if size == 8:
            self.table = list(range(0, size, 2)) + list(range(size - 1, 0, -2))
        else:
            self.table = list(range(size))
        spot = [self.table.index(i) for i in range(size)]
        ahead = [[self.table[(spot[i] + k) % size] for k in range(size)] for i in range(size)]
        self.ahead = index(jnp.asarray(ahead, jnp.int32), lax.axis_index(axis), 0)

    def step(self, x, way):
        n = self.size
        return lax.ppermute(x, self.axis, [(self.table[r], self.table[(r + way) % n]) for r in range(n)])

    def gather(self, x, way):
        return Gather(self, x, way)

    def reduce(self, x, way):
        return Reduce(self, x, way)


class Gather:
    def __init__(self, ring, x, way):
        self.ring, self.way, self.k = ring, way, 0
        self.blocks = {0: x}
        self.ends = [x, x]

    def step(self, *done):
        ring, n = self.ring, self.ring.size
        self.k += 1
        if self.k > 1 or done:
            self.ends = list(lax.optimization_barrier(tuple(self.ends) + done)[:2])
        self.ends[0] = ring.step(self.ends[0], self.way)
        self.blocks[-self.k * self.way % n] = self.ends[0]
        if self.k <= (n - 1) // 2:
            self.ends[1] = ring.step(self.ends[1], -self.way)
            self.blocks[self.k * self.way % n] = self.ends[1]
        return self.ends

    def all(self):
        while self.k < self.ring.size // 2:
            self.step()
        return [self.blocks[k] for k in range(self.ring.size)]


class Reduce:
    def __init__(self, ring, x, way):
        self.ring, self.x, self.k = ring, x, 0
        n = ring.size
        self.ways = ((way, n // 2), (-way, (n - 1) // 2))
        self.moving = [None, None]

    def block(self, k):
        return index(self.x, index(self.ring.ahead, k % self.ring.size, 0), 0)

    def step(self, *done):
        self.k += 1
        if self.k > 1:
            tied = lax.optimization_barrier(tuple(self.moving) + done)
            self.moving = list(tied[:2])
        for j, (way, far) in enumerate(self.ways):
            left = far - self.k + 1
            if left < 1:
                continue
            own = self.block(way * left)
            if self.k > 1:
                own = (self.moving[j].astype(F32) + own.astype(F32)).astype(LOW)
            self.moving[j] = self.ring.step(own, way)
        return self.moving

    def all(self):
        while self.k < self.ring.size // 2:
            self.step()
        return sum(m.astype(F32) for m in self.moving if m is not None) + self.block(0).astype(F32)


def sum_all(x, axis, size):
    bit = 1
    while bit < size:
        x = x + lax.ppermute(x, axis, [(i, i ^ bit) for i in range(size)])
        bit *= 2
    return x


def place_kernel(where, *refs, arrays, size, rows, tail):
    out, sem = refs[arrays], refs[-1]
    copies = []
    block = 0
    for ref in refs[:arrays]:
        for j in range(ref.shape[0] // size):
            spans = [(out, rows, j * size)] + ([(refs[arrays + 1], tail, j * size + rows)] if tail else [])
            for to, count, at in spans:
                to_at = pl.multiple_of(where[block] * count, count)
                copies.append(
                    pltpu.make_async_copy(
                        ref.at[pl.ds(at, count), :], to.at[pl.ds(to_at, count), :], sem.at[len(copies)]
                    )
                )
            block += 1
    for copy in copies:
        copy.start()
    for copy in copies:
        copy.wait()


def place(parts, where, size, tail=0):
    n = parts[0].shape[1]
    count = sum(p.shape[0] for p in parts) // size
    shapes = [jax.ShapeDtypeStruct((count * r, n), LOW) for r in (size - tail, tail) if r]
    out = pl.pallas_call(
        functools.partial(place_kernel, arrays=len(parts), size=size, rows=size - tail, tail=tail),
        in_specs=[pl.BlockSpec(memory_space=pltpu.SMEM)] + [pl.BlockSpec(memory_space=pl.ANY)] * len(parts),
        out_specs=[pl.BlockSpec(memory_space=pltpu.VMEM)] * len(shapes),
        out_shape=shapes,
        scratch_shapes=[pltpu.SemaphoreType.DMA((2 * count,))],
        compiler_params=pltpu.CompilerParams(vmem_limit_bytes=40 * 2**20),
        cost_estimate=cost(0, 4 * count * size * n),
        name="place",
    )(where, *parts)
    return out if tail else out[0]


def make_body(dp, tn):
    def body(
        inputs, cotangent, picture_start, picture_length,
        qkvg_weight, forget_weight, forget_bias, out_weight, gate_up, down_weight,
        attn_gain, feed_gain,
        qkvg_first, qkvg_second, forget_first, forget_second, bias_first, bias_second,
        out_first, out_second, gateup_first, gateup_second, down_first, down_second,
        attngain_first, attngain_second, feedgain_first, feedgain_second,
    ):
        dims = inputs.shape[1]
        local, rank_rows, width = inputs.shape[0], qkvg_weight.shape[1], qkvg_weight.shape[2]
        hidden_size = gate_up.shape[2]
        heads = forget_weight.shape[1]
        seqs = picture_start.shape[0]
        rows_group = local * tn
        length = rows_group // seqs
        data = Ring("dp", dp)
        rank = lax.axis_index("tensor")
        paired = tn == 4 and local * 2 == length
        core, side = lax.rem(rank, 2), lax.div(rank, 2)
        rows_each = dims // dp

        def swap(x, bit):
            return lax.ppermute(x, "tensor", [(i, i ^ bit) for i in range(tn)])

        def rows_start(x):
            if not paired:
                return [lax.all_gather(x, "tensor", axis=0, tiled=True)], None
            return [x, swap(x, 1)], swap(x, 2)

        def far(moved, *done):
            there = after(moved[1], *done) if done else moved[1]
            return [there, swap(there, 1)]

        def spread_far(parts, count=1):
            if not paired:
                return parts[0], [lax.psum_scatter(parts[0], "tensor", scatter_dimension=0, tiled=True)]
            both = (parts[0].astype(F32) + swap(parts[1], 1).astype(F32)).astype(LOW)
            came, size = [], local // count
            for k in range(count):
                came.append(swap(after(both[k * size:(k + 1) * size], *came[-1:]), 2))
            return both, came

        def spread_own(parts, *done):
            return [parts[0], swap(after(parts[1], *done), 1)] if paired else []

        def spread_sum(back, own):
            total = jnp.concatenate(back).astype(F32)
            for p in own:
                total = total + p.astype(F32)
            return total

        if paired:
            pc = Pieces(jnp.stack([core, 1 - core]).astype(jnp.int32), 2, local)
        else:
            pc = Pieces(jnp.zeros((1,), jnp.int32), 1, rows_group)

        if paired:
            order = [side, 1 - side]
            starts = [index(picture_start.reshape(2, 1), o, 0) for o in order]
            sizes = [index(picture_length.reshape(2, 1), o, 0) for o in order]
            seqs_each = 1
        else:
            starts, sizes, seqs_each = [picture_start], [picture_length], seqs
        chunks = len(starts)
        hb, pairs, _ = head_shapes(width)

        def flat(w):
            return w.transpose(1, 0, 2).reshape(w.shape[1], -1).astype(LOW)

        now = [()]

        def at(x):
            return after(x, *now[0])

        def done(*xs):
            now[0] = tuple(x for x in xs if x is not None)

        inputs_f = inputs.astype(F32)
        tail = 16
        forget_row = forget_weight.T.astype(LOW)
        forget_row = jnp.pad(forget_row, ((0, tail - heads), (0, 3 * width - rows_each)))
        pack = jnp.concatenate([flat(qkvg_weight[:3]), forget_row])
        ring_one = data.gather(pack, 1)
        ring_one.step()
        scale_one = rms_scale(inputs_f)
        normed_one = after((inputs_f * scale_one * attn_gain).astype(LOW), pack)
        low_go = jnp.concatenate([after(qkvg_weight[3], normed_one), out_weight.T], axis=1).astype(LOW)
        low_feed = jnp.concatenate([flat(after(gate_up, normed_one)), down_weight.T.astype(LOW)], axis=1)
        if paired:
            near, came = [normed_one, swap(normed_one, 1)], []
            for k in range(2):
                part = normed_one[k * local // 2:(k + 1) * local // 2]
                if k:
                    ring_one.step()
                    part = after(part, came[-1])
                    ring_one.step(came[-1])
                came.append(swap(part, 2))
            move_one = (near, jnp.concatenate(came))
        else:
            move_one = rows_start(normed_one)
        blocks = ring_one.all()
        w_qkv, w_tail = place([after(blocks[0], low_feed)] + blocks[1:], data.ahead, rows_each + tail, tail)
        w_forget = w_tail.reshape(dp, tail, -1)[:, :heads, :rows_each].transpose(1, 0, 2)
        w_forget = jnp.pad(w_forget.reshape(pairs, hb, dims), ((0, 0), (0, 8 - hb), (0, 0))).reshape(-1, dims)
        bias_local = index(forget_bias.reshape(tn, heads), rank, 0)
        bias_local = jnp.pad(bias_local.reshape(pairs, hb), ((0, 0), (0, 8 - hb))).reshape(-1, 1)
        w_feed = lax.all_gather(after(low_feed, blocks[-1], blocks[dp // 2]), "dp", axis=0, tiled=True)
        done(w_qkv)
        ring_go = data.gather(at(low_go), -1)
        ring_go.step()
        rows_one = [move_one[0]]
        if paired:
            rows_one.append(far(move_one))
        move_feed = rows_start(after(cotangent, rows_one[-1][0]))

        qkv, zf, attended, gate_sig, gated = ([None] * chunks for _ in range(5))
        for i in range(chunks):
            first = at(rows_one[i][0])
            qkv[i], zf[i] = project(pc, [first] + rows_one[i][1:], w_qkv, w_forget, bias_local)
            done(qkv[i])
        ring_go.step(qkv[-1])
        back, own = None, []
        feed_grad = [move_feed[0]]
        for i in reversed(range(chunks)):
            attended[i] = attend(starts[i], sizes[i], at(qkv[i]), zf[i], seqs_each)
            done(attended[i][0])
            ring_go.step(attended[i][0])
        w_go = place([at(ring_go.blocks[0])] + ring_go.all()[1:], data.ahead, rows_each)
        w_gate, w_out = w_go[:, :width], w_go[:, width:]
        if paired:
            feed_grad.append(far(move_feed))
        done(attended[0][0], w_go)
        for i in reversed(range(chunks)):
            gate_sig[i], gated[i], parts = close(
                pc, [at(rows_one[i][0])] + rows_one[i][1:], attended[i][0], w_gate, w_out
            )
            if back is None:
                sent, back = spread_far(parts)
                done(sent, feed_grad[-1][-1])
            else:
                own = spread_own(parts, back[0])
                done(gated[i], *own)
        middle = inputs_f + spread_sum(back, own)
        scale_two = rms_scale(middle)
        normed_two = (middle * scale_two * feed_gain).astype(LOW)
        move_two = rows_start(normed_two)

        hidden, grad_act, rows_two = ([None] * chunks for _ in range(3))
        done(w_feed)
        for i in range(chunks):
            rows_two[i] = far(move_two, *now[0]) if i else move_two[0]
            hidden[i], grad_act[i], parts = feed(
                pc, [at(rows_two[i][0])] + rows_two[i][1:], feed_grad[i], w_feed
            )
            done(hidden[i])
            if i == 0:
                own = spread_own(parts)
                done(hidden[i], *own)
            if i == chunks - 1:
                sent, back = spread_far(parts)
                done(sent)
        lefts = [[at(r[0])] + r[1:] for r in rows_two]
        groups = [
            [(r, (g, 2 * hidden_size, 0), False) for r, g in zip(lefts, grad_act)],
            [(y, (h, hidden_size, 0), False) for y, h in zip(feed_grad, hidden)],
        ]
        grad_feed = weight_grads(pc, groups, "grad_feed", 256)
        done(grad_feed)
        shard_feed = lax.psum_scatter(after(grad_feed, back[0]), "dp", scatter_dimension=0, tiled=True).astype(F32)
        shard_up, shard_down = shard_feed[:, :2 * hidden_size], shard_feed[:, 2 * hidden_size:]
        grad_two = spread_sum([after(back[0], grad_feed)], own)
        grad_middle, gain_two_grad = norm_back(grad_two, middle, scale_two, feed_gain)
        grad_middle = grad_middle + cotangent.astype(F32)
        grad_low = grad_middle.astype(LOW)
        done(grad_low)
        move_back = rows_start(grad_low)
        out_parts = [None] * chunks
        out_parts[-1] = feed_out(pc, at(hidden[-1]), w_feed)
        done(out_parts[-1][0])

        grad_gatepre, grad_proj, grad_zf, attn_grad = ([None] * chunks for _ in range(4))
        for i in range(chunks):
            attn_grad[i] = far(move_back, grad_proj[i - 1][0]) if i else move_back[0]
            up_stream, grad_gatepre[i] = open_back(
                pc, [at(attn_grad[i][0])] + attn_grad[i][1:], w_out, attended[i][0], gate_sig[i]
            )
            done(up_stream)
            if i == chunks - 1:
                groups = [
                    [([at(r[0])] + r[1:], (g, width, 0), True) for r, g in zip(rows_one, grad_gatepre)],
                    [(y, (g, width, 0), False) for y, g in zip(attn_grad, gated)],
                ]
                grad_go = weight_grads(pc, groups, "grad_gate_out", 512)
                done(grad_go)
                ring_go = data.reduce(grad_go.reshape(dp, rows_each, -1), 1)
                ring_go.step()
                sent, out_back = spread_far([after(p, attn_grad[i][-1]) for p in out_parts[-1]])
                done(grad_go, sent)
            *grad_proj[i], grad_zf[i] = attend_back(
                starts[i], sizes[i], qkv[i], zf[i], attended[i][1], attended[i][0], at(up_stream), seqs_each, 0, pairs
            )
            done(grad_proj[i][0])
            if i < chunks - 1:
                out_parts[i] = feed_out(pc, at(hidden[i]), w_feed)
                done(out_parts[i][0])
        ring_go.step(grad_proj[-1][0])
        bias_local_grad = sum(jnp.sum(z[:, :hb], axis=2).reshape(heads) for z in grad_zf)
        done(grad_proj[-1][0], *out_back)
        back, own = None, []
        for i in reversed(range(chunks)):
            g = list(grad_proj[i])
            parts = project_back(pc, [at(g[0])] + g[1:] + [grad_gatepre[i]], grad_zf[i], w_qkv, w_gate, w_forget)
            if back is None:
                sent, back = spread_far(parts, 2)
                done(sent)
            else:
                own = spread_own(parts, back[-1])
                done(parts[0], back[0])
        ring_go.step(back[0])
        packed = project_grads(
            pc,
            [([at(r[0])] + r[1:], [(x, 0) for x in g], z) for r, g, z in zip(rows_one, grad_proj, grad_zf)],
            rows_each, tail, width,
        )
        packed = after(packed, back[-1])
        ring_go.step(packed)
        ring_qkv = data.reduce(packed, -1)
        ring_qkv.step()
        outputs = middle + spread_sum(out_back, spread_own(out_parts[0]) if paired else [])
        shard_go = ring_go.all()
        shard_gate, shard_out = shard_go[:, :width], shard_go[:, width:]
        shard_qkv = ring_qkv.all()
        shard_forget = shard_qkv[rows_each:rows_each + heads, :rows_each].T
        shard_qkv = shard_qkv[:rows_each]
        grad_one = spread_sum(back, own)
        grad_inputs, gain_one_grad = norm_back(grad_one, inputs_f, scale_one, attn_gain)
        input_grad = grad_inputs + grad_middle

        bias_full = jnp.where(jnp.arange(tn)[:, None] == rank, bias_local_grad[None], 0.0).reshape(-1)
        owned = (shard_qkv, shard_gate, shard_forget, shard_out, shard_up, shard_down)
        square = sum(jnp.sum(s * s) for s in owned)
        pad = 128 - forget_bias.shape[0] - 1
        packed = jnp.concatenate([gain_one_grad, gain_two_grad, bias_full, square[None], jnp.zeros((pad,), F32)])
        packed = sum_all(sum_all(packed.reshape(-1, 128), "tensor", tn), "dp", dp).reshape(-1)
        gain_one_sum, gain_two_sum = packed[:dims], packed[dims:2 * dims]
        bias_sum = packed[2 * dims:2 * dims + forget_bias.shape[0]]
        total = (
            packed[2 * dims + forget_bias.shape[0]]
            + jnp.sum(gain_one_sum * gain_one_sum)
            + jnp.sum(gain_two_sum * gain_two_sum)
            + jnp.sum(bias_sum * bias_sum)
        )
        grad_norm = jnp.sqrt(total)
        clip_scale = jnp.minimum(1.0, MAX_NORM / (grad_norm + 1e-06))

        def unflat(s, parts):
            return s.reshape(s.shape[0], parts, -1).transpose(1, 0, 2)

        def adam(weight, gradient, first_old, second_old, decay):
            return adam_step(weight, gradient, first_old, second_old, clip_scale, decay, dims)

        grad_attn = unflat(jnp.concatenate([shard_qkv, shard_gate], axis=1), 4)
        return (
            (outputs, input_grad, grad_norm)
            + adam(qkvg_weight, grad_attn, qkvg_first, qkvg_second, WEIGHT_DECAY)
            + adam(forget_weight, shard_forget, forget_first, forget_second, WEIGHT_DECAY)
            + adam(forget_bias, bias_sum, bias_first, bias_second, 0.0)
            + adam(out_weight, shard_out.T, out_first, out_second, WEIGHT_DECAY)
            + adam(gate_up, unflat(shard_up, 2), gateup_first, gateup_second, WEIGHT_DECAY)
            + adam(down_weight, shard_down.T, down_first, down_second, WEIGHT_DECAY)
            + adam(attn_gain, gain_one_sum, attngain_first, attngain_second, 0.0)
            + adam(feed_gain, gain_two_sum, feedgain_first, feedgain_second, 0.0)
        )

    return body


def solution(mesh):
    tokens = P(("dp", "tensor"), None)
    stack, tall, wide = P(None, "dp", "tensor"), P("dp", "tensor"), P("tensor", "dp")
    return jax.shard_map(
        make_body(mesh.shape["dp"], mesh.shape["tensor"]),
        mesh=mesh,
        in_specs=(tokens, tokens, P("dp"), P("dp"), stack, tall, P(), wide, stack, wide, P(), P())
        + (stack, stack, tall, tall, P(), P(), wide, wide, stack, stack, wide, wide, P(), P(), P(), P()),
        out_specs=(tokens, tokens, P())
        + (stack,) * 3 + (tall,) * 3 + (P(),) * 3 + (wide,) * 3 + (stack,) * 3 + (wide,) * 3 + (P(),) * 6,
        check_vma=False,
    )
```

time: 834 us -> 685 us (0.82)
  matrix products: 182 us -> 0 us
  Pallas kernels: 110 us -> 286 us
  waiting for transfers between devices: 256 us -> 197 us
  other arithmetic: 109 us -> 79.8 us
  starting transfers between devices: 85.6 us -> 56.8 us
  local copies, waits for them, and re-layouts: 58.3 us -> 35.5 us
    dot_general x36 -> x0, matrix products: 182 us -> none  [mm(): return lax.dot_general(a, b, dims, preferred_element_type=F32)]
    pallas_call x4 -> x17, Pallas kernels: 10.1 us -> 191 us  [the longest x12 132 us: call(): pl.pallas_call(kernel, grid_spec=pltpu.PrefetchScalarGridSpec(num_scalar_...]
    ppermute x56 -> x28, waiting for transfers between devices: 192 us -> 101 us  [step(): lax.ppermute(x, self.axis, [(self.table[r], self.table[(r + way) % n]) fo...]
    ppermute x56 -> x28, starting transfers between devices: 61.8 us -> 34.7 us  [step(): lax.ppermute(x, self.axis, [(self.table[r], self.table[(r + way) % n]) fo...]
    ppermute x24 -> x26, waiting for transfers between devices: 62.7 us -> 89.2 us  [swap(): return lax.ppermute(x, 'tensor', [(i, i ^ bit) for i in range(tn)])]
    select_n x12 -> x1, other arithmetic: 25.3 us -> 0.07 us  [body(): jnp.where(jnp.arange(tn)[:, None] == rank, bias_local_grad[None], 0.0)]
    ppermute x10 -> x5, starting transfers between devices: 12.5 us -> 3.86 us  [sum_all(): x = x + lax.ppermute(x, axis, [(i, i ^ bit) for i in range(size)])]
    unnamed x293 -> x220, local copies, waits for them, and re-layouts: 30.8 us -> 23.7 us
  transfers between devices with their start and end apart: 90 -> 61, of which waited for: 40 -> 37; matrix products, arithmetic and copies ran while one was open for 32% -> 10% of each run, Pallas kernels for 10% -> 38%
where the time goes in v2:
time: 685 us; the launch traced here: 679 us
  Pallas kernels  286 us (42%)
  waiting for transfers between devices  197 us (29%)
  other arithmetic  79.8 us (12%)
  starting transfers between devices  56.8 us (8%)
  local copies, waits for them, and re-layouts  35.5 us (5%)
  between operations  23.6 us (3%)
    pallas_call x12, Pallas kernels, call(): pl.pallas_call(kernel, grid_spec=pltpu.PrefetchScalarGridSpec(num_scalar_...  132 us
    ppermute x28, waiting for transfers between devices, step(): lax.ppermute(x, self.axis, [(self.table[r], self.table[(r + way) % n]) fo...  101 us
    ppermute x26, waiting for transfers between devices, swap(): return lax.ppermute(x, 'tensor', [(i, i ^ bit) for i in range(tn)])  89.2 us
    pallas_call x2, Pallas kernels, attend_back(): pl.pallas_call(functools.partial(attn_bwd_kernel, hb=hb), grid_spec=pltpu...  61.8 us
    pallas_call x2, Pallas kernels, weight_grads(): pl.pallas_call(kernel, grid_spec=pltpu.PrefetchScalarGridSpec(num_scalar_...  39.3 us
    ppermute x28, starting transfers between devices, step(): lax.ppermute(x, self.axis, [(self.table[r], self.table[(r + way) % n]) fo...  34.7 us
    pallas_call x2, Pallas kernels, attend(): pl.pallas_call(functools.partial(attn_fwd_kernel, hb=hb), grid_spec=pltpu...  33.8 us
    unnamed x220, local copies, waits for them, and re-layouts  23.7 us
  transfers between devices with their start and end apart: 61, of which 37 were waited for; matrix products, arithmetic and copies ran while one was open for 10% of the time, Pallas kernels for 38%

profile of v2, /device:TPU:0, one launch (start us, length us, event | category | flops | bytes accessed | tf_op | source)
XLA Modules:
  0.0 679.1 jit_solution(4568733483780857140)
XLA Ops:
  39.8 8.2 %collective-permute-done.6.refs_3_ = bf16[208,1152]{1,0:T(8,128)(2,1)S(1)} collective-permute-done((bf16[208,1152]{1,0:T(8,128)(2,1)S(1)}, bf16[208,1152]{1,0:T(8,128)(2,1)S(1)}, u32[]{:S(2)}, u32[]{:S(2)}) %collective-permute-start.6) | collective-permute-done | bytes 479264 | tf_op jit(solution)/shard_map/ppermute | solution.py:665
  51.9 7.8 %collective-permute-done.8.refs_4_ = bf16[208,1152]{1,0:T(8,128)(2,1)} collective-permute-done((bf16[208,1152]{1,0:T(8,128)(2,1)}, bf16[208,1152]{1,0:T(8,128)(2,1)}, u32[]{:S(2)}, u32[]{:S(2)}) %collective-permute-start.8) | collective-permute-done | bytes 479264 | tf_op jit(solution)/shard_map/ppermute | solution.py:665
  63.4 11.4 %collective-permute-done.1 = bf16[256,1536]{1,0:T(8,128)(2,1)S(1)} collective-permute-done((bf16[256,1536]{1,0:T(8,128)(2,1)}, bf16[256,1536]{1,0:T(8,128)(2,1)S(1)}, u32[]{:S(2)}, u32[]{:S(2)}) %collective-permute-start.1) | collective-permute-done | bytes 786464 | tf_op jit(solution)/shard_map/ppermute | solution.py:798
  90.4 8.3 %project.2 = (bf16[1024,1152]{1,0:T(8,128)(2,1)S(1)}, f32[3,8,1024]{2,1,0:T(8,128)S(1)}) custom-call(s32[2]{0:T(128)S(1)} %pad_add_fusion.half, bf16[512,1536]{1,0:T(8,128)(2,1)S(1)} %fusion.4.refs_0_, bf16[512,1536]{1,0:T(8,128)(2,1)} %collective-permute-done.9.refs_1_.refs_2_.refs_5_, bf16[1536,1152]{1,0:T(8,128)(2,1)} %copy-done.22, ...), custom_call_target="tpu_custom_call" | custom-call | flops 5435817984 | bytes 9216096 | tf_op jit(solution)/shard_map/project/pallas_call | solution.py:355
  98.7 8.7 %project.3 = (bf16[1024,1152]{1,0:T(8,128)(2,1)S(1)}, f32[3,8,1024]{2,1,0:T(8,128)S(1)}) custom-call(s32[2]{0:T(128)S(1)} %pad_add_fusion.half, bf16[512,1536]{1,0:T(8,128)(2,1)} %constant_dynamic-update-slice_fusion.refs_0_.refs_4_.refs_10_, bf16[512,1536]{1,0:T(8,128)(2,1)} %collective-permute-done.10.refs_1_.refs_6_.refs_15_, ...), custom_call_target="tpu_custom_call" | custom-call | flops 5435817984 | bytes 9216096 | tf_op jit(solution)/shard_map/project/pallas_call | solution.py:355
  112.9 16.6 %attend.2 = (f32[1024,384]{1,0:T(8,128)S(1)}, f32[3,8,1024]{2,1,0:T(8,128)S(1)}) custom-call(s32[1]{0:T(128)} %get-tuple-element.318.start, s32[1]{0:T(128)} %get-tuple-element.313.size, bf16[1024,1152]{1,0:T(8,128)(2,1)S(1)} %get-tuple-element.150.q_ref.k_ref.v_ref, bf16[1024,1152]{1,0:T(8,128)(2,1)S(1)} %get-tuple-element.150.q_ref.k_ref.v_ref, ...), custom_call_target="tpu_custom_call" | custom-call | flops 10066329600 | bytes 3932160 | tf_op jit(solution)/shard_map/attend/pallas_call | solution.py:250
  133.6 17.2 %attend.3 = (f32[1024,384]{1,0:T(8,128)S(1)}, f32[3,8,1024]{2,1,0:T(8,128)S(1)}) custom-call(s32[1]{0:T(128)} %get-tuple-element.317.start, s32[1]{0:T(128)} %get-tuple-element.314.size, bf16[1024,1152]{1,0:T(8,128)(2,1)S(1)} %get-tuple-element.153.q_ref.k_ref.v_ref, bf16[1024,1152]{1,0:T(8,128)(2,1)S(1)} %get-tuple-element.153.q_ref.k_ref.v_ref, ...), custom_call_target="tpu_custom_call" | custom-call | flops 10066329600 | bytes 3932160 | tf_op jit(solution)/shard_map/attend/pallas_call | solution.py:250
  156.9 18.5 %collective-permute-done.17.refs_4_ = bf16[192,768]{1,0:T(8,128)(2,1)S(1)} collective-permute-done((bf16[192,768]{1,0:T(8,128)(2,1)S(1)}, bf16[192,768]{1,0:T(8,128)(2,1)S(1)}, u32[]{:S(2)}, u32[]{:S(2)}) %collective-permute-start.17) | collective-permute-done | bytes 294944 | tf_op jit(solution)/shard_map/ppermute | solution.py:665
  176.9 8.1 %close.2 = (f32[1024,384]{1,0:T(8,128)S(1)}, bf16[1024,384]{1,0:T(8,128)(2,1)S(1)}, bf16[512,1536]{1,0:T(8,128)(2,1)}, bf16[512,1536]{1,0:T(8,128)(2,1)}) custom-call(s32[2]{0:T(128)S(1)} %pad_add_fusion.half, bf16[512,1536]{1,0:T(8,128)(2,1)} %constant_dynamic-update-slice_fusion.refs_0_.refs_4_.refs_10_, ...), custom_call_target="tpu_custom_call" | custom-call | flops 3623878656 | bytes 12582912 | tf_op jit(solution)/shard_map/close/pallas_call | solution.py:355
  194.4 8.1 %close.3 = (f32[1024,384]{1,0:T(8,128)S(1)}, bf16[1024,384]{1,0:T(8,128)(2,1)S(1)}, bf16[512,1536]{1,0:T(8,128)(2,1)}, bf16[512,1536]{1,0:T(8,128)(2,1)}) custom-call(s32[2]{0:T(128)S(1)} %pad_add_fusion.half, bf16[512,1536]{1,0:T(8,128)(2,1)} %copy-done, bf16[512,1536]{1,0:T(8,128)(2,1)} %collective-permute-done.9.refs_1_.refs_2_.refs_5_, ...), custom_call_target="tpu_custom_call" | custom-call | flops 3623878656 | bytes 12582912 | tf_op jit(solution)/shard_map/close/pallas_call | solution.py:355
  202.4 26.9 %collective-permute-done.19 = bf16[512,1536]{1,0:T(8,128)(2,1)S(1)} collective-permute-done((bf16[512,1536]{1,0:T(8,128)(2,1)S(1)}, bf16[512,1536]{1,0:T(8,128)(2,1)S(1)}, u32[]{:S(2)}, u32[]{:S(2)}) %collective-permute-start.19) | collective-permute-done | bytes 1572896 | tf_op jit(solution)/shard_map/ppermute | solution.py:798
  244.6 25.0 %feed.2 = (bf16[1024,1024]{1,0:T(8,128)(2,1)}, bf16[1024,2048]{1,0:T(8,128)(2,1)}, bf16[512,1536]{1,0:T(8,128)(2,1)S(1)}, bf16[512,1536]{1,0:T(8,128)(2,1)S(1)}) custom-call(s32[2]{0:T(128)S(1)} %pad_add_fusion.half, bf16[512,1536]{1,0:T(8,128)(2,1)} %multiply_convert_fusion.refs_0_, bf16[512,1536]{1,0:T(8,128)(2,1)} %collective-permute-done.24.refs_1_.refs_2_, ...), custom_call_target="tpu_custom_call" | custom-call | flops 24159191040 | bytes 25165824 | tf_op jit(solution)/shard_map/feed/pallas_call | solution.py:355
  269.7 8.3 %collective-permute-done.23.refs_0_.refs_4_ = bf16[512,1536]{1,0:T(8,128)(2,1)} collective-permute-done((bf16[512,1536]{1,0:T(8,128)(2,1)}, bf16[512,1536]{1,0:T(8,128)(2,1)}, u32[]{:S(2)}, u32[]{:S(2)}) %collective-permute-start.23) | collective-permute-done | bytes 1572896 | tf_op jit(solution)/shard_map/ppermute | solution.py:798
  282.8 25.2 %feed.3 = (bf16[1024,1024]{1,0:T(8,128)(2,1)}, bf16[1024,2048]{1,0:T(8,128)(2,1)}, bf16[512,1536]{1,0:T(8,128)(2,1)S(1)}, bf16[512,1536]{1,0:T(8,128)(2,1)S(1)}) custom-call(s32[2]{0:T(128)S(1)} %pad_add_fusion.half, bf16[512,1536]{1,0:T(8,128)(2,1)} %collective-permute-done.23.refs_0_.refs_4_, bf16[512,1536]{1,0:T(8,128)(2,1)} %copy-done.108, ...), custom_call_target="tpu_custom_call" | custom-call | flops 24159191040 | bytes 25165824 | tf_op jit(solution)/shard_map/feed/pallas_call | solution.py:355
  314.4 28.1 %grad_feed.1 = bf16[1536,3072]{1,0:T(8,128)(2,1)} custom-call(s32[2]{0:T(128)S(1)} %pad_add_fusion.half, bf16[512,1536]{1,0:T(8,128)(2,1)} %multiply_convert_fusion.refs_0_, bf16[1024,2048]{1,0:T(8,128)(2,1)} %get-tuple-element.183.refs_1_.refs_3_, bf16[512,1536]{1,0:T(8,128)(2,1)} %collective-permute-done.24.refs_1_.refs_2_, ...), custom_call_target="tpu_custom_call" | custom-call | flops 28991029248 | bytes 28311552 | tf_op jit(solution)/shard_map/grad_feed/pallas_call | solution.py:536
  375.9 32.6 %attend_back.2 = (bf16[1024,384]{1,0:T(8,128)(2,1)S(1)}, bf16[1024,384]{1,0:T(8,128)(2,1)S(1)}, bf16[1024,384]{1,0:T(8,128)(2,1)S(1)}, f32[3,8,1024]{2,1,0:T(8,128)S(1)}) custom-call(s32[1]{0:T(128)} %get-tuple-element.317.start, s32[1]{0:T(128)} %get-tuple-element.314.size, bf16[1024,1152]{1,0:T(8,128)(2,1)S(1)} %copy-done.37, ...), custom_call_target="tpu_custom_call" | custom-call | flops 16357785600 | bytes 7864320 | tf_op jit(solution)/shard_map/attend_back/pallas_call | solution.py:274
  414.8 7.7 %feed_out.3 = (bf16[512,1536]{1,0:T(8,128)(2,1)S(1)}, bf16[512,1536]{1,0:T(8,128)(2,1)}) custom-call(s32[2]{0:T(128)S(1)} %pad_add_fusion.half, bf16[1024,1024]{1,0:T(8,128)(2,1)S(1)} %copy-done.28, bf16[1536,3072]{1,0:T(8,128)(2,1)} %all-gather.2.cloned.1.call-done.refs_4_.w_ref), custom_call_target="tpu_custom_call" | custom-call | flops 4831838208 | bytes 14680064 | tf_op jit(solution)/shard_map/feed_out/pallas_call | solution.py:355
  432.1 11.2 %grad_gate_out.1 = bf16[1536,768]{1,0:T(8,128)(2,1)} custom-call(s32[2]{0:T(128)S(1)} %pad_add_fusion.half, bf16[512,1536]{1,0:T(8,128)(2,1)} %copy-done, bf16[1024,384]{1,0:T(8,128)(2,1)S(1)} %get-tuple-element.206.refs_1_.refs_3_, bf16[512,1536]{1,0:T(8,128)(2,1)} %collective-permute-done.9.refs_1_.refs_2_.refs_5_, ...), custom_call_target="tpu_custom_call" | custom-call | flops 7247757312 | bytes 7077888 | tf_op jit(solution)/shard_map/grad_gate_out/pallas_call | solution.py:536
  443.4 29.2 %attend_back.3 = (bf16[1024,384]{1,0:T(8,128)(2,1)S(1)}, bf16[1024,384]{1,0:T(8,128)(2,1)S(1)}, bf16[1024,384]{1,0:T(8,128)(2,1)S(1)}, f32[3,8,1024]{2,1,0:T(8,128)S(1)}) custom-call(s32[1]{0:T(128)} %get-tuple-element.318.start, s32[1]{0:T(128)} %get-tuple-element.313.size, bf16[1024,1152]{1,0:T(8,128)(2,1)S(1)} %copy-done.35, ...), custom_call_target="tpu_custom_call" | custom-call | flops 16357785600 | bytes 7864320 | tf_op jit(solution)/shard_map/attend_back/pallas_call | solution.py:274
  472.6 12.1 %project_back.2 = (bf16[512,1536]{1,0:T(8,128)(2,1)S(1)}, bf16[512,1536]{1,0:T(8,128)(2,1)}) custom-call(s32[2]{0:T(128)S(1)} %pad_add_fusion.half, bf16[1024,384]{1,0:T(8,128)(2,1)S(1)} %get-tuple-element.213.refs_0_.refs_11_.refs_16_, bf16[1024,384]{1,0:T(8,128)(2,1)S(1)} %get-tuple-element.214.refs_1_.refs_12_.refs_17_, ...), custom_call_target="tpu_custom_call" | custom-call | flops 7247757312 | bytes 11182080 | tf_op jit(solution)/shard_map/project_back/pallas_call | solution.py:355
  491.3 12.4 %collective-permute-done.47 = bf16[192,768]{1,0:T(8,128)(2,1)S(1)} collective-permute-done((bf16[192,768]{1,0:T(8,128)(2,1)S(1)}, bf16[192,768]{1,0:T(8,128)(2,1)S(1)}, u32[]{:S(2)}, u32[]{:S(2)}) %collective-permute-start.47) | collective-permute-done | bytes 294944 | tf_op jit(solution)/shard_map/ppermute | solution.py:665
  503.7 8.8 %collective-permute-done.48 = bf16[192,768]{1,0:T(8,128)(2,1)S(1)} collective-permute-done((bf16[192,768]{1,0:T(8,128)(2,1)S(1)}, bf16[192,768]{1,0:T(8,128)(2,1)S(1)}, u32[]{:S(2)}, u32[]{:S(2)}) %collective-permute-start.48) | collective-permute-done | bytes 294944 | tf_op jit(solution)/shard_map/ppermute | solution.py:665
  521.7 11.2 %project_back.3 = (bf16[512,1536]{1,0:T(8,128)(2,1)S(1)}, bf16[512,1536]{1,0:T(8,128)(2,1)}) custom-call(s32[2]{0:T(128)S(1)} %pad_add_fusion.half, bf16[1024,384]{1,0:T(8,128)(2,1)S(1)} %copy-done.39, bf16[1024,384]{1,0:T(8,128)(2,1)S(1)} %copy-done.41, bf16[1024,384]{1,0:T(8,128)(2,1)S(1)} %copy-done.43, ...), custom_call_target="tpu_custom_call" | custom-call | flops 7247757312 | bytes 11182080 | tf_op jit(solution)/shard_map/project_back/pallas_call | solution.py:355
  537.8 15.0 %project_grads.1 = bf16[8,208,1152]{2,1,0:T(8,128)(2,1)} custom-call(s32[2]{0:T(128)S(1)} %pad_add_fusion.half, bf16[512,1536]{1,0:T(8,128)(2,1)} %copy-done, bf16[1024,384]{1,0:T(8,128)(2,1)S(1)} %copy-done.39, bf16[1024,384]{1,0:T(8,128)(2,1)S(1)} %copy-done.41, bf16[1024,384]{1,0:T(8,128)(2,1)S(1)} %copy-done.43, ...), custom_call_target="tpu_custom_call" | custom-call | flops 10871635968 | bytes 10616832 | tf_op jit(solution)/shard_map/project_grads/pallas_call | solution.py:596
  (427 shorter events, 289.1 us)
Async XLA Ops:
  7.2 235.3 %all-gather.2.cloned.1.call-start = ((), (), s32[]{:S(2)}) async-start(), calls=%async_computation.1 | async-start | bytes 10616832 | tf_op jit(solution)/shard_map/all_gather | solution.py:882
  59.6 562.6 %reduce-scatter.2.cloned.1.call-start = ((), (), s32[]{:S(2)}) async-start(), calls=%async_computation.2 | async-start | bytes 10616832 | tf_op jit(solution)/shard_map/reduce_scatter | solution.py:944
  61.3 29.0 %collective-permute-start.9 = (bf16[512,1536]{1,0:T(8,128)(2,1)S(1)}, bf16[512,1536]{1,0:T(8,128)(2,1)}, u32[]{:S(2)}, u32[]{:S(2)}) collective-permute-start(bf16[512,1536]{1,0:T(8,128)(2,1)S(1)} %fusion.4.refs_0_), channel_id=1, source_target_pairs={{0,1},{1,0},{2,3},{3,2},{4,5},{5,4},{6,7},{7,6},{8,9},{9,8},{10,11... | collective-permute-start | bytes 4718600 | tf_op jit(solution)/shard_map/ppermute | solution.py:798
  75.8 22.8 %collective-permute-start.10 = (bf16[512,1536]{1,0:T(8,128)(2,1)}, bf16[512,1536]{1,0:T(8,128)(2,1)}, u32[]{:S(2)}, u32[]{:S(2)}) collective-permute-start(bf16[512,1536]{1,0:T(8,128)(2,1)} %constant_dynamic-update-slice_fusion.refs_0_.refs_4_.refs_10_), channel_id=1, source_target_pairs={{0,1},{1,0},{2,3},{3,2},{4,5},{5,4},{6,7},{7,6},{8,9},{9,8},{10,11... | collective-permute-start | bytes 4718600 | tf_op jit(solution)/shard_map/ppermute | solution.py:798
  88.2 22.4 %collective-permute-start.11 = (bf16[192,768]{1,0:T(8,128)(2,1)S(1)}, bf16[192,768]{1,0:T(8,128)(2,1)S(1)}, u32[]{:S(2)}, u32[]{:S(2)}) collective-permute-start(bf16[192,768]{1,0:T(8,128)(2,1)S(1)} %pad_maximum_fusion.1.refs_0_), channel_id=1, source_target_pairs={{0,4},{8,0},{16,8},{24,16},{28,24},{20,28},{12,20},{4,12},{1,5},{9... | collective-permute-start | bytes 884744 | tf_op jit(solution)/shard_map/ppermute | solution.py:665
  89.7 20.9 %collective-permute-start.12 = (bf16[192,768]{1,0:T(8,128)(2,1)S(1)}, bf16[192,768]{1,0:T(8,128)(2,1)S(1)}, u32[]{:S(2)}, u32[]{:S(2)}) collective-permute-start(bf16[192,768]{1,0:T(8,128)(2,1)S(1)} %pad_maximum_fusion.1.refs_0_), channel_id=1, source_target_pairs={{0,8},{8,16},{16,24},{24,28},{28,20},{20,12},{12,4},{4,0},{1,9},{9... | collective-permute-start | bytes 884744 | tf_op jit(solution)/shard_map/ppermute | solution.py:665
  110.6 20.1 %collective-permute-start.13 = (bf16[192,768]{1,0:T(8,128)(2,1)S(1)}, bf16[192,768]{1,0:T(8,128)(2,1)S(1)}, u32[]{:S(2)}, u32[]{:S(2)}) collective-permute-start(bf16[192,768]{1,0:T(8,128)(2,1)S(1)} %collective-permute-done.11.refs_1_), channel_id=1, source_target_pairs={{0,4},{8,0},{16,8},{24,16},{28,24},{20,28},{12,20},{4,12},{1,5},{9... | collective-permute-start | bytes 884744 | tf_op jit(solution)/shard_map/ppermute | solution.py:665
  130.7 22.1 %collective-permute-start.15 = (bf16[192,768]{1,0:T(8,128)(2,1)S(1)}, bf16[192,768]{1,0:T(8,128)(2,1)S(1)}, u32[]{:S(2)}, u32[]{:S(2)}) collective-permute-start(bf16[192,768]{1,0:T(8,128)(2,1)S(1)} %collective-permute-done.13.refs_2_), channel_id=1, source_target_pairs={{0,4},{8,0},{16,8},{24,16},{28,24},{20,28},{12,20},{4,12},{1,5},{9... | collective-permute-start | bytes 884744 | tf_op jit(solution)/shard_map/ppermute | solution.py:665
  133.3 19.5 %collective-permute-start.16 = (bf16[192,768]{1,0:T(8,128)(2,1)S(1)}, bf16[192,768]{1,0:T(8,128)(2,1)S(1)}, u32[]{:S(2)}, u32[]{:S(2)}) collective-permute-start(bf16[192,768]{1,0:T(8,128)(2,1)S(1)} %collective-permute-done.14.refs_6_), channel_id=1, source_target_pairs={{0,8},{8,16},{16,24},{24,28},{28,20},{20,12},{12,4},{4,0},{1,9},{9... | collective-permute-start | bytes 884744 | tf_op jit(solution)/shard_map/ppermute | solution.py:665
  152.8 22.6 %collective-permute-start.17 = (bf16[192,768]{1,0:T(8,128)(2,1)S(1)}, bf16[192,768]{1,0:T(8,128)(2,1)S(1)}, u32[]{:S(2)}, u32[]{:S(2)}) collective-permute-start(bf16[192,768]{1,0:T(8,128)(2,1)S(1)} %collective-permute-done.15.refs_3_), channel_id=1, source_target_pairs={{0,4},{8,0},{16,8},{24,16},{28,24},{20,28},{12,20},{4,12},{1,5},{9... | collective-permute-start | bytes 884744 | tf_op jit(solution)/shard_map/ppermute | solution.py:665
  155.8 34.8 %collective-permute-start.20 = (bf16[512,1536]{1,0:T(8,128)(2,1)}, bf16[512,1536]{1,0:T(8,128)(2,1)S(1)}, u32[]{:S(2)}, u32[]{:S(2)}) collective-permute-start(bf16[512,1536]{1,0:T(8,128)(2,1)} %refs_8_), channel_id=1, source_target_pairs={{0,2},{1,3},{2,0},{3,1},{4,6},{5,7},{6,4},{7,5},{8,10},{9,11},{10,... | collective-permute-start | bytes 4718600 | tf_op jit(solution)/shard_map/ppermute | solution.py:798
  193.0 36.3 %collective-permute-start.19 = (bf16[512,1536]{1,0:T(8,128)(2,1)S(1)}, bf16[512,1536]{1,0:T(8,128)(2,1)S(1)}, u32[]{:S(2)}, u32[]{:S(2)}) collective-permute-start(bf16[512,1536]{1,0:T(8,128)(2,1)S(1)} %add_convert_fusion.3), channel_id=1, source_target_pairs={{0,2},{1,3},{2,0},{3,1},{4,6},{5,7},{6,4},{7,5},{8,10},{9,11},{10,... | collective-permute-start | bytes 4718600 | tf_op jit(solution)/shard_map/ppermute | solution.py:798
  241.0 37.0 %collective-permute-start.23 = (bf16[512,1536]{1,0:T(8,128)(2,1)}, bf16[512,1536]{1,0:T(8,128)(2,1)}, u32[]{:S(2)}, u32[]{:S(2)}) collective-permute-start(bf16[512,1536]{1,0:T(8,128)(2,1)} %multiply_convert_fusion.refs_0_), channel_id=1, source_target_pairs={{0,2},{1,3},{2,0},{3,1},{4,6},{5,7},{6,4},{7,5},{8,10},{9,11},{10,... | collective-permute-start | bytes 4718600 | tf_op jit(solution)/shard_map/ppermute | solution.py:798
  312.9 36.8 %collective-permute-start.29 = (bf16[512,1536]{1,0:T(8,128)(2,1)}, bf16[512,1536]{1,0:T(8,128)(2,1)}, u32[]{:S(2)}, u32[]{:S(2)}) collective-permute-start(bf16[512,1536]{1,0:T(8,128)(2,1)} %add_convert_fusion.2), channel_id=1, source_target_pairs={{0,2},{1,3},{2,0},{3,1},{4,6},{5,7},{6,4},{7,5},{8,10},{9,11},{10,... | collective-permute-start | bytes 4718600 | tf_op jit(solution)/shard_map/ppermute | solution.py:798
  359.8 51.4 %collective-permute-start.30 = (bf16[512,1536]{1,0:T(8,128)(2,1)}, bf16[512,1536]{1,0:T(8,128)(2,1)S(1)}, u32[]{:S(2)}, u32[]{:S(2)}) collective-permute-start(bf16[512,1536]{1,0:T(8,128)(2,1)} %get-tuple-element.190.refs_0_.refs_8_), channel_id=1, source_target_pairs={{0,2},{1,3},{2,0},{3,1},{4,6},{5,7},{6,4},{7,5},{8,10},{9,11},{10,... | collective-permute-start | bytes 4718600 | tf_op jit(solution)/shard_map/ppermute | solution.py:798
  430.9 41.6 %collective-permute-start.34 = (bf16[512,1536]{1,0:T(8,128)(2,1)}, bf16[512,1536]{1,0:T(8,128)(2,1)}, u32[]{:S(2)}, u32[]{:S(2)}) collective-permute-start(bf16[512,1536]{1,0:T(8,128)(2,1)} %add_convert_fusion.1), channel_id=1, source_target_pairs={{0,2},{1,3},{2,0},{3,1},{4,6},{5,7},{6,4},{7,5},{8,10},{9,11},{10,... | collective-permute-start | bytes 4718600 | tf_op jit(solution)/shard_map/ppermute | solution.py:798
  484.7 27.8 %collective-permute-start.36 = (bf16[512,1536]{1,0:T(8,128)(2,1)}, bf16[512,1536]{1,0:T(8,128)(2,1)S(1)}, u32[]{:S(2)}, u32[]{:S(2)}) collective-permute-start(bf16[512,1536]{1,0:T(8,128)(2,1)} %get-tuple-element.218), channel_id=1, source_target_pairs={{0,1},{1,0},{2,3},{3,2},{4,5},{5,4},{6,7},{7,6},{8,9},{9,8},{10,11... | collective-permute-start | bytes 4718600 | tf_op jit(solution)/shard_map/ppermute | solution.py:798
  490.1 22.4 %collective-permute-start.48 = (bf16[192,768]{1,0:T(8,128)(2,1)S(1)}, bf16[192,768]{1,0:T(8,128)(2,1)S(1)}, u32[]{:S(2)}, u32[]{:S(2)}) collective-permute-start(bf16[192,768]{1,0:T(8,128)(2,1)S(1)} %get-tuple-element.289), channel_id=1, source_target_pairs={{0,4},{8,0},{16,8},{24,16},{28,24},{20,28},{12,20},{4,12},{1,5},{9... | collective-permute-start | bytes 884744 | tf_op jit(solution)/shard_map/ppermute | solution.py:665
  513.9 22.1 %collective-permute-start.37 = (bf16[256,1536]{1,0:T(8,128)(2,1)S(1)}, bf16[256,1536]{1,0:T(8,128)(2,1)S(1)}, u32[]{:S(2)}, u32[]{:S(2)}) collective-permute-start(bf16[256,1536]{1,0:T(8,128)(2,1)S(1)} %get-tuple-element.293), channel_id=1, source_target_pairs={{0,2},{1,3},{2,0},{3,1},{4,6},{5,7},{6,4},{7,5},{8,10},{9,11},{10,... | collective-permute-start | bytes 2359304 | tf_op jit(solution)/shard_map/ppermute | solution.py:798
  519.6 40.4 %collective-permute-start.49 = (bf16[192,768]{1,0:T(8,128)(2,1)S(1)}, bf16[192,768]{1,0:T(8,128)(2,1)S(1)}, u32[]{:S(2)}, u32[]{:S(2)}) collective-permute-start(bf16[192,768]{1,0:T(8,128)(2,1)S(1)} %get-tuple-element.288), channel_id=1, source_target_pairs={{0,8},{8,16},{16,24},{24,28},{28,20},{20,12},{12,4},{4,0},{1,9},{9... | collective-permute-start | bytes 884744 | tf_op jit(solution)/shard_map/ppermute | solution.py:665
  519.7 40.3 %collective-permute-start.50 = (bf16[192,768]{1,0:T(8,128)(2,1)S(1)}, bf16[192,768]{1,0:T(8,128)(2,1)}, u32[]{:S(2)}, u32[]{:S(2)}) collective-permute-start(bf16[192,768]{1,0:T(8,128)(2,1)S(1)} %get-tuple-element.287), channel_id=1, source_target_pairs={{0,4},{8,0},{16,8},{24,16},{28,24},{20,28},{12,20},{4,12},{1,5},{9... | collective-permute-start | bytes 884744 | tf_op jit(solution)/shard_map/ppermute | solution.py:665
  536.0 19.3 %collective-permute-start.38 = (bf16[256,1536]{1,0:T(8,128)(2,1)}, bf16[256,1536]{1,0:T(8,128)(2,1)S(1)}, u32[]{:S(2)}, u32[]{:S(2)}) collective-permute-start(bf16[256,1536]{1,0:T(8,128)(2,1)} %get-tuple-element.219), channel_id=1, source_target_pairs={{0,2},{1,3},{2,0},{3,1},{4,6},{5,7},{6,4},{7,5},{8,10},{9,11},{10,... | collective-permute-start | bytes 2359304 | tf_op jit(solution)/shard_map/ppermute | solution.py:798
  559.9 76.4 %collective-permute-start.35 = (bf16[512,1536]{1,0:T(8,128)(2,1)}, bf16[512,1536]{1,0:T(8,128)(2,1)}, u32[]{:S(2)}, u32[]{:S(2)}) collective-permute-start(bf16[512,1536]{1,0:T(8,128)(2,1)} %get-tuple-element.200), channel_id=1, source_target_pairs={{0,1},{1,0},{2,3},{3,2},{4,5},{5,4},{6,7},{7,6},{8,9},{9,8},{10,11... | collective-permute-start | bytes 4718600 | tf_op jit(solution)/shard_map/ppermute | solution.py:798
  577.8 27.0 %collective-permute-start.39 = (bf16[512,1536]{1,0:T(8,128)(2,1)}, bf16[512,1536]{1,0:T(8,128)(2,1)S(1)}, u32[]{:S(2)}, u32[]{:S(2)}) collective-permute-start(bf16[512,1536]{1,0:T(8,128)(2,1)} %get-tuple-element.226), channel_id=1, source_target_pairs={{0,1},{1,0},{2,3},{3,2},{4,5},{5,4},{6,7},{7,6},{8,9},{9,8},{10,11... | collective-permute-start | bytes 4718600 | tf_op jit(solution)/shard_map/ppermute | solution.py:798
  (146 other events, 1435.3 us)
Sparse Core Ops, SparseCore 0:
  59.8 153.7 all-gather.1
  359.9 169.9 reduce-scatter.1

commit v3 on v2

--- a/solution.py
+++ b/solution.py
@@ -368,17 +368,18 @@
     return pl.BlockSpec((rows, n), lambda *_: (0, at), pipeline_mode=pl.Buffered(1))
 
 
-def project(pc, xs, w, wf, bias):
-    dims, width = w.shape[0], w.shape[1] // 3
+def project(pc, xs, w, wf, bias, width):
+    dims = w.shape[0]
     pairs = wf.shape[0] // 8
 
     def kernel(half, *refs):
         i = pl.program_id(0)
-        w_ref, wf_ref, bias_ref, qkv_ref, zf_ref = refs[pc.count:]
+        w_ref, wf_ref, bias_ref, qkv_ref, sig_ref, zf_ref = refs[pc.count:]
         x = pc.pick(refs[:pc.count], i)
         q = mm(x, w_ref[:, :width]) * (HEAD_DIM**-0.5 * LOG2E)
         qkv_ref[:, :width] = q.astype(LOW)
-        qkv_ref[:, width:] = mm(x, w_ref[:, width:]).astype(LOW)
+        qkv_ref[:, width:] = mm(x, w_ref[:, width:3 * width]).astype(LOW)
+        sig_ref[...] = jax.nn.sigmoid(mm(x, w_ref[:, 3 * width:]))
         z = mm(wf_ref[...], x, NT) + bias_ref[...]
         for p in range(pairs):
             zf_ref[p] = z[8 * p:8 * p + 8, :]
@@ -387,35 +388,35 @@
     return pc.call(
         kernel, "project",
         list(xs) + [w, wf, bias],
-        pc.own_specs(dims) + [whole(dims, 3 * width), whole(8 * pairs, dims), whole(8 * pairs, 1)],
-        [jax.ShapeDtypeStruct((rows, 3 * width), LOW), jax.ShapeDtypeStruct((pairs, 8, rows), F32)],
-        [pc.true_spec(3 * width), pc.lane_spec((pairs, 8))],
-        6 * rows * dims * width,
+        pc.own_specs(dims) + [whole(dims, 4 * width), whole(8 * pairs, dims), whole(8 * pairs, 1)],
+        [
+            jax.ShapeDtypeStruct((rows, 3 * width), LOW),
+            jax.ShapeDtypeStruct((rows, width), F32),
+            jax.ShapeDtypeStruct((pairs, 8, rows), F32),
+        ],
+        [pc.true_spec(3 * width), pc.true_spec(width), pc.lane_spec((pairs, 8))],
+        8 * rows * dims * width,
     )
 
 
-def close(pc, xs, core, w_gate, w_out):
+def close(pc, core, sig, w_out):
     dims, width = w_out.shape
 
-    def kernel(half, *refs):
-        i = pl.program_id(0)
-        core_ref, wg_ref, w_ref, sig_ref, gated_ref = refs[pc.count:pc.count + 5]
-        sig = jax.nn.sigmoid(mm(pc.pick(refs[:pc.count], i), wg_ref[...]))
-        sig_ref[...] = sig
-        g = (core_ref[...] * sig).astype(LOW)
+    def kernel(half, core_ref, sig_ref, w_ref, gated_ref, *parts):
+        g = (core_ref[...] * sig_ref[...]).astype(LOW)
         gated_ref[...] = g
-        pc.put(refs[pc.count + 5:], i, mm(g, w_ref[...], NT).astype(LOW))
+        pc.put(parts, pl.program_id(0), mm(g, w_ref[...], NT).astype(LOW))
 
     rows = pc.all_rows()
     out = pc.call(
         kernel, "close",
-        list(xs) + [core, w_gate, w_out],
-        pc.own_specs(dims) + [pc.true_spec(width), whole(dims, width), whole(dims, width)],
-        [jax.ShapeDtypeStruct((rows, width), F32), jax.ShapeDtypeStruct((rows, width), LOW)] + pc.shapes(dims),
-        [pc.true_spec(width), pc.flat_spec(width)] + pc.own_specs(dims),
-        4 * rows * dims * width,
+        [core, sig, w_out],
+        [pc.true_spec(width), pc.true_spec(width), whole(dims, width)],
+        [jax.ShapeDtypeStruct((rows, width), LOW)] + pc.shapes(dims),
+        [pc.flat_spec(width)] + pc.own_specs(dims),
+        2 * rows * dims * width,
     )
-    return out[0], out[1], out[2:]
+    return out[0], out[1:]
 
 
 def feed(pc, xs, ys, w):
@@ -481,25 +482,24 @@
     )
 
 
-def project_back(pc, grads, dz, w_qkv, w_gate, wf):
-    dims = w_qkv.shape[0]
+def project_back(pc, grads, dz, w, wf, width):
+    dims = w.shape[0]
     pairs = dz.shape[0]
     n = len(grads)
-    width = w_gate.shape[1]
 
     def kernel(half, *refs):
-        dz_ref, w_ref, wg_ref, wf_ref = refs[n:n + 4]
-        g = jnp.concatenate([r[...] for r in refs[:n - 1]], axis=1)
-        total = mm(g, w_ref[...], NT) + mm(refs[n - 1][...], wg_ref[...], NT)
+        dz_ref, w_ref, wf_ref = refs[n:n + 3]
+        g = jnp.concatenate([r[...] for r in refs[:n]], axis=1)
+        total = mm(g, w_ref[...], NT)
         z = jnp.concatenate([dz_ref[p] for p in range(pairs)], axis=0).astype(LOW)
         total = total + mm(z, wf_ref[...], TN)
-        pc.put(refs[n + 4:], pl.program_id(0), total.astype(LOW))
+        pc.put(refs[n + 3:], pl.program_id(0), total.astype(LOW))
 
     return pc.call(
         kernel, "project_back",
-        list(grads) + [dz, w_qkv, w_gate, wf],
+        list(grads) + [dz, w, wf],
         [pc.true_spec(g.shape[1]) for g in grads]
-        + [pc.lane_spec((pairs, 8)), whole(dims, 3 * width), whole(dims, width), whole(8 * pairs, dims)],
+        + [pc.lane_spec((pairs, 8)), whole(dims, 4 * width), whole(8 * pairs, dims)],
         pc.shapes(dims), pc.own_specs(dims), 8 * pc.all_rows() * dims * width,
     )
 
@@ -546,53 +546,57 @@
     )(pc.half, *ins)
 
 
-def project_grads(pc, chunks, size, tail, n):
+def project_grads(pc, chunks, size, tail, heads_each):
     dims = chunks[0][0][0].shape[1]
     step = 384
     per = step // size
+    n = sum(g.shape[1] for g in chunks[0][1][0])
     cols = len(chunks[0][1])
-    pairs = chunks[0][2].shape[0] if tail else 0
+    pairs = chunks[0][2].shape[0]
     ins, specs, plan = [], [], []
     for lefts, grads, dz in chunks:
         for p, left in enumerate(lefts):
-            plan.append(len(ins))
-            ins += [left] + [g for g, _ in grads]
+            at, groups = len(ins), []
+            ins.append(left)
             specs.append(pl.BlockSpec((pc.rows, step), lambda i, *_: (0, i)))
-            for _, c in grads:
-                specs.append(
-                    pl.BlockSpec((pc.rows, n), lambda i, half, p=p, c=c: (half[p], c), pipeline_mode=pl.Buffered(1))
-                )
-            if tail:
-                ins.append(dz)
-                specs.append(pl.BlockSpec((pairs, 8, pc.rows), lambda i, half, p=p: (0, 0, half[p])))
+            for group in grads:
+                groups.append(range(len(ins), len(ins) + len(group)))
+                for g in group:
+                    ins.append(g)
+                    specs.append(
+                        pl.BlockSpec(
+                            (pc.rows, g.shape[1]), lambda i, half, p=p: (half[p], 0), pipeline_mode=pl.Buffered(1)
+                        )
+                    )
+            plan.append((at, groups, len(ins)))
+            ins.append(dz)
+            specs.append(pl.BlockSpec((pairs, 8, pc.rows), lambda i, half, p=p: (0, 0, half[p])))
 
     def kernel(half, *refs):
         out = refs[-1]
         for c in range(cols):
             total = None
-            for at in plan:
-                t = mm(refs[at][...], refs[at + 1 + c][...], TN)
+            for at, groups, _ in plan:
+                right = [refs[j][...] for j in groups[c]]
+                right = jnp.concatenate(right, axis=1) if len(right) > 1 else right[0]
+                t = mm(refs[at][...], right, TN)
                 total = t if total is None else total + t
             total = total.astype(LOW)
             for b in range(per):
                 out[b, :size, c * n:(c + 1) * n] = total[b * size:(b + 1) * size]
-        if not tail:
-            return
         total = None
-        for at in plan:
-            z = jnp.concatenate([refs[at + 1 + cols][p] for p in range(pairs)], axis=0).astype(LOW)
+        for at, _, z_at in plan:
+            z = jnp.concatenate([refs[z_at][p] for p in range(pairs)], axis=0).astype(LOW)
             t = mm(z, refs[at][...])
             total = t if total is None else total + t
-        hb = tail_heads
-        heads = [total[8 * p:8 * p + hb] for p in range(pairs)]
-        heads.append(jnp.zeros((tail - hb * pairs, step), F32))
+        heads = [total[8 * p:8 * p + heads_each] for p in range(pairs)]
+        heads.append(jnp.zeros((tail - heads_each * pairs, step), F32))
         total = jnp.concatenate(heads, axis=0)
         for b in range(per):
             row = total[:, b * size:(b + 1) * size]
             row = jnp.concatenate([row, jnp.zeros((tail, cols * n - size), F32)], axis=1)
             out[b, size:, :] = row.astype(LOW)
 
-    tail_heads = head_shapes(n)[0]
     return pl.pallas_call(
         kernel,
         grid_spec=pltpu.PrefetchScalarGridSpec(
@@ -853,13 +857,13 @@
         inputs_f = inputs.astype(F32)
         tail = 16
         forget_row = forget_weight.T.astype(LOW)
-        forget_row = jnp.pad(forget_row, ((0, tail - heads), (0, 3 * width - rows_each)))
-        pack = jnp.concatenate([flat(qkvg_weight[:3]), forget_row])
+        forget_row = jnp.pad(forget_row, ((0, tail - heads), (0, 5 * width - rows_each)))
+        pack = jnp.concatenate([flat(qkvg_weight), out_weight.T.astype(LOW)], axis=1)
+        pack = jnp.concatenate([pack, forget_row])
         ring_one = data.gather(pack, 1)
         ring_one.step()
         scale_one = rms_scale(inputs_f)
         normed_one = after((inputs_f * scale_one * attn_gain).astype(LOW), pack)
-        low_go = jnp.concatenate([after(qkvg_weight[3], normed_one), out_weight.T], axis=1).astype(LOW)
         low_feed = jnp.concatenate([flat(after(gate_up, normed_one)), down_weight.T.astype(LOW)], axis=1)
         if paired:
             near, came = [normed_one, swap(normed_one, 1)], []
@@ -873,16 +877,18 @@
             move_one = (near, jnp.concatenate(came))
         else:
             move_one = rows_start(normed_one)
+        while ring_one.k < dp // 2 - 1:
+            ring_one.step()
+        early = tuple(ring_one.ends)
         blocks = ring_one.all()
-        w_qkv, w_tail = place([after(blocks[0], low_feed)] + blocks[1:], data.ahead, rows_each + tail, tail)
+        w_one, w_tail = place([after(blocks[0], low_feed)] + blocks[1:], data.ahead, rows_each + tail, tail)
+        w_out = w_one[:, 4 * width:]
         w_forget = w_tail.reshape(dp, tail, -1)[:, :heads, :rows_each].transpose(1, 0, 2)
         w_forget = jnp.pad(w_forget.reshape(pairs, hb, dims), ((0, 0), (0, 8 - hb), (0, 0))).reshape(-1, dims)
         bias_local = index(forget_bias.reshape(tn, heads), rank, 0)
         bias_local = jnp.pad(bias_local.reshape(pairs, hb), ((0, 0), (0, 8 - hb))).reshape(-1, 1)
-        w_feed = lax.all_gather(after(low_feed, blocks[-1], blocks[dp // 2]), "dp", axis=0, tiled=True)
-        done(w_qkv)
-        ring_go = data.gather(at(low_go), -1)
-        ring_go.step()
+        w_feed = lax.all_gather(after(low_feed, *early), "dp", axis=0, tiled=True)
+        done(w_one)
         rows_one = [move_one[0]]
         if paired:
             rows_one.append(far(move_one))
@@ -891,26 +897,18 @@
         qkv, zf, attended, gate_sig, gated = ([None] * chunks for _ in range(5))
         for i in range(chunks):
             first = at(rows_one[i][0])
-            qkv[i], zf[i] = project(pc, [first] + rows_one[i][1:], w_qkv, w_forget, bias_local)
+            qkv[i], gate_sig[i], zf[i] = project(pc, [first] + rows_one[i][1:], w_one, w_forget, bias_local, width)
             done(qkv[i])
-        ring_go.step(qkv[-1])
         back, own = None, []
         feed_grad = [move_feed[0]]
         for i in reversed(range(chunks)):
             attended[i] = attend(starts[i], sizes[i], at(qkv[i]), zf[i], seqs_each)
             done(attended[i][0])
-            ring_go.step(attended[i][0])
-        w_go = place([at(ring_go.blocks[0])] + ring_go.all()[1:], data.ahead, rows_each)
-        w_gate, w_out = w_go[:, :width], w_go[:, width:]
-        if paired:
-            feed_grad.append(far(move_feed))
-        done(attended[0][0], w_go)
-        for i in reversed(range(chunks)):
-            gate_sig[i], gated[i], parts = close(
-                pc, [at(rows_one[i][0])] + rows_one[i][1:], attended[i][0], w_gate, w_out
-            )
+            gated[i], parts = close(pc, at(attended[i][0]), gate_sig[i], w_out)
             if back is None:
                 sent, back = spread_far(parts)
+                if paired:
+                    feed_grad.append(far(move_feed))
                 done(sent, feed_grad[-1][-1])
             else:
                 own = spread_own(parts, back[0])
@@ -941,8 +939,7 @@
         ]
         grad_feed = weight_grads(pc, groups, "grad_feed", 256)
         done(grad_feed)
-        shard_feed = lax.psum_scatter(after(grad_feed, back[0]), "dp", scatter_dimension=0, tiled=True).astype(F32)
-        shard_up, shard_down = shard_feed[:, :2 * hidden_size], shard_feed[:, 2 * hidden_size:]
+        shard_feed = lax.psum_scatter(after(grad_feed, back[0]), "dp", scatter_dimension=0, tiled=True)
         grad_two = spread_sum([after(back[0], grad_feed)], own)
         grad_middle, gain_two_grad = norm_back(grad_two, middle, scale_two, feed_gain)
         grad_middle = grad_middle + cotangent.astype(F32)
@@ -974,46 +971,63 @@
             *grad_proj[i], grad_zf[i] = attend_back(
                 starts[i], sizes[i], qkv[i], zf[i], attended[i][1], attended[i][0], at(up_stream), seqs_each, 0, pairs
             )
-            done(grad_proj[i][0])
+            grad_proj[i] = [[g] for g in grad_proj[i]]
+            done(grad_proj[i][0][0])
             if i < chunks - 1:
                 out_parts[i] = feed_out(pc, at(hidden[i]), w_feed)
                 done(out_parts[i][0])
-        ring_go.step(grad_proj[-1][0])
+
+        def going():
+            return [m for m in ring_go.moving if m is not None]
+
         bias_local_grad = sum(jnp.sum(z[:, :hb], axis=2).reshape(heads) for z in grad_zf)
-        done(grad_proj[-1][0], *out_back)
-        back, own = None, []
-        for i in reversed(range(chunks)):
-            g = list(grad_proj[i])
-            parts = project_back(pc, [at(g[0])] + g[1:] + [grad_gatepre[i]], grad_zf[i], w_qkv, w_gate, w_forget)
-            if back is None:
-                sent, back = spread_far(parts, 2)
-                done(sent)
-            else:
-                own = spread_own(parts, back[-1])
-                done(parts[0], back[0])
-        ring_go.step(back[0])
+        done(grad_proj[-1][0][0], *going(), *out_back)
+        ring_go.step(grad_proj[-1][0][0])
+
+        def rows_back(i):
+            g = [x for group in grad_proj[i] for x in group]
+            return project_back(pc, [at(g[0])] + g[1:] + [grad_gatepre[i]], grad_zf[i], w_one, w_forget, width)
+
+        parts = rows_back(chunks - 1)
+        sent, back = spread_far(parts, 2)
+        done(sent)
         packed = project_grads(
-            pc,
-            [([at(r[0])] + r[1:], [(x, 0) for x in g], z) for r, g, z in zip(rows_one, grad_proj, grad_zf)],
-            rows_each, tail, width,
+            pc, [([at(r[0])] + r[1:], g, z) for r, g, z in zip(rows_one, grad_proj, grad_zf)], rows_each, tail, hb
         )
-        packed = after(packed, back[-1])
+        packed = after(packed, back[0], *going())
         ring_go.step(packed)
         ring_qkv = data.reduce(packed, -1)
         ring_qkv.step()
-        outputs = middle + spread_sum(out_back, spread_own(out_parts[0]) if paired else [])
+        own = []
+        if paired:
+            done(packed)
+            parts = rows_back(0)
+            own = spread_own(parts, back[-1])
+            outputs = after(middle, parts[0]) + spread_sum(out_back, spread_own(out_parts[0]))
+            ring_qkv.step(parts[0], *going())
+            ring_go.step(parts[0])
+            shard_feed = after(shard_feed, outputs).astype(F32)
+            square_feed = jnp.sum(shard_feed * shard_feed)
+            ring_qkv.step(outputs, *going())
+        else:
+            outputs = middle + spread_sum(out_back, [])
+            shard_feed = shard_feed.astype(F32)
+            square_feed = jnp.sum(shard_feed * shard_feed)
+        shard_up, shard_down = shard_feed[:, :2 * hidden_size], shard_feed[:, 2 * hidden_size:]
+        grad_one = spread_sum(back, own)
+        grad_inputs, gain_one_grad = norm_back(grad_one, inputs_f, scale_one, attn_gain)
+        input_grad = grad_inputs + grad_middle
+        while ring_go.k < dp // 2:
+            ring_go.step()
         shard_go = ring_go.all()
+        square_go = jnp.sum(shard_go * shard_go)
+        ring_qkv.step(square_feed, gain_one_grad)
         shard_gate, shard_out = shard_go[:, :width], shard_go[:, width:]
         shard_qkv = ring_qkv.all()
         shard_forget = shard_qkv[rows_each:rows_each + heads, :rows_each].T
         shard_qkv = shard_qkv[:rows_each]
-        grad_one = spread_sum(back, own)
-        grad_inputs, gain_one_grad = norm_back(grad_one, inputs_f, scale_one, attn_gain)
-        input_grad = grad_inputs + grad_middle
-
         bias_full = jnp.where(jnp.arange(tn)[:, None] == rank, bias_local_grad[None], 0.0).reshape(-1)
-        owned = (shard_qkv, shard_gate, shard_forget, shard_out, shard_up, shard_down)
-        square = sum(jnp.sum(s * s) for s in owned)
+        square = square_feed + square_go + sum(jnp.sum(s * s) for s in (shard_qkv, shard_forget))
         pad = 128 - forget_bias.shape[0] - 1
         packed = jnp.concatenate([gain_one_grad, gain_two_grad, bias_full, square[None], jnp.zeros((pad,), F32)])
         packed = sum_all(sum_all(packed.reshape(-1, 128), "tensor", tn), "dp", dp).reshape(-1)

time: 685 us -> 635 us (0.927)
  waiting for transfers between devices: 197 us -> 160 us
    ppermute x28 -> x21, waiting for transfers between devices: 101 us -> 71.3 us  [step(): lax.ppermute(x, self.axis, [(self.table[r], self.table[(r + way) % n]) fo...]
    ppermute x26, waiting for transfers between devices: 89.2 us -> 76.7 us  [swap(): return lax.ppermute(x, 'tensor', [(i, i ^ bit) for i in range(tn)])]
    unnamed x220 -> x193, local copies, waits for them, and re-layouts: 23.7 us -> 22 us
    ppermute x28 -> x21, starting transfers between devices: 34.7 us -> 34.1 us  [step(): lax.ppermute(x, self.axis, [(self.table[r], self.table[(r + way) % n]) fo...]
  transfers between devices with their start and end apart: 61 -> 54, of which waited for: 37 -> 29; matrix products, arithmetic and copies ran while one was open for 10% -> 11% of each run, Pallas kernels for 38% -> 41%
where the time goes in v3:
time: 635 us; the launch traced here: 631 us
  Pallas kernels  286 us (45%)
  waiting for transfers between devices  160 us (25%)
  other arithmetic  76.8 us (12%)
  starting transfers between devices  50.2 us (8%)
  local copies, waits for them, and re-layouts  36 us (6%)
  between operations  22.1 us (3%)
    pallas_call x12, Pallas kernels, call(): pl.pallas_call(kernel, grid_spec=pltpu.PrefetchScalarGridSpec(num_scalar_...  130 us
    ppermute x26, waiting for transfers between devices, swap(): return lax.ppermute(x, 'tensor', [(i, i ^ bit) for i in range(tn)])  76.7 us
    ppermute x21, waiting for transfers between devices, step(): lax.ppermute(x, self.axis, [(self.table[r], self.table[(r + way) % n]) fo...  71.3 us
    pallas_call x2, Pallas kernels, attend_back(): pl.pallas_call(functools.partial(attn_bwd_kernel, hb=hb), grid_spec=pltpu...  65 us
    pallas_call x2, Pallas kernels, weight_grads(): pl.pallas_call(kernel, grid_spec=pltpu.PrefetchScalarGridSpec(num_scalar_...  39.1 us
    ppermute x21, starting transfers between devices, step(): lax.ppermute(x, self.axis, [(self.table[r], self.table[(r + way) % n]) fo...  34.1 us
    pallas_call x2, Pallas kernels, attend(): pl.pallas_call(functools.partial(attn_fwd_kernel, hb=hb), grid_spec=pltpu...  33.9 us
    unnamed x193, local copies, waits for them, and re-layouts  22 us
  transfers between devices with their start and end apart: 54, of which 29 were waited for; matrix products, arithmetic and copies ran while one was open for 11% of the time, Pallas kernels for 41%

profile of v3, /device:TPU:0, one launch (start us, length us, event | category | flops | bytes accessed | tf_op | source)
XLA Modules:
  0.0 631.3 jit_solution(15588157220137648399)
XLA Ops:
  14.6 16.8 %collective-permute-done.2.refs_1_ = bf16[208,1920]{1,0:T(8,128)(2,1)S(1)} collective-permute-done((bf16[208,1920]{1,0:T(8,128)(2,1)S(1)}, bf16[208,1920]{1,0:T(8,128)(2,1)S(1)}, u32[]{:S(2)}, u32[]{:S(2)}) %collective-permute-start.2) | collective-permute-done | bytes 798752 | tf_op jit(solution)/shard_map/ppermute | solution.py:669
  37.2 16.0 %collective-permute-done = bf16[256,1536]{1,0:T(8,128)(2,1)S(1)} collective-permute-done((bf16[256,1536]{1,0:T(8,128)(2,1)S(1)}, bf16[256,1536]{1,0:T(8,128)(2,1)S(1)}, u32[]{:S(2)}, u32[]{:S(2)}) %collective-permute-start) | collective-permute-done | bytes 786464 | tf_op jit(solution)/shard_map/ppermute | solution.py:802
  56.7 13.9 %collective-permute-done.6.refs_3_ = bf16[208,1920]{1,0:T(8,128)(2,1)} collective-permute-done((bf16[208,1920]{1,0:T(8,128)(2,1)}, bf16[208,1920]{1,0:T(8,128)(2,1)}, u32[]{:S(2)}, u32[]{:S(2)}) %collective-permute-start.6) | collective-permute-done | bytes 798752 | tf_op jit(solution)/shard_map/ppermute | solution.py:669
  76.3 11.5 %collective-permute-done.1 = bf16[256,1536]{1,0:T(8,128)(2,1)S(1)} collective-permute-done((bf16[256,1536]{1,0:T(8,128)(2,1)}, bf16[256,1536]{1,0:T(8,128)(2,1)S(1)}, u32[]{:S(2)}, u32[]{:S(2)}) %collective-permute-start.1) | collective-permute-done | bytes 786464 | tf_op jit(solution)/shard_map/ppermute | solution.py:802
  92.4 13.6 %collective-permute-done.8.refs_4_ = bf16[208,1920]{1,0:T(8,128)(2,1)} collective-permute-done((bf16[208,1920]{1,0:T(8,128)(2,1)}, bf16[208,1920]{1,0:T(8,128)(2,1)}, u32[]{:S(2)}, u32[]{:S(2)}) %collective-permute-start.8) | collective-permute-done | bytes 798752 | tf_op jit(solution)/shard_map/ppermute | solution.py:669
  113.5 10.9 %project.2 = (bf16[1024,1152]{1,0:T(8,128)(2,1)}, f32[1024,384]{1,0:T(8,128)S(1)}, f32[3,8,1024]{2,1,0:T(8,128)S(1)}) custom-call(s32[2]{0:T(128)S(1)} %pad_add_fusion.half, bf16[512,1536]{1,0:T(8,128)(2,1)S(1)} %fusion.4.refs_0_, bf16[512,1536]{1,0:T(8,128)(2,1)} %collective-permute-done.9.refs_1_.refs_2_.refs_5_, bf16[1536,1920]{1,0:T(8,128)(2,1)} %copy-done.13, ...), custom_call_target="tpu_custom_call" | custom-call | flops 7247757312 | bytes 13148256 | tf_op jit(solution)/shard_map/project/pallas_call | solution.py:355
  125.6 10.9 %project.3 = (bf16[1024,1152]{1,0:T(8,128)(2,1)}, f32[1024,384]{1,0:T(8,128)S(1)}, f32[3,8,1024]{2,1,0:T(8,128)S(1)}) custom-call(s32[2]{0:T(128)S(1)} %pad_add_fusion.half, bf16[512,1536]{1,0:T(8,128)(2,1)} %constant_dynamic-update-slice_fusion.refs_0_.refs_4_.refs_10_, bf16[512,1536]{1,0:T(8,128)(2,1)} %collective-permute-done.10.refs_1_.refs_6_.refs_15_, ...), custom_call_target="tpu_custom_call" | custom-call | flops 7247757312 | bytes 13148256 | tf_op jit(solution)/shard_map/project/pallas_call | solution.py:355
  139.0 17.2 %attend.2 = (f32[1024,384]{1,0:T(8,128)S(1)}, f32[3,8,1024]{2,1,0:T(8,128)S(1)}) custom-call(s32[1]{0:T(128)} %get-tuple-element.303.start, s32[1]{0:T(128)} %get-tuple-element.298.size, bf16[1024,1152]{1,0:T(8,128)(2,1)S(1)} %copy-done.26, bf16[1024,1152]{1,0:T(8,128)(2,1)S(1)} %copy-done.26, bf16[1024,1152]{1,0:T(8,128)(2,1)S(1)} %copy-done.26, ...), custom_call_target="tpu_custom_call" | custom-call | flops 10066329600 | bytes 3932160 | tf_op jit(solution)/shard_map/attend/pallas_call | solution.py:250
  170.2 16.7 %attend.3 = (f32[1024,384]{1,0:T(8,128)S(1)}, f32[3,8,1024]{2,1,0:T(8,128)S(1)}) custom-call(s32[1]{0:T(128)} %get-tuple-element.302.start, s32[1]{0:T(128)} %get-tuple-element.299.size, bf16[1024,1152]{1,0:T(8,128)(2,1)S(1)} %copy-done.28, bf16[1024,1152]{1,0:T(8,128)(2,1)S(1)} %copy-done.28, bf16[1024,1152]{1,0:T(8,128)(2,1)S(1)} %copy-done.28, ...), custom_call_target="tpu_custom_call" | custom-call | flops 10066329600 | bytes 3932160 | tf_op jit(solution)/shard_map/attend/pallas_call | solution.py:250
  193.2 12.2 %collective-permute-done.12 = bf16[512,1536]{1,0:T(8,128)(2,1)S(1)} collective-permute-done((bf16[512,1536]{1,0:T(8,128)(2,1)S(1)}, bf16[512,1536]{1,0:T(8,128)(2,1)S(1)}, u32[]{:S(2)}, u32[]{:S(2)}) %collective-permute-start.12) | collective-permute-done | bytes 1572896 | tf_op jit(solution)/shard_map/ppermute | solution.py:802
  219.2 25.2 %feed.2 = (bf16[1024,1024]{1,0:T(8,128)(2,1)}, bf16[1024,2048]{1,0:T(8,128)(2,1)}, bf16[512,1536]{1,0:T(8,128)(2,1)S(1)}, bf16[512,1536]{1,0:T(8,128)(2,1)S(1)}) custom-call(s32[2]{0:T(128)S(1)} %pad_add_fusion.half, bf16[512,1536]{1,0:T(8,128)(2,1)} %multiply_convert_fusion.refs_0_, bf16[512,1536]{1,0:T(8,128)(2,1)} %collective-permute-done.17.refs_1_.refs_2_, ...), custom_call_target="tpu_custom_call" | custom-call | flops 24159191040 | bytes 25165824 | tf_op jit(solution)/shard_map/feed/pallas_call | solution.py:355
  244.6 8.0 %collective-permute-done.16.refs_0_.refs_4_ = bf16[512,1536]{1,0:T(8,128)(2,1)} collective-permute-done((bf16[512,1536]{1,0:T(8,128)(2,1)}, bf16[512,1536]{1,0:T(8,128)(2,1)}, u32[]{:S(2)}, u32[]{:S(2)}) %collective-permute-start.16) | collective-permute-done | bytes 1572896 | tf_op jit(solution)/shard_map/ppermute | solution.py:802
  257.4 25.0 %feed.3 = (bf16[1024,1024]{1,0:T(8,128)(2,1)}, bf16[1024,2048]{1,0:T(8,128)(2,1)}, bf16[512,1536]{1,0:T(8,128)(2,1)S(1)}, bf16[512,1536]{1,0:T(8,128)(2,1)S(1)}) custom-call(s32[2]{0:T(128)S(1)} %pad_add_fusion.half, bf16[512,1536]{1,0:T(8,128)(2,1)} %collective-permute-done.16.refs_0_.refs_4_, bf16[512,1536]{1,0:T(8,128)(2,1)} %copy-done.95, ...), custom_call_target="tpu_custom_call" | custom-call | flops 24159191040 | bytes 25165824 | tf_op jit(solution)/shard_map/feed/pallas_call | solution.py:355
  287.7 28.1 %grad_feed.1 = bf16[1536,3072]{1,0:T(8,128)(2,1)} custom-call(s32[2]{0:T(128)S(1)} %pad_add_fusion.half, bf16[512,1536]{1,0:T(8,128)(2,1)} %multiply_convert_fusion.refs_0_, bf16[1024,2048]{1,0:T(8,128)(2,1)} %get-tuple-element.171.refs_1_.refs_3_, bf16[512,1536]{1,0:T(8,128)(2,1)} %collective-permute-done.17.refs_1_.refs_2_, ...), custom_call_target="tpu_custom_call" | custom-call | flops 28991029248 | bytes 28311552 | tf_op jit(solution)/shard_map/grad_feed/pallas_call | solution.py:536
  315.8 8.3 %collective-permute-done.22 = bf16[512,1536]{1,0:T(8,128)(2,1)} collective-permute-done((bf16[512,1536]{1,0:T(8,128)(2,1)}, bf16[512,1536]{1,0:T(8,128)(2,1)}, u32[]{:S(2)}, u32[]{:S(2)}) %collective-permute-start.22) | collective-permute-done | bytes 1572896 | tf_op jit(solution)/shard_map/ppermute | solution.py:802
  334.8 7.8 %feed_out.2 = (bf16[512,1536]{1,0:T(8,128)(2,1)S(1)}, bf16[512,1536]{1,0:T(8,128)(2,1)}) custom-call(s32[2]{0:T(128)S(1)} %pad_add_fusion.half, bf16[1024,1024]{1,0:T(8,128)(2,1)S(1)} %copy-done.25, bf16[1536,3072]{1,0:T(8,128)(2,1)} %all-gather.2.cloned.1.call-done.refs_4_.w_ref), custom_call_target="tpu_custom_call" | custom-call | flops 4831838208 | bytes 14680064 | tf_op jit(solution)/shard_map/feed_out/pallas_call | solution.py:355
  349.6 32.6 %attend_back.2 = (bf16[1024,384]{1,0:T(8,128)(2,1)S(1)}, bf16[1024,384]{1,0:T(8,128)(2,1)S(1)}, bf16[1024,384]{1,0:T(8,128)(2,1)S(1)}, f32[3,8,1024]{2,1,0:T(8,128)S(1)}) custom-call(s32[1]{0:T(128)} %get-tuple-element.302.start, s32[1]{0:T(128)} %get-tuple-element.299.size, bf16[1024,1152]{1,0:T(8,128)(2,1)S(1)} %copy-done.29, ...), custom_call_target="tpu_custom_call" | custom-call | flops 16357785600 | bytes 7864320 | tf_op jit(solution)/shard_map/attend_back/pallas_call | solution.py:274
  389.3 7.0 %feed_out.3 = (bf16[512,1536]{1,0:T(8,128)(2,1)S(1)}, bf16[512,1536]{1,0:T(8,128)(2,1)S(1)}) custom-call(s32[2]{0:T(128)S(1)} %pad_add_fusion.half, bf16[1024,1024]{1,0:T(8,128)(2,1)S(1)} %copy-done.24, bf16[1536,3072]{1,0:T(8,128)(2,1)} %all-gather.2.cloned.1.call-done.refs_4_.w_ref), custom_call_target="tpu_custom_call" | custom-call | flops 4831838208 | bytes 14680064 | tf_op jit(solution)/shard_map/feed_out/pallas_call | solution.py:355
  401.6 10.9 %grad_gate_out.1 = bf16[1536,768]{1,0:T(8,128)(2,1)} custom-call(s32[2]{0:T(128)S(1)} %pad_add_fusion.half, bf16[512,1536]{1,0:T(8,128)(2,1)} %copy-done, bf16[1024,384]{1,0:T(8,128)(2,1)S(1)} %get-tuple-element.188.refs_1_.refs_3_, bf16[512,1536]{1,0:T(8,128)(2,1)} %collective-permute-done.9.refs_1_.refs_2_.refs_5_, ...), custom_call_target="tpu_custom_call" | custom-call | flops 7247757312 | bytes 7077888 | tf_op jit(solution)/shard_map/grad_gate_out/pallas_call | solution.py:536
  429.7 32.4 %attend_back.3 = (bf16[1024,384]{1,0:T(8,128)(2,1)S(1)}, bf16[1024,384]{1,0:T(8,128)(2,1)S(1)}, bf16[1024,384]{1,0:T(8,128)(2,1)S(1)}, f32[3,8,1024]{2,1,0:T(8,128)S(1)}) custom-call(s32[1]{0:T(128)} %get-tuple-element.303.start, s32[1]{0:T(128)} %get-tuple-element.298.size, bf16[1024,1152]{1,0:T(8,128)(2,1)S(1)} %copy-done.27, ...), custom_call_target="tpu_custom_call" | custom-call | flops 16357785600 | bytes 7864320 | tf_op jit(solution)/shard_map/attend_back/pallas_call | solution.py:274
  462.2 11.1 %project_back.2 = (bf16[512,1536]{1,0:T(8,128)(2,1)S(1)}, bf16[512,1536]{1,0:T(8,128)(2,1)}) custom-call(s32[2]{0:T(128)S(1)} %pad_add_fusion.half, bf16[1024,384]{1,0:T(8,128)(2,1)S(1)} %get-tuple-element.198.refs_0_.refs_11_.refs_16_, bf16[1024,384]{1,0:T(8,128)(2,1)S(1)} %get-tuple-element.199.refs_1_.refs_12_.refs_17_, ...), custom_call_target="tpu_custom_call" | custom-call | flops 7247757312 | bytes 12361728 | tf_op jit(solution)/shard_map/project_back/pallas_call | solution.py:355
  481.3 15.1 %project_grads.1 = bf16[8,208,1152]{2,1,0:T(8,128)(2,1)} custom-call(s32[2]{0:T(128)S(1)} %pad_add_fusion.half, bf16[512,1536]{1,0:T(8,128)(2,1)} %copy-done, bf16[1024,384]{1,0:T(8,128)(2,1)S(1)} %copy-done.31, bf16[1024,384]{1,0:T(8,128)(2,1)S(1)} %copy-done.33, bf16[1024,384]{1,0:T(8,128)(2,1)S(1)} %copy-done.35, ...), custom_call_target="tpu_custom_call" | custom-call | flops 10871635968 | bytes 10616832 | tf_op jit(solution)/shard_map/project_grads/pallas_call | solution.py:600
  512.3 10.7 %project_back.3 = (bf16[512,1536]{1,0:T(8,128)(2,1)S(1)}, bf16[512,1536]{1,0:T(8,128)(2,1)}) custom-call(s32[2]{0:T(128)S(1)} %pad_add_fusion.half, bf16[1024,384]{1,0:T(8,128)(2,1)S(1)} %copy-done.31, bf16[1024,384]{1,0:T(8,128)(2,1)S(1)} %copy-done.33, bf16[1024,384]{1,0:T(8,128)(2,1)S(1)} %copy-done.35, ...), custom_call_target="tpu_custom_call" | custom-call | flops 7247757312 | bytes 12361728 | tf_op jit(solution)/shard_map/project_back/pallas_call | solution.py:355
  536.5 6.8 %collective-permute-done.42 = bf16[208,1152]{1,0:T(8,128)(2,1)S(1)} collective-permute-done((bf16[208,1152]{1,0:T(8,128)(2,1)S(1)}, bf16[208,1152]{1,0:T(8,128)(2,1)S(1)}, u32[]{:S(2)}, u32[]{:S(2)}) %collective-permute-start.42) | collective-permute-done | bytes 479264 | tf_op jit(solution)/shard_map/ppermute | solution.py:669
  (383 shorter events, 240.5 us)
Async XLA Ops:
  7.2 211.6 %all-gather.2.cloned.1.call-start = ((), (), s32[]{:S(2)}) async-start(), calls=%async_computation.1 | async-start | bytes 10616832 | tf_op jit(solution)/shard_map/all_gather | solution.py:890
  10.4 20.9 %collective-permute-start.2 = (bf16[208,1920]{1,0:T(8,128)(2,1)S(1)}, bf16[208,1920]{1,0:T(8,128)(2,1)S(1)}, u32[]{:S(2)}, u32[]{:S(2)}) collective-permute-start(bf16[208,1920]{1,0:T(8,128)(2,1)S(1)} %fusion.23.refs_0_), channel_id=1, source_target_pairs={{0,4},{8,0},{16,8},{24,16},{28,24},{20,28},{12,20},{4,12},{1,5},{9... | collective-permute-start | bytes 2396168 | tf_op jit(solution)/shard_map/ppermute | solution.py:669
  13.4 19.3 %collective-permute-start.3 = (bf16[208,1920]{1,0:T(8,128)(2,1)S(1)}, bf16[208,1920]{1,0:T(8,128)(2,1)S(1)}, u32[]{:S(2)}, u32[]{:S(2)}) collective-permute-start(bf16[208,1920]{1,0:T(8,128)(2,1)S(1)} %fusion.23.refs_0_), channel_id=1, source_target_pairs={{0,8},{8,16},{16,24},{24,28},{28,20},{20,12},{12,4},{4,0},{1,9},{9... | collective-permute-start | bytes 2396168 | tf_op jit(solution)/shard_map/ppermute | solution.py:669
  32.7 20.5 %collective-permute-start.4 = (bf16[208,1920]{1,0:T(8,128)(2,1)S(1)}, bf16[208,1920]{1,0:T(8,128)(2,1)}, u32[]{:S(2)}, u32[]{:S(2)}) collective-permute-start(bf16[208,1920]{1,0:T(8,128)(2,1)S(1)} %collective-permute-done.2.refs_1_), channel_id=1, source_target_pairs={{0,4},{8,0},{16,8},{24,16},{28,24},{20,28},{12,20},{4,12},{1,5},{9... | collective-permute-start | bytes 2396168 | tf_op jit(solution)/shard_map/ppermute | solution.py:669
  34.3 19.0 %collective-permute-start.5 = (bf16[208,1920]{1,0:T(8,128)(2,1)S(1)}, bf16[208,1920]{1,0:T(8,128)(2,1)}, u32[]{:S(2)}, u32[]{:S(2)}) collective-permute-start(bf16[208,1920]{1,0:T(8,128)(2,1)S(1)} %collective-permute-done.3.refs_7_), channel_id=1, source_target_pairs={{0,8},{8,16},{16,24},{24,28},{28,20},{20,12},{12,4},{4,0},{1,9},{9... | collective-permute-start | bytes 2396168 | tf_op jit(solution)/shard_map/ppermute | solution.py:669
  71.9 482.9 %reduce-scatter.2.cloned.1.call-start = ((), (), s32[]{:S(2)}) async-start(), calls=%async_computation.2 | async-start | bytes 10616832 | tf_op jit(solution)/shard_map/reduce_scatter | solution.py:942
  73.6 39.9 %collective-permute-start.9 = (bf16[512,1536]{1,0:T(8,128)(2,1)S(1)}, bf16[512,1536]{1,0:T(8,128)(2,1)}, u32[]{:S(2)}, u32[]{:S(2)}) collective-permute-start(bf16[512,1536]{1,0:T(8,128)(2,1)S(1)} %fusion.4.refs_0_), channel_id=1, source_target_pairs={{0,1},{1,0},{2,3},{3,2},{4,5},{5,4},{6,7},{7,6},{8,9},{9,8},{10,11... | collective-permute-start | bytes 4718600 | tf_op jit(solution)/shard_map/ppermute | solution.py:802
  73.6 32.4 %collective-permute-start.8 = (bf16[208,1920]{1,0:T(8,128)(2,1)}, bf16[208,1920]{1,0:T(8,128)(2,1)}, u32[]{:S(2)}, u32[]{:S(2)}) collective-permute-start(bf16[208,1920]{1,0:T(8,128)(2,1)} %collective-permute-done.7.refs_5_), channel_id=1, source_target_pairs={{0,8},{8,16},{16,24},{24,28},{28,20},{20,12},{12,4},{4,0},{1,9},{9... | collective-permute-start | bytes 2396168 | tf_op jit(solution)/shard_map/ppermute | solution.py:669
  88.7 36.9 %collective-permute-start.10 = (bf16[512,1536]{1,0:T(8,128)(2,1)}, bf16[512,1536]{1,0:T(8,128)(2,1)}, u32[]{:S(2)}, u32[]{:S(2)}) collective-permute-start(bf16[512,1536]{1,0:T(8,128)(2,1)} %constant_dynamic-update-slice_fusion.refs_0_.refs_4_.refs_10_), channel_id=1, source_target_pairs={{0,1},{1,0},{2,3},{3,2},{4,5},{5,4},{6,7},{7,6},{8,9},{9,8},{10,11... | collective-permute-start | bytes 4718600 | tf_op jit(solution)/shard_map/ppermute | solution.py:802
  90.9 72.9 %collective-permute-start.13 = (bf16[512,1536]{1,0:T(8,128)(2,1)}, bf16[512,1536]{1,0:T(8,128)(2,1)}, u32[]{:S(2)}, u32[]{:S(2)}) collective-permute-start(bf16[512,1536]{1,0:T(8,128)(2,1)} %refs_8_), channel_id=1, source_target_pairs={{0,2},{1,3},{2,0},{3,1},{4,6},{5,7},{6,4},{7,5},{8,10},{9,11},{10,... | collective-permute-start | bytes 4718600 | tf_op jit(solution)/shard_map/ppermute | solution.py:802
  168.9 36.5 %collective-permute-start.12 = (bf16[512,1536]{1,0:T(8,128)(2,1)S(1)}, bf16[512,1536]{1,0:T(8,128)(2,1)S(1)}, u32[]{:S(2)}, u32[]{:S(2)}) collective-permute-start(bf16[512,1536]{1,0:T(8,128)(2,1)S(1)} %add_convert_fusion.3), channel_id=1, source_target_pairs={{0,2},{1,3},{2,0},{3,1},{4,6},{5,7},{6,4},{7,5},{8,10},{9,11},{10,... | collective-permute-start | bytes 4718600 | tf_op jit(solution)/shard_map/ppermute | solution.py:802
  215.6 37.0 %collective-permute-start.16 = (bf16[512,1536]{1,0:T(8,128)(2,1)}, bf16[512,1536]{1,0:T(8,128)(2,1)}, u32[]{:S(2)}, u32[]{:S(2)}) collective-permute-start(bf16[512,1536]{1,0:T(8,128)(2,1)} %multiply_convert_fusion.refs_0_), channel_id=1, source_target_pairs={{0,2},{1,3},{2,0},{3,1},{4,6},{5,7},{6,4},{7,5},{8,10},{9,11},{10,... | collective-permute-start | bytes 4718600 | tf_op jit(solution)/shard_map/ppermute | solution.py:802
  287.4 36.8 %collective-permute-start.22 = (bf16[512,1536]{1,0:T(8,128)(2,1)}, bf16[512,1536]{1,0:T(8,128)(2,1)}, u32[]{:S(2)}, u32[]{:S(2)}) collective-permute-start(bf16[512,1536]{1,0:T(8,128)(2,1)} %add_convert_fusion.2), channel_id=1, source_target_pairs={{0,2},{1,3},{2,0},{3,1},{4,6},{5,7},{6,4},{7,5},{8,10},{9,11},{10,... | collective-permute-start | bytes 4718600 | tf_op jit(solution)/shard_map/ppermute | solution.py:802
  334.5 50.3 %collective-permute-start.24 = (bf16[512,1536]{1,0:T(8,128)(2,1)S(1)}, bf16[512,1536]{1,0:T(8,128)(2,1)S(1)}, u32[]{:S(2)}, u32[]{:S(2)}) collective-permute-start(bf16[512,1536]{1,0:T(8,128)(2,1)S(1)} %get-tuple-element.178.refs_0_.refs_8_), channel_id=1, source_target_pairs={{0,2},{1,3},{2,0},{3,1},{4,6},{5,7},{6,4},{7,5},{8,10},{9,11},{10,... | collective-permute-start | bytes 4718600 | tf_op jit(solution)/shard_map/ppermute | solution.py:802
  388.3 24.3 %collective-permute-start.26 = (bf16[512,1536]{1,0:T(8,128)(2,1)}, bf16[512,1536]{1,0:T(8,128)(2,1)}, u32[]{:S(2)}, u32[]{:S(2)}) collective-permute-start(bf16[512,1536]{1,0:T(8,128)(2,1)} %get-tuple-element.195), channel_id=1, source_target_pairs={{0,1},{1,0},{2,3},{3,2},{4,5},{5,4},{6,7},{7,6},{8,9},{9,8},{10,11... | collective-permute-start | bytes 4718600 | tf_op jit(solution)/shard_map/ppermute | solution.py:802
  414.6 47.6 %collective-permute-start.29 = (bf16[512,1536]{1,0:T(8,128)(2,1)S(1)}, bf16[512,1536]{1,0:T(8,128)(2,1)S(1)}, u32[]{:S(2)}, u32[]{:S(2)}) collective-permute-start(bf16[512,1536]{1,0:T(8,128)(2,1)S(1)} %add_convert_fusion.1), channel_id=1, source_target_pairs={{0,2},{1,3},{2,0},{3,1},{4,6},{5,7},{6,4},{7,5},{8,10},{9,11},{10,... | collective-permute-start | bytes 4718600 | tf_op jit(solution)/shard_map/ppermute | solution.py:802
  419.0 43.2 %collective-permute-start.27 = (bf16[192,768]{1,0:T(8,128)(2,1)S(1)}, bf16[192,768]{1,0:T(8,128)(2,1)S(1)}, u32[]{:S(2)}, u32[]{:S(2)}) collective-permute-start(bf16[192,768]{1,0:T(8,128)(2,1)S(1)} %get-tuple-element.278), channel_id=1, source_target_pairs={{0,8},{8,16},{16,24},{24,28},{28,20},{20,12},{12,4},{4,0},{1,9},{9... | collective-permute-start | bytes 884744 | tf_op jit(solution)/shard_map/ppermute | solution.py:669
  425.6 36.5 %collective-permute-start.28 = (bf16[192,768]{1,0:T(8,128)(2,1)S(1)}, bf16[192,768]{1,0:T(8,128)(2,1)S(1)}, u32[]{:S(2)}, u32[]{:S(2)}) collective-permute-start(bf16[192,768]{1,0:T(8,128)(2,1)S(1)} %get-tuple-element.277), channel_id=1, source_target_pairs={{0,4},{8,0},{16,8},{24,16},{28,24},{20,28},{12,20},{4,12},{1,5},{9... | collective-permute-start | bytes 884744 | tf_op jit(solution)/shard_map/ppermute | solution.py:669
  476.4 19.9 %collective-permute-start.32 = (bf16[192,768]{1,0:T(8,128)(2,1)S(1)}, bf16[192,768]{1,0:T(8,128)(2,1)S(1)}, u32[]{:S(2)}, u32[]{:S(2)}) collective-permute-start(bf16[192,768]{1,0:T(8,128)(2,1)S(1)} %get-tuple-element.276), channel_id=1, source_target_pairs={{0,8},{8,16},{16,24},{24,28},{28,20},{20,12},{12,4},{4,0},{1,9},{9... | collective-permute-start | bytes 884744 | tf_op jit(solution)/shard_map/ppermute | solution.py:669
  476.5 22.7 %collective-permute-start.33 = (bf16[192,768]{1,0:T(8,128)(2,1)S(1)}, bf16[192,768]{1,0:T(8,128)(2,1)S(1)}, u32[]{:S(2)}, u32[]{:S(2)}) collective-permute-start(bf16[192,768]{1,0:T(8,128)(2,1)S(1)} %get-tuple-element.275), channel_id=1, source_target_pairs={{0,4},{8,0},{16,8},{24,16},{28,24},{20,28},{12,20},{4,12},{1,5},{9... | collective-permute-start | bytes 884744 | tf_op jit(solution)/shard_map/ppermute | solution.py:669
  479.1 20.1 %collective-permute-start.31 = (bf16[256,1536]{1,0:T(8,128)(2,1)S(1)}, bf16[256,1536]{1,0:T(8,128)(2,1)S(1)}, u32[]{:S(2)}, u32[]{:S(2)}) collective-permute-start(bf16[256,1536]{1,0:T(8,128)(2,1)S(1)} %get-tuple-element.280), channel_id=1, source_target_pairs={{0,2},{1,3},{2,0},{3,1},{4,6},{5,7},{6,4},{7,5},{8,10},{9,11},{10,... | collective-permute-start | bytes 2359304 | tf_op jit(solution)/shard_map/ppermute | solution.py:802
  503.4 29.0 %collective-permute-start.34 = (bf16[512,1536]{1,0:T(8,128)(2,1)S(1)}, bf16[512,1536]{1,0:T(8,128)(2,1)}, u32[]{:S(2)}, u32[]{:S(2)}) collective-permute-start(bf16[512,1536]{1,0:T(8,128)(2,1)S(1)} %copy-done.17), channel_id=1, source_target_pairs={{0,1},{1,0},{2,3},{3,2},{4,5},{5,4},{6,7},{7,6},{8,9},{9,8},{10,11... | collective-permute-start | bytes 4718600 | tf_op jit(solution)/shard_map/ppermute | solution.py:802
  506.0 21.0 %collective-permute-start.35 = (bf16[256,1536]{1,0:T(8,128)(2,1)S(1)}, bf16[256,1536]{1,0:T(8,128)(2,1)S(1)}, u32[]{:S(2)}, u32[]{:S(2)}) collective-permute-start(bf16[256,1536]{1,0:T(8,128)(2,1)S(1)} %get-tuple-element.216), channel_id=1, source_target_pairs={{0,2},{1,3},{2,0},{3,1},{4,6},{5,7},{6,4},{7,5},{8,10},{9,11},{10,... | collective-permute-start | bytes 2359304 | tf_op jit(solution)/shard_map/ppermute | solution.py:802
  527.0 24.5 %collective-permute-start.36 = (bf16[512,1536]{1,0:T(8,128)(2,1)}, bf16[512,1536]{1,0:T(8,128)(2,1)}, u32[]{:S(2)}, u32[]{:S(2)}) collective-permute-start(bf16[512,1536]{1,0:T(8,128)(2,1)} %get-tuple-element.218), channel_id=1, source_target_pairs={{0,1},{1,0},{2,3},{3,2},{4,5},{5,4},{6,7},{7,6},{8,9},{9,8},{10,11... | collective-permute-start | bytes 4718600 | tf_op jit(solution)/shard_map/ppermute | solution.py:802
  (126 other events, 1264.6 us)
Sparse Core Ops, SparseCore 0:
  72.0 146.7 all-gather.1
  324.3 183.1 reduce-scatter.1

commit v4 on v3

--- a/solution.py
+++ b/solution.py
@@ -72,40 +72,51 @@
     if lse_ref.shape[0] > hb:
         lse_ref[...] = jnp.zeros(lse_ref.shape, F32)
 
+    def stack(rows):
+        return jnp.concatenate([jnp.broadcast_to(r, (PIECE, r.shape[1])) for r in rows], axis=0)
+
+    causal = jnp.concatenate([causal] * hb, axis=0)
+    heads = range(hb)
+    spans_of = [slice(h * PIECE, (h + 1) * PIECE) for h in heads]
+
     def block(i, wide):
         lo, hi = i * PIECE, (i + 1) * PIECE
         in_pic = (lo >= first) & (lo < first + extent)
+        q_all = q_ref[lo:hi, :]
+        q = jnp.concatenate([jnp.where(m, q_all, jnp.zeros((), LOW)) for m in mine], axis=0)
+        c_row = [c_rows[h:h + 1, :] for h in heads]
+        base = [c_row[h][:, lo:lo + 1] for h in heads]
+        back = jnp.concatenate([base[h] - 2.0 * c_cols[lo:hi, h:h + 1] for h in heads], axis=0)
+        parts, spans = [], []
+        if i:
+            parts.append(mm(q, k_ref[0:lo, :], NT) + stack([base[h] - c_row[h][:, :lo] for h in heads]))
+            spans.append((0, lo))
+        ahead = stack([base[h] - c_row[h][:, lo:hi] for h in heads])
+        other = jnp.where(in_pic, back + stack([c_row[h][:, lo:hi] for h in heads]), HIDE)
+        parts.append(mm(q, k_ref[lo:hi, :], NT) + jnp.where(causal, ahead, other))
+        spans.append((lo, hi))
+        if wide:
+            more = stack([c_row[h][:, hi:hi + PIECE] for h in heads])
+            parts.append(mm(q, k_ref[hi:hi + PIECE, :], NT) + (back + more))
+            spans.append((hi, hi + PIECE))
+        peak = functools.reduce(jnp.maximum, [jnp.max(p, axis=1, keepdims=True) for p in parts])
+        acc = [None] * hb
+        for p, (a, b) in zip(parts, spans):
+            p = jnp.exp2(p - peak).astype(LOW)
+            for h in heads:
+                v = jnp.where(mine[h], v_ref[a:b, :], jnp.ones((), LOW))
+                t = mm(p[spans_of[h]], v)
+                acc[h] = t if acc[h] is None else acc[h] + t
         out, lse = None, None
-        for h in range(hb):
-            q = jnp.where(mine[h], q_ref[lo:hi, :], jnp.zeros((), LOW))
-            c_row = c_rows[h:h + 1, :]
-            c_col = c_cols[lo:hi, h:h + 1]
-            base = c_row[:, lo:lo + 1]
-            parts, spans = [], []
-            if i:
-                parts.append(mm(q, k_ref[0:lo, :], NT) + (base - c_row[:, :lo]))
-                spans.append((0, lo))
-            back = base - 2.0 * c_col
-            other = jnp.where(in_pic, back + c_row[:, lo:hi], HIDE)
-            parts.append(mm(q, k_ref[lo:hi, :], NT) + jnp.where(causal, base - c_row[:, lo:hi], other))
-            spans.append((lo, hi))
-            if wide:
-                parts.append(mm(q, k_ref[hi:hi + PIECE, :], NT) + (back + c_row[:, hi:hi + PIECE]))
-                spans.append((hi, hi + PIECE))
-            peak = functools.reduce(jnp.maximum, [jnp.max(p, axis=1, keepdims=True) for p in parts])
-            acc = None
-            for p, (a, b) in zip(parts, spans):
-                v = jnp.where(mine[h], v_ref[a:b, :], jnp.ones((), LOW))
-                t = mm(jnp.exp2(p - peak).astype(LOW), v)
-                acc = t if acc is None else acc + t
-            total = acc[:, spare[h]:spare[h] + 1]
-            o_h = acc / total
-            l_h = jnp.broadcast_to(peak + jnp.log2(total), o_h.shape)
+        for h in heads:
+            total = acc[h][:, spare[h]:spare[h] + 1]
+            o_h = acc[h] / total
+            l_h = jnp.broadcast_to(peak[spans_of[h]] + jnp.log2(total), o_h.shape)
             out = o_h if out is None else jnp.where(mine[h], o_h, out)
             lse = l_h if lse is None else jnp.where(mine[h], l_h, lse)
         o_ref[lo:hi, :] = out
         turned = lse.T
-        for h in range(hb):
+        for h in heads:
             lse_ref[h:h + 1, lo:hi] = turned[h * HEAD_DIM:h * HEAD_DIM + 1, :]
 
     for i in range(count):
@@ -143,45 +154,47 @@
     p_lo = (prod - p_hi.astype(F32)).astype(LOW)
     delta = mm(pick, p_hi, NT) + mm(pick, p_lo, NT)
 
+    heads = range(hb)
+    parts_of = [slice(h * PIECE, (h + 1) * PIECE) for h in heads]
+    causal_all = jnp.concatenate([causal] * hb, axis=1)
+
+    def side(xs):
+        return jnp.concatenate(xs, axis=1)
+
     def block(i, wide):
         lo, hi = i * PIECE, (i + 1) * PIECE
         in_pic = (lo >= first) & (lo < first + extent)
-        out = None
-        for h in range(hb):
-            q_all = q_ref[lo:hi, :]
-            q = jnp.where(mine[h], q_all, zero)
-            q_one = jnp.where(mine[h], q_all, one)
-            do = jnp.where(mine[h], do_ref[lo:hi, :], zero)
-            c_row = c_rows[h:h + 1, lo:hi]
-            base = c_row[:, :1]
-            lse = lse_ref[h:h + 1, lo:hi]
-            dl = delta[h:h + 1, lo:hi]
-            back = base - 2.0 * c_row - lse
-            acc = None
-            todo = ([(0, lo, 0)] if i else []) + [(lo, hi, 1)] + ([(hi, hi + PIECE, 2)] if wide else [])
-            for a, b, kind in todo:
-                c_col = c_cols[a:b, h:h + 1]
-                st = mm(k_ref[a:b, :], q, NT)
-                if kind == 0:
-                    st = st + (base - c_col) - lse
-                elif kind == 1:
-                    other = jnp.where(in_pic, back + c_col, HIDE)
-                    st = st + jnp.where(causal, (base - c_col) - lse, other)
-                else:
-                    st = st + (back + c_col)
-                p = jnp.exp2(st)
-                ds = p * (mm(v_ref[a:b, :], do, NT) - dl)
-                ds = ds.astype(LOW)
-                dv_acc[a:b, :] += mm(p.astype(LOW), do)
-                k_one = jnp.where(mine[h], k_ref[a:b, :], one)
-                if kind == 2:
-                    q_one = jnp.where(mine[h], q_all, -one)
-                    k_one = jnp.where(mine[h], k_ref[a:b, :], -one)
-                dk_acc[h, a:b, :] += mm(ds, q_one)
-                t = mm(ds, k_one, TN)
-                acc = t if acc is None else acc + t
+        q_all, do_all = q_ref[lo:hi, :], do_ref[lo:hi, :]
+        q = jnp.concatenate([jnp.where(m, q_all, zero) for m in mine], axis=0)
+        do = jnp.concatenate([jnp.where(m, do_all, zero) for m in mine], axis=0)
+        c_row = [c_rows[h:h + 1, lo:hi] for h in heads]
+        lse = side([lse_ref[h:h + 1, lo:hi] for h in heads])
+        dl = side([delta[h:h + 1, lo:hi] for h in heads])
+        base = side([jnp.broadcast_to(c[:, :1], (1, PIECE)) for c in c_row])
+        ahead = base - lse
+        back = ahead - 2.0 * side(c_row)
+        acc = [None] * hb
+        todo = ([(0, lo, 0)] if i else []) + [(lo, hi, 1)] + ([(hi, hi + PIECE, 2)] if wide else [])
+        for a, b, kind in todo:
+            c_col = side([jnp.broadcast_to(c_cols[a:b, h:h + 1], (b - a, PIECE)) for h in heads])
+            st = mm(k_ref[a:b, :], q, NT)
+            if kind == 0:
+                st = st + (ahead - c_col)
+            elif kind == 1:
+                st = st + jnp.where(causal_all, ahead - c_col, jnp.where(in_pic, back + c_col, HIDE))
+            else:
+                st = st + (back + c_col)
+            p = jnp.exp2(st)
+            ds_all = (p * (mm(v_ref[a:b, :], do, NT) - dl)).astype(LOW)
+            dv_acc[a:b, :] += mm(p.astype(LOW), do)
+            mark = -one if kind == 2 else one
+            for h in heads:
+                ds = ds_all[:, parts_of[h]]
+                dk_acc[h, a:b, :] += mm(ds, jnp.where(mine[h], q_all, mark))
+                t = mm(ds, jnp.where(mine[h], k_ref[a:b, :], mark), TN)
+                acc[h] = t if acc[h] is None else acc[h] + t
                 if kind == 1:
-                    def signs(ds=ds, lo=lo, hi=hi, h=h):
+                    def signs(ds=ds, h=h):
                         minus = jnp.where(causal, zero, ds)
                         m2 = jnp.where(mine[h], zero, jnp.full((), -2.0, LOW))
                         m2 = jnp.broadcast_to(m2, (PIECE, width))
@@ -191,10 +204,11 @@
                         dc_acc[h] = jnp.zeros((PIECE, width), F32)
                     pl.when(in_pic)(signs)
                     pl.when(jnp.logical_not(in_pic))(none)
-                    acc = acc + dc_acc[h]
-            out = acc if out is None else jnp.where(mine[h], acc, out)
-            dc_row = acc.T[spare[h]:spare[h] + 1, :]
-            dzf_ref[h:h + 1, lo:hi] = dc_row
+                    acc[h] = acc[h] + dc_acc[h]
+        out = acc[0]
+        for h in heads:
+            out = jnp.where(mine[h], acc[h], out)
+            dzf_ref[h:h + 1, lo:hi] = acc[h].T[spare[h]:spare[h] + 1, :]
         dq_ref[lo:hi, :] = (out * HEAD_DIM ** -0.5).astype(LOW)
 
     if dzf_ref.shape[0] > hb:

time: 635 us -> 634 us (level)
  starting transfers between devices: 50.2 us -> 57.9 us
  Pallas kernels: 286 us -> 279 us
    pallas_call x2, Pallas kernels: 65 us -> 52.2 us  [attend_back(): pl.pallas_call(functools.partial(attn_bwd_kernel, hb=hb), grid_spec=pltpu...]
    pallas_call x12, Pallas kernels: 130 us -> 141 us  [call(): pl.pallas_call(kernel, grid_spec=pltpu.PrefetchScalarGridSpec(num_scalar_...]
    ppermute x21, starting transfers between devices: 34.1 us -> 41 us  [step(): lax.ppermute(x, self.axis, [(self.table[r], self.table[(r + way) % n]) fo...]
  transfers between devices with their start and end apart: 54 -> 54, of which waited for: 29 -> 29; matrix products, arithmetic and copies ran while one was open for 11% -> 11% of each run, Pallas kernels for 41% -> 40%
where the time goes in v4:
time: 634 us; the launch traced here: 630 us
  Pallas kernels  279 us (44%)
  waiting for transfers between devices  158 us (25%)
  other arithmetic  76.8 us (12%)
  starting transfers between devices  57.9 us (9%)
  local copies, waits for them, and re-layouts  35.9 us (6%)
  between operations  22.1 us (3%)
    pallas_call x12, Pallas kernels, call(): pl.pallas_call(kernel, grid_spec=pltpu.PrefetchScalarGridSpec(num_scalar_...  141 us
    ppermute x26, waiting for transfers between devices, swap(): return lax.ppermute(x, 'tensor', [(i, i ^ bit) for i in range(tn)])  74.2 us
    ppermute x21, waiting for transfers between devices, step(): lax.ppermute(x, self.axis, [(self.table[r], self.table[(r + way) % n]) fo...  68.2 us
    pallas_call x2, Pallas kernels, attend_back(): pl.pallas_call(functools.partial(attn_bwd_kernel, hb=hb), grid_spec=pltpu...  52.2 us
    ppermute x21, starting transfers between devices, step(): lax.ppermute(x, self.axis, [(self.table[r], self.table[(r + way) % n]) fo...  41 us
    pallas_call x2, Pallas kernels, weight_grads(): pl.pallas_call(kernel, grid_spec=pltpu.PrefetchScalarGridSpec(num_scalar_...  39.1 us
    pallas_call x2, Pallas kernels, attend(): pl.pallas_call(functools.partial(attn_fwd_kernel, hb=hb), grid_spec=pltpu...  28.3 us
    unnamed x193, local copies, waits for them, and re-layouts  22 us
  transfers between devices with their start and end apart: 54, of which 29 were waited for; matrix products, arithmetic and copies ran while one was open for 11% of the time, Pallas kernels for 40%

profile of v4, /device:TPU:0, one launch (start us, length us, event | category | flops | bytes accessed | tf_op | source)
XLA Modules:
  0.0 629.9 jit_solution(15240391475056022292)
XLA Ops:
  14.6 16.8 %collective-permute-done.2.refs_1_ = bf16[208,1920]{1,0:T(8,128)(2,1)S(1)} collective-permute-done((bf16[208,1920]{1,0:T(8,128)(2,1)S(1)}, bf16[208,1920]{1,0:T(8,128)(2,1)S(1)}, u32[]{:S(2)}, u32[]{:S(2)}) %collective-permute-start.2) | collective-permute-done | bytes 798752 | tf_op jit(solution)/shard_map/ppermute | solution.py:683
  37.2 16.0 %collective-permute-done = bf16[256,1536]{1,0:T(8,128)(2,1)S(1)} collective-permute-done((bf16[256,1536]{1,0:T(8,128)(2,1)S(1)}, bf16[256,1536]{1,0:T(8,128)(2,1)S(1)}, u32[]{:S(2)}, u32[]{:S(2)}) %collective-permute-start) | collective-permute-done | bytes 786464 | tf_op jit(solution)/shard_map/ppermute | solution.py:816
  56.7 13.9 %collective-permute-done.6.refs_3_ = bf16[208,1920]{1,0:T(8,128)(2,1)} collective-permute-done((bf16[208,1920]{1,0:T(8,128)(2,1)}, bf16[208,1920]{1,0:T(8,128)(2,1)}, u32[]{:S(2)}, u32[]{:S(2)}) %collective-permute-start.6) | collective-permute-done | bytes 798752 | tf_op jit(solution)/shard_map/ppermute | solution.py:683
  76.3 11.5 %collective-permute-done.1 = bf16[256,1536]{1,0:T(8,128)(2,1)S(1)} collective-permute-done((bf16[256,1536]{1,0:T(8,128)(2,1)}, bf16[256,1536]{1,0:T(8,128)(2,1)S(1)}, u32[]{:S(2)}, u32[]{:S(2)}) %collective-permute-start.1) | collective-permute-done | bytes 786464 | tf_op jit(solution)/shard_map/ppermute | solution.py:816
  92.4 13.6 %collective-permute-done.8.refs_4_ = bf16[208,1920]{1,0:T(8,128)(2,1)} collective-permute-done((bf16[208,1920]{1,0:T(8,128)(2,1)}, bf16[208,1920]{1,0:T(8,128)(2,1)}, u32[]{:S(2)}, u32[]{:S(2)}) %collective-permute-start.8) | collective-permute-done | bytes 798752 | tf_op jit(solution)/shard_map/ppermute | solution.py:683
  113.5 10.9 %project.2 = (bf16[1024,1152]{1,0:T(8,128)(2,1)}, f32[1024,384]{1,0:T(8,128)S(1)}, f32[3,8,1024]{2,1,0:T(8,128)S(1)}) custom-call(s32[2]{0:T(128)S(1)} %pad_add_fusion.half, bf16[512,1536]{1,0:T(8,128)(2,1)S(1)} %fusion.4.refs_0_, bf16[512,1536]{1,0:T(8,128)(2,1)} %collective-permute-done.9.refs_1_.refs_2_.refs_5_, bf16[1536,1920]{1,0:T(8,128)(2,1)} %copy-done.13, ...), custom_call_target="tpu_custom_call" | custom-call | flops 7247757312 | bytes 13148256 | tf_op jit(solution)/shard_map/project/pallas_call | solution.py:369
  125.6 10.9 %project.3 = (bf16[1024,1152]{1,0:T(8,128)(2,1)}, f32[1024,384]{1,0:T(8,128)S(1)}, f32[3,8,1024]{2,1,0:T(8,128)S(1)}) custom-call(s32[2]{0:T(128)S(1)} %pad_add_fusion.half, bf16[512,1536]{1,0:T(8,128)(2,1)} %constant_dynamic-update-slice_fusion.refs_0_.refs_4_.refs_10_, bf16[512,1536]{1,0:T(8,128)(2,1)} %collective-permute-done.10.refs_1_.refs_6_.refs_15_, ...), custom_call_target="tpu_custom_call" | custom-call | flops 7247757312 | bytes 13148256 | tf_op jit(solution)/shard_map/project/pallas_call | solution.py:369
  139.0 14.0 %attend.2 = (f32[1024,384]{1,0:T(8,128)S(1)}, f32[3,8,1024]{2,1,0:T(8,128)S(1)}) custom-call(s32[1]{0:T(128)} %get-tuple-element.303.start, s32[1]{0:T(128)} %get-tuple-element.298.size, bf16[1024,1152]{1,0:T(8,128)(2,1)S(1)} %copy-done.26, bf16[1024,1152]{1,0:T(8,128)(2,1)S(1)} %copy-done.26, bf16[1024,1152]{1,0:T(8,128)(2,1)S(1)} %copy-done.26, ...), custom_call_target="tpu_custom_call" | custom-call | flops 10066329600 | bytes 3932160 | tf_op jit(solution)/shard_map/attend/pallas_call | solution.py:264
  166.6 14.3 %attend.3 = (f32[1024,384]{1,0:T(8,128)S(1)}, f32[3,8,1024]{2,1,0:T(8,128)S(1)}) custom-call(s32[1]{0:T(128)} %get-tuple-element.302.start, s32[1]{0:T(128)} %get-tuple-element.299.size, bf16[1024,1152]{1,0:T(8,128)(2,1)S(1)} %copy-done.28, bf16[1024,1152]{1,0:T(8,128)(2,1)S(1)} %copy-done.28, bf16[1024,1152]{1,0:T(8,128)(2,1)S(1)} %copy-done.28, ...), custom_call_target="tpu_custom_call" | custom-call | flops 10066329600 | bytes 3932160 | tf_op jit(solution)/shard_map/attend/pallas_call | solution.py:264
  187.1 14.7 %collective-permute-done.12 = bf16[512,1536]{1,0:T(8,128)(2,1)S(1)} collective-permute-done((bf16[512,1536]{1,0:T(8,128)(2,1)S(1)}, bf16[512,1536]{1,0:T(8,128)(2,1)S(1)}, u32[]{:S(2)}, u32[]{:S(2)}) %collective-permute-start.12) | collective-permute-done | bytes 1572896 | tf_op jit(solution)/shard_map/ppermute | solution.py:816
  218.8 36.0 %feed.2 = (bf16[1024,1024]{1,0:T(8,128)(2,1)}, bf16[1024,2048]{1,0:T(8,128)(2,1)}, bf16[512,1536]{1,0:T(8,128)(2,1)S(1)}, bf16[512,1536]{1,0:T(8,128)(2,1)S(1)}) custom-call(s32[2]{0:T(128)S(1)} %pad_add_fusion.half, bf16[512,1536]{1,0:T(8,128)(2,1)} %multiply_convert_fusion.refs_0_, bf16[512,1536]{1,0:T(8,128)(2,1)} %collective-permute-done.17.refs_1_.refs_2_, ...), custom_call_target="tpu_custom_call" | custom-call | flops 24159191040 | bytes 25165824 | tf_op jit(solution)/shard_map/feed/pallas_call | solution.py:369
  263.1 25.0 %feed.3 = (bf16[1024,1024]{1,0:T(8,128)(2,1)}, bf16[1024,2048]{1,0:T(8,128)(2,1)}, bf16[512,1536]{1,0:T(8,128)(2,1)S(1)}, bf16[512,1536]{1,0:T(8,128)(2,1)S(1)}) custom-call(s32[2]{0:T(128)S(1)} %pad_add_fusion.half, bf16[512,1536]{1,0:T(8,128)(2,1)} %collective-permute-done.16.refs_0_.refs_4_, bf16[512,1536]{1,0:T(8,128)(2,1)} %copy-done.95, ...), custom_call_target="tpu_custom_call" | custom-call | flops 24159191040 | bytes 25165824 | tf_op jit(solution)/shard_map/feed/pallas_call | solution.py:369
  294.6 28.1 %grad_feed.1 = bf16[1536,3072]{1,0:T(8,128)(2,1)} custom-call(s32[2]{0:T(128)S(1)} %pad_add_fusion.half, bf16[512,1536]{1,0:T(8,128)(2,1)} %multiply_convert_fusion.refs_0_, bf16[1024,2048]{1,0:T(8,128)(2,1)} %get-tuple-element.171.refs_1_.refs_3_, bf16[512,1536]{1,0:T(8,128)(2,1)} %collective-permute-done.17.refs_1_.refs_2_, ...), custom_call_target="tpu_custom_call" | custom-call | flops 28991029248 | bytes 28311552 | tf_op jit(solution)/shard_map/grad_feed/pallas_call | solution.py:550
  322.7 7.1 %collective-permute-done.22 = bf16[512,1536]{1,0:T(8,128)(2,1)} collective-permute-done((bf16[512,1536]{1,0:T(8,128)(2,1)}, bf16[512,1536]{1,0:T(8,128)(2,1)}, u32[]{:S(2)}, u32[]{:S(2)}) %collective-permute-start.22) | collective-permute-done | bytes 1572896 | tf_op jit(solution)/shard_map/ppermute | solution.py:816
  341.7 8.4 %feed_out.2 = (bf16[512,1536]{1,0:T(8,128)(2,1)S(1)}, bf16[512,1536]{1,0:T(8,128)(2,1)}) custom-call(s32[2]{0:T(128)S(1)} %pad_add_fusion.half, bf16[1024,1024]{1,0:T(8,128)(2,1)S(1)} %copy-done.25, bf16[1536,3072]{1,0:T(8,128)(2,1)} %all-gather.2.cloned.1.call-done.refs_4_.w_ref), custom_call_target="tpu_custom_call" | custom-call | flops 4831838208 | bytes 14680064 | tf_op jit(solution)/shard_map/feed_out/pallas_call | solution.py:369
  357.1 26.3 %attend_back.2 = (bf16[1024,384]{1,0:T(8,128)(2,1)S(1)}, bf16[1024,384]{1,0:T(8,128)(2,1)S(1)}, bf16[1024,384]{1,0:T(8,128)(2,1)S(1)}, f32[3,8,1024]{2,1,0:T(8,128)S(1)}) custom-call(s32[1]{0:T(128)} %get-tuple-element.302.start, s32[1]{0:T(128)} %get-tuple-element.299.size, bf16[1024,1152]{1,0:T(8,128)(2,1)S(1)} %copy-done.29, ...), custom_call_target="tpu_custom_call" | custom-call | flops 16357785600 | bytes 7864320 | tf_op jit(solution)/shard_map/attend_back/pallas_call | solution.py:288
  390.4 7.0 %feed_out.3 = (bf16[512,1536]{1,0:T(8,128)(2,1)S(1)}, bf16[512,1536]{1,0:T(8,128)(2,1)S(1)}) custom-call(s32[2]{0:T(128)S(1)} %pad_add_fusion.half, bf16[1024,1024]{1,0:T(8,128)(2,1)S(1)} %copy-done.24, bf16[1536,3072]{1,0:T(8,128)(2,1)} %all-gather.2.cloned.1.call-done.refs_4_.w_ref), custom_call_target="tpu_custom_call" | custom-call | flops 4831838208 | bytes 14680064 | tf_op jit(solution)/shard_map/feed_out/pallas_call | solution.py:369
  402.7 10.9 %grad_gate_out.1 = bf16[1536,768]{1,0:T(8,128)(2,1)} custom-call(s32[2]{0:T(128)S(1)} %pad_add_fusion.half, bf16[512,1536]{1,0:T(8,128)(2,1)} %copy-done, bf16[1024,384]{1,0:T(8,128)(2,1)S(1)} %get-tuple-element.188.refs_1_.refs_3_, bf16[512,1536]{1,0:T(8,128)(2,1)} %collective-permute-done.9.refs_1_.refs_2_.refs_5_, ...), custom_call_target="tpu_custom_call" | custom-call | flops 7247757312 | bytes 7077888 | tf_op jit(solution)/shard_map/grad_gate_out/pallas_call | solution.py:550
  418.2 7.2 %collective-permute-start.27 = (bf16[192,768]{1,0:T(8,128)(2,1)S(1)}, bf16[192,768]{1,0:T(8,128)(2,1)S(1)}, u32[]{:S(2)}, u32[]{:S(2)}) collective-permute-start(bf16[192,768]{1,0:T(8,128)(2,1)S(1)} %get-tuple-element.278), channel_id=1, source_target_pairs={{0,8},{8,16},{16,24},{24,28},{28,20},{20,12},{12,4},{4,0},{1,9},{9... | collective-permute-start | bytes 884744 | tf_op jit(solution)/shard_map/ppermute | solution.py:683
  431.5 25.9 %attend_back.3 = (bf16[1024,384]{1,0:T(8,128)(2,1)S(1)}, bf16[1024,384]{1,0:T(8,128)(2,1)S(1)}, bf16[1024,384]{1,0:T(8,128)(2,1)S(1)}, f32[3,8,1024]{2,1,0:T(8,128)S(1)}) custom-call(s32[1]{0:T(128)} %get-tuple-element.303.start, s32[1]{0:T(128)} %get-tuple-element.298.size, bf16[1024,1152]{1,0:T(8,128)(2,1)S(1)} %copy-done.27, ...), custom_call_target="tpu_custom_call" | custom-call | flops 16357785600 | bytes 7864320 | tf_op jit(solution)/shard_map/attend_back/pallas_call | solution.py:288
  457.5 11.9 %project_back.2 = (bf16[512,1536]{1,0:T(8,128)(2,1)S(1)}, bf16[512,1536]{1,0:T(8,128)(2,1)}) custom-call(s32[2]{0:T(128)S(1)} %pad_add_fusion.half, bf16[1024,384]{1,0:T(8,128)(2,1)S(1)} %get-tuple-element.198.refs_0_.refs_11_.refs_16_, bf16[1024,384]{1,0:T(8,128)(2,1)S(1)} %get-tuple-element.199.refs_1_.refs_12_.refs_17_, ...), custom_call_target="tpu_custom_call" | custom-call | flops 7247757312 | bytes 12361728 | tf_op jit(solution)/shard_map/project_back/pallas_call | solution.py:369
  480.1 15.0 %project_grads.1 = bf16[8,208,1152]{2,1,0:T(8,128)(2,1)} custom-call(s32[2]{0:T(128)S(1)} %pad_add_fusion.half, bf16[512,1536]{1,0:T(8,128)(2,1)} %copy-done, bf16[1024,384]{1,0:T(8,128)(2,1)S(1)} %copy-done.31, bf16[1024,384]{1,0:T(8,128)(2,1)S(1)} %copy-done.33, bf16[1024,384]{1,0:T(8,128)(2,1)S(1)} %copy-done.35, ...), custom_call_target="tpu_custom_call" | custom-call | flops 10871635968 | bytes 10616832 | tf_op jit(solution)/shard_map/project_grads/pallas_call | solution.py:614
  512.8 10.7 %project_back.3 = (bf16[512,1536]{1,0:T(8,128)(2,1)S(1)}, bf16[512,1536]{1,0:T(8,128)(2,1)}) custom-call(s32[2]{0:T(128)S(1)} %pad_add_fusion.half, bf16[1024,384]{1,0:T(8,128)(2,1)S(1)} %copy-done.31, bf16[1024,384]{1,0:T(8,128)(2,1)S(1)} %copy-done.33, bf16[1024,384]{1,0:T(8,128)(2,1)S(1)} %copy-done.35, ...), custom_call_target="tpu_custom_call" | custom-call | flops 7247757312 | bytes 12361728 | tf_op jit(solution)/shard_map/project_back/pallas_call | solution.py:369
  536.0 7.3 %collective-permute-done.42 = bf16[208,1152]{1,0:T(8,128)(2,1)S(1)} collective-permute-done((bf16[208,1152]{1,0:T(8,128)(2,1)S(1)}, bf16[208,1152]{1,0:T(8,128)(2,1)S(1)}, u32[]{:S(2)}, u32[]{:S(2)}) %collective-permute-start.42) | collective-permute-done | bytes 479264 | tf_op jit(solution)/shard_map/ppermute | solution.py:683
  (383 shorter events, 244.5 us)
Async XLA Ops:
  7.2 211.6 %all-gather.2.cloned.1.call-start = ((), (), s32[]{:S(2)}) async-start(), calls=%async_computation.1 | async-start | bytes 10616832 | tf_op jit(solution)/shard_map/all_gather | solution.py:904
  10.4 20.9 %collective-permute-start.2 = (bf16[208,1920]{1,0:T(8,128)(2,1)S(1)}, bf16[208,1920]{1,0:T(8,128)(2,1)S(1)}, u32[]{:S(2)}, u32[]{:S(2)}) collective-permute-start(bf16[208,1920]{1,0:T(8,128)(2,1)S(1)} %fusion.23.refs_0_), channel_id=1, source_target_pairs={{0,4},{8,0},{16,8},{24,16},{28,24},{20,28},{12,20},{4,12},{1,5},{9... | collective-permute-start | bytes 2396168 | tf_op jit(solution)/shard_map/ppermute | solution.py:683
  13.4 19.3 %collective-permute-start.3 = (bf16[208,1920]{1,0:T(8,128)(2,1)S(1)}, bf16[208,1920]{1,0:T(8,128)(2,1)S(1)}, u32[]{:S(2)}, u32[]{:S(2)}) collective-permute-start(bf16[208,1920]{1,0:T(8,128)(2,1)S(1)} %fusion.23.refs_0_), channel_id=1, source_target_pairs={{0,8},{8,16},{16,24},{24,28},{28,20},{20,12},{12,4},{4,0},{1,9},{9... | collective-permute-start | bytes 2396168 | tf_op jit(solution)/shard_map/ppermute | solution.py:683
  32.7 20.5 %collective-permute-start.4 = (bf16[208,1920]{1,0:T(8,128)(2,1)S(1)}, bf16[208,1920]{1,0:T(8,128)(2,1)}, u32[]{:S(2)}, u32[]{:S(2)}) collective-permute-start(bf16[208,1920]{1,0:T(8,128)(2,1)S(1)} %collective-permute-done.2.refs_1_), channel_id=1, source_target_pairs={{0,4},{8,0},{16,8},{24,16},{28,24},{20,28},{12,20},{4,12},{1,5},{9... | collective-permute-start | bytes 2396168 | tf_op jit(solution)/shard_map/ppermute | solution.py:683
  34.3 19.0 %collective-permute-start.5 = (bf16[208,1920]{1,0:T(8,128)(2,1)S(1)}, bf16[208,1920]{1,0:T(8,128)(2,1)}, u32[]{:S(2)}, u32[]{:S(2)}) collective-permute-start(bf16[208,1920]{1,0:T(8,128)(2,1)S(1)} %collective-permute-done.3.refs_7_), channel_id=1, source_target_pairs={{0,8},{8,16},{16,24},{24,28},{28,20},{20,12},{12,4},{4,0},{1,9},{9... | collective-permute-start | bytes 2396168 | tf_op jit(solution)/shard_map/ppermute | solution.py:683
  71.9 481.4 %reduce-scatter.2.cloned.1.call-start = ((), (), s32[]{:S(2)}) async-start(), calls=%async_computation.2 | async-start | bytes 10616832 | tf_op jit(solution)/shard_map/reduce_scatter | solution.py:956
  73.6 39.9 %collective-permute-start.9 = (bf16[512,1536]{1,0:T(8,128)(2,1)S(1)}, bf16[512,1536]{1,0:T(8,128)(2,1)}, u32[]{:S(2)}, u32[]{:S(2)}) collective-permute-start(bf16[512,1536]{1,0:T(8,128)(2,1)S(1)} %fusion.4.refs_0_), channel_id=1, source_target_pairs={{0,1},{1,0},{2,3},{3,2},{4,5},{5,4},{6,7},{7,6},{8,9},{9,8},{10,11... | collective-permute-start | bytes 4718600 | tf_op jit(solution)/shard_map/ppermute | solution.py:816
  73.6 32.4 %collective-permute-start.8 = (bf16[208,1920]{1,0:T(8,128)(2,1)}, bf16[208,1920]{1,0:T(8,128)(2,1)}, u32[]{:S(2)}, u32[]{:S(2)}) collective-permute-start(bf16[208,1920]{1,0:T(8,128)(2,1)} %collective-permute-done.7.refs_5_), channel_id=1, source_target_pairs={{0,8},{8,16},{16,24},{24,28},{28,20},{20,12},{12,4},{4,0},{1,9},{9... | collective-permute-start | bytes 2396168 | tf_op jit(solution)/shard_map/ppermute | solution.py:683
  88.7 36.8 %collective-permute-start.10 = (bf16[512,1536]{1,0:T(8,128)(2,1)}, bf16[512,1536]{1,0:T(8,128)(2,1)}, u32[]{:S(2)}, u32[]{:S(2)}) collective-permute-start(bf16[512,1536]{1,0:T(8,128)(2,1)} %constant_dynamic-update-slice_fusion.refs_0_.refs_4_.refs_10_), channel_id=1, source_target_pairs={{0,1},{1,0},{2,3},{3,2},{4,5},{5,4},{6,7},{7,6},{8,9},{9,8},{10,11... | collective-permute-start | bytes 4718600 | tf_op jit(solution)/shard_map/ppermute | solution.py:816
  90.9 69.2 %collective-permute-start.13 = (bf16[512,1536]{1,0:T(8,128)(2,1)}, bf16[512,1536]{1,0:T(8,128)(2,1)}, u32[]{:S(2)}, u32[]{:S(2)}) collective-permute-start(bf16[512,1536]{1,0:T(8,128)(2,1)} %refs_8_), channel_id=1, source_target_pairs={{0,2},{1,3},{2,0},{3,1},{4,6},{5,7},{6,4},{7,5},{8,10},{9,11},{10,... | collective-permute-start | bytes 4718600 | tf_op jit(solution)/shard_map/ppermute | solution.py:816
  165.3 36.5 %collective-permute-start.12 = (bf16[512,1536]{1,0:T(8,128)(2,1)S(1)}, bf16[512,1536]{1,0:T(8,128)(2,1)S(1)}, u32[]{:S(2)}, u32[]{:S(2)}) collective-permute-start(bf16[512,1536]{1,0:T(8,128)(2,1)S(1)} %add_convert_fusion.3), channel_id=1, source_target_pairs={{0,2},{1,3},{2,0},{3,1},{4,6},{5,7},{6,4},{7,5},{8,10},{9,11},{10,... | collective-permute-start | bytes 4718600 | tf_op jit(solution)/shard_map/ppermute | solution.py:816
  212.0 42.8 %collective-permute-start.16 = (bf16[512,1536]{1,0:T(8,128)(2,1)}, bf16[512,1536]{1,0:T(8,128)(2,1)}, u32[]{:S(2)}, u32[]{:S(2)}) collective-permute-start(bf16[512,1536]{1,0:T(8,128)(2,1)} %multiply_convert_fusion.refs_0_), channel_id=1, source_target_pairs={{0,2},{1,3},{2,0},{3,1},{4,6},{5,7},{6,4},{7,5},{8,10},{9,11},{10,... | collective-permute-start | bytes 4718600 | tf_op jit(solution)/shard_map/ppermute | solution.py:816
  293.1 36.8 %collective-permute-start.22 = (bf16[512,1536]{1,0:T(8,128)(2,1)}, bf16[512,1536]{1,0:T(8,128)(2,1)}, u32[]{:S(2)}, u32[]{:S(2)}) collective-permute-start(bf16[512,1536]{1,0:T(8,128)(2,1)} %add_convert_fusion.2), channel_id=1, source_target_pairs={{0,2},{1,3},{2,0},{3,1},{4,6},{5,7},{6,4},{7,5},{8,10},{9,11},{10,... | collective-permute-start | bytes 4718600 | tf_op jit(solution)/shard_map/ppermute | solution.py:816
  340.2 45.8 %collective-permute-start.24 = (bf16[512,1536]{1,0:T(8,128)(2,1)S(1)}, bf16[512,1536]{1,0:T(8,128)(2,1)S(1)}, u32[]{:S(2)}, u32[]{:S(2)}) collective-permute-start(bf16[512,1536]{1,0:T(8,128)(2,1)S(1)} %get-tuple-element.178.refs_0_.refs_8_), channel_id=1, source_target_pairs={{0,2},{1,3},{2,0},{3,1},{4,6},{5,7},{6,4},{7,5},{8,10},{9,11},{10,... | collective-permute-start | bytes 4718600 | tf_op jit(solution)/shard_map/ppermute | solution.py:816
  389.4 24.2 %collective-permute-start.26 = (bf16[512,1536]{1,0:T(8,128)(2,1)}, bf16[512,1536]{1,0:T(8,128)(2,1)}, u32[]{:S(2)}, u32[]{:S(2)}) collective-permute-start(bf16[512,1536]{1,0:T(8,128)(2,1)} %get-tuple-element.195), channel_id=1, source_target_pairs={{0,1},{1,0},{2,3},{3,2},{4,5},{5,4},{6,7},{7,6},{8,9},{9,8},{10,11... | collective-permute-start | bytes 4718600 | tf_op jit(solution)/shard_map/ppermute | solution.py:816
  415.6 41.8 %collective-permute-start.29 = (bf16[512,1536]{1,0:T(8,128)(2,1)S(1)}, bf16[512,1536]{1,0:T(8,128)(2,1)S(1)}, u32[]{:S(2)}, u32[]{:S(2)}) collective-permute-start(bf16[512,1536]{1,0:T(8,128)(2,1)S(1)} %add_convert_fusion.1), channel_id=1, source_target_pairs={{0,2},{1,3},{2,0},{3,1},{4,6},{5,7},{6,4},{7,5},{8,10},{9,11},{10,... | collective-permute-start | bytes 4718600 | tf_op jit(solution)/shard_map/ppermute | solution.py:816
  418.2 39.2 %collective-permute-start.27 = (bf16[192,768]{1,0:T(8,128)(2,1)S(1)}, bf16[192,768]{1,0:T(8,128)(2,1)S(1)}, u32[]{:S(2)}, u32[]{:S(2)}) collective-permute-start(bf16[192,768]{1,0:T(8,128)(2,1)S(1)} %get-tuple-element.278), channel_id=1, source_target_pairs={{0,8},{8,16},{16,24},{24,28},{28,20},{20,12},{12,4},{4,0},{1,9},{9... | collective-permute-start | bytes 884744 | tf_op jit(solution)/shard_map/ppermute | solution.py:683
  425.4 32.0 %collective-permute-start.28 = (bf16[192,768]{1,0:T(8,128)(2,1)S(1)}, bf16[192,768]{1,0:T(8,128)(2,1)S(1)}, u32[]{:S(2)}, u32[]{:S(2)}) collective-permute-start(bf16[192,768]{1,0:T(8,128)(2,1)S(1)} %get-tuple-element.277), channel_id=1, source_target_pairs={{0,4},{8,0},{16,8},{24,16},{28,24},{20,28},{12,20},{4,12},{1,5},{9... | collective-permute-start | bytes 884744 | tf_op jit(solution)/shard_map/ppermute | solution.py:683
  472.5 22.7 %collective-permute-start.32 = (bf16[192,768]{1,0:T(8,128)(2,1)S(1)}, bf16[192,768]{1,0:T(8,128)(2,1)S(1)}, u32[]{:S(2)}, u32[]{:S(2)}) collective-permute-start(bf16[192,768]{1,0:T(8,128)(2,1)S(1)} %get-tuple-element.276), channel_id=1, source_target_pairs={{0,8},{8,16},{16,24},{24,28},{28,20},{20,12},{12,4},{4,0},{1,9},{9... | collective-permute-start | bytes 884744 | tf_op jit(solution)/shard_map/ppermute | solution.py:683
  472.5 24.2 %collective-permute-start.33 = (bf16[192,768]{1,0:T(8,128)(2,1)S(1)}, bf16[192,768]{1,0:T(8,128)(2,1)S(1)}, u32[]{:S(2)}, u32[]{:S(2)}) collective-permute-start(bf16[192,768]{1,0:T(8,128)(2,1)S(1)} %get-tuple-element.275), channel_id=1, source_target_pairs={{0,4},{8,0},{16,8},{24,16},{28,24},{20,28},{12,20},{4,12},{1,5},{9... | collective-permute-start | bytes 884744 | tf_op jit(solution)/shard_map/ppermute | solution.py:683
  478.3 19.7 %collective-permute-start.31 = (bf16[256,1536]{1,0:T(8,128)(2,1)S(1)}, bf16[256,1536]{1,0:T(8,128)(2,1)S(1)}, u32[]{:S(2)}, u32[]{:S(2)}) collective-permute-start(bf16[256,1536]{1,0:T(8,128)(2,1)S(1)} %get-tuple-element.280), channel_id=1, source_target_pairs={{0,2},{1,3},{2,0},{3,1},{4,6},{5,7},{6,4},{7,5},{8,10},{9,11},{10,... | collective-permute-start | bytes 2359304 | tf_op jit(solution)/shard_map/ppermute | solution.py:816
  501.5 30.5 %collective-permute-start.34 = (bf16[512,1536]{1,0:T(8,128)(2,1)S(1)}, bf16[512,1536]{1,0:T(8,128)(2,1)}, u32[]{:S(2)}, u32[]{:S(2)}) collective-permute-start(bf16[512,1536]{1,0:T(8,128)(2,1)S(1)} %copy-done.17), channel_id=1, source_target_pairs={{0,1},{1,0},{2,3},{3,2},{4,5},{5,4},{6,7},{7,6},{8,9},{9,8},{10,11... | collective-permute-start | bytes 4718600 | tf_op jit(solution)/shard_map/ppermute | solution.py:816
  504.1 22.9 %collective-permute-start.35 = (bf16[256,1536]{1,0:T(8,128)(2,1)S(1)}, bf16[256,1536]{1,0:T(8,128)(2,1)S(1)}, u32[]{:S(2)}, u32[]{:S(2)}) collective-permute-start(bf16[256,1536]{1,0:T(8,128)(2,1)S(1)} %get-tuple-element.216), channel_id=1, source_target_pairs={{0,2},{1,3},{2,0},{3,1},{4,6},{5,7},{6,4},{7,5},{8,10},{9,11},{10,... | collective-permute-start | bytes 2359304 | tf_op jit(solution)/shard_map/ppermute | solution.py:816
  526.9 23.0 %collective-permute-start.36 = (bf16[512,1536]{1,0:T(8,128)(2,1)}, bf16[512,1536]{1,0:T(8,128)(2,1)}, u32[]{:S(2)}, u32[]{:S(2)}) collective-permute-start(bf16[512,1536]{1,0:T(8,128)(2,1)} %get-tuple-element.218), channel_id=1, source_target_pairs={{0,1},{1,0},{2,3},{3,2},{4,5},{5,4},{6,7},{7,6},{8,9},{9,8},{10,11... | collective-permute-start | bytes 4718600 | tf_op jit(solution)/shard_map/ppermute | solution.py:816
  (126 other events, 1244.5 us)
Sparse Core Ops, SparseCore 0:
  72.0 146.7 all-gather.1
  330.0 178.3 reduce-scatter.1

commit v5 on v4

--- a/solution.py
+++ b/solution.py
@@ -72,51 +72,40 @@
     if lse_ref.shape[0] > hb:
         lse_ref[...] = jnp.zeros(lse_ref.shape, F32)
 
-    def stack(rows):
-        return jnp.concatenate([jnp.broadcast_to(r, (PIECE, r.shape[1])) for r in rows], axis=0)
-
-    causal = jnp.concatenate([causal] * hb, axis=0)
-    heads = range(hb)
-    spans_of = [slice(h * PIECE, (h + 1) * PIECE) for h in heads]
-
     def block(i, wide):
         lo, hi = i * PIECE, (i + 1) * PIECE
         in_pic = (lo >= first) & (lo < first + extent)
-        q_all = q_ref[lo:hi, :]
-        q = jnp.concatenate([jnp.where(m, q_all, jnp.zeros((), LOW)) for m in mine], axis=0)
-        c_row = [c_rows[h:h + 1, :] for h in heads]
-        base = [c_row[h][:, lo:lo + 1] for h in heads]
-        back = jnp.concatenate([base[h] - 2.0 * c_cols[lo:hi, h:h + 1] for h in heads], axis=0)
-        parts, spans = [], []
-        if i:
-            parts.append(mm(q, k_ref[0:lo, :], NT) + stack([base[h] - c_row[h][:, :lo] for h in heads]))
-            spans.append((0, lo))
-        ahead = stack([base[h] - c_row[h][:, lo:hi] for h in heads])
-        other = jnp.where(in_pic, back + stack([c_row[h][:, lo:hi] for h in heads]), HIDE)
-        parts.append(mm(q, k_ref[lo:hi, :], NT) + jnp.where(causal, ahead, other))
-        spans.append((lo, hi))
-        if wide:
-            more = stack([c_row[h][:, hi:hi + PIECE] for h in heads])
-            parts.append(mm(q, k_ref[hi:hi + PIECE, :], NT) + (back + more))
-            spans.append((hi, hi + PIECE))
-        peak = functools.reduce(jnp.maximum, [jnp.max(p, axis=1, keepdims=True) for p in parts])
-        acc = [None] * hb
-        for p, (a, b) in zip(parts, spans):
-            p = jnp.exp2(p - peak).astype(LOW)
-            for h in heads:
+        out, lse = None, None
+        for h in range(hb):
+            q = jnp.where(mine[h], q_ref[lo:hi, :], jnp.zeros((), LOW))
+            c_row = c_rows[h:h + 1, :]
+            c_col = c_cols[lo:hi, h:h + 1]
+            base = c_row[:, lo:lo + 1]
+            parts, spans = [], []
+            if i:
+                parts.append(mm(q, k_ref[0:lo, :], NT) + (base - c_row[:, :lo]))
+                spans.append((0, lo))
+            back = base - 2.0 * c_col
+            other = jnp.where(in_pic, back + c_row[:, lo:hi], HIDE)
+            parts.append(mm(q, k_ref[lo:hi, :], NT) + jnp.where(causal, base - c_row[:, lo:hi], other))
+            spans.append((lo, hi))
+            if wide:
+                parts.append(mm(q, k_ref[hi:hi + PIECE, :], NT) + (back + c_row[:, hi:hi + PIECE]))
+                spans.append((hi, hi + PIECE))
+            peak = functools.reduce(jnp.maximum, [jnp.max(p, axis=1, keepdims=True) for p in parts])
+            acc = None
+            for p, (a, b) in zip(parts, spans):
                 v = jnp.where(mine[h], v_ref[a:b, :], jnp.ones((), LOW))
-                t = mm(p[spans_of[h]], v)
-                acc[h] = t if acc[h] is None else acc[h] + t
-        out, lse = None, None
-        for h in heads:
-            total = acc[h][:, spare[h]:spare[h] + 1]
-            o_h = acc[h] / total
-            l_h = jnp.broadcast_to(peak[spans_of[h]] + jnp.log2(total), o_h.shape)
+                t = mm(jnp.exp2(p - peak).astype(LOW), v)
+                acc = t if acc is None else acc + t
+            total = acc[:, spare[h]:spare[h] + 1]
+            o_h = acc / total
+            l_h = jnp.broadcast_to(peak + jnp.log2(total), o_h.shape)
             out = o_h if out is None else jnp.where(mine[h], o_h, out)
             lse = l_h if lse is None else jnp.where(mine[h], l_h, lse)
         o_ref[lo:hi, :] = out
         turned = lse.T
-        for h in heads:
+        for h in range(hb):
             lse_ref[h:h + 1, lo:hi] = turned[h * HEAD_DIM:h * HEAD_DIM + 1, :]
 
     for i in range(count):
@@ -624,6 +613,58 @@
     )(pc.half, *ins)
 
 
+def norm_grads(backs, own, values, gain, base, low):
+    rows, dims = values.shape
+    block = rows // 4
+    per = rows // len(backs) // block
+    n, m = len(backs), len(own)
+
+    def kernel(*refs):
+        i = pl.program_id(0)
+        values_ref, gain_ref, base_ref = refs[n + m:n + m + 3]
+        outs = refs[n + m + 3:]
+        g = refs[0][...]
+        for p in range(1, n):
+            g = jnp.where(i >= p * per, refs[p][...], g)
+        g = g.astype(F32)
+        for r in refs[n:n + m]:
+            g = g + r[...].astype(F32)
+        v = values_ref[...].astype(F32)
+        s = lax.rsqrt(jnp.mean(v * v, axis=1, keepdims=True) + 1e-05)
+        normed = v * s
+        scaled = g * gain_ref[...]
+        total = base_ref[...].astype(F32) + s * (scaled - normed * jnp.mean(scaled * normed, axis=1, keepdims=True))
+        outs[0][...] = total
+        if low:
+            outs[1][...] = total.astype(LOW)
+        part = jnp.sum(g * normed, axis=0, keepdims=True)
+
+        def start():
+            outs[-1][...] = part
+
+        def more():
+            outs[-1][...] += part
+
+        pl.when(i == 0)(start)
+        pl.when(i > 0)(more)
+
+    wide = pl.BlockSpec((block, dims), lambda i: (i, 0))
+    row = pl.BlockSpec((1, dims), lambda i: (0, 0))
+    parts = [pl.BlockSpec((block, dims), lambda i, p=p: (jnp.clip(i - p * per, 0, per - 1), 0)) for p in range(n)]
+    return pl.pallas_call(
+        kernel,
+        grid=(4,),
+        in_specs=parts + [wide] * (m + 1) + [row, wide],
+        out_specs=[wide] * (2 if low else 1) + [row],
+        out_shape=[jax.ShapeDtypeStruct((rows, dims), F32)]
+        + ([jax.ShapeDtypeStruct((rows, dims), LOW)] if low else [])
+        + [jax.ShapeDtypeStruct((1, dims), F32)],
+        compiler_params=pltpu.CompilerParams(vmem_limit_bytes=32 * 2**20),
+        cost_estimate=cost(0, rows * dims * 20),
+        name="norm_grads",
+    )(*backs, *own, values, gain.reshape(1, dims), base)
+
+
 from jax.sharding import PartitionSpec as P
 
 NORM_EPS = 1e-05
@@ -637,13 +678,6 @@
 
 def rms_scale(values):
     return lax.rsqrt(jnp.mean(values * values, axis=-1, keepdims=True) + NORM_EPS)
-
-
-def norm_back(gradient, values, inv_scale, gain_row):
-    normed = values * inv_scale
-    scaled = gradient * gain_row
-    backward = inv_scale * (scaled - normed * jnp.mean(scaled * normed, axis=-1, keepdims=True))
-    return (backward, jnp.sum(gradient * normed, axis=0))
 
 
 def adam_step(weight, gradient, first_old, second_old, clip_scale, decay_rate, width):
@@ -954,10 +988,9 @@
         grad_feed = weight_grads(pc, groups, "grad_feed", 256)
         done(grad_feed)
         shard_feed = lax.psum_scatter(after(grad_feed, back[0]), "dp", scatter_dimension=0, tiled=True)
-        grad_two = spread_sum([after(back[0], grad_feed)], own)
-        grad_middle, gain_two_grad = norm_back(grad_two, middle, scale_two, feed_gain)
-        grad_middle = grad_middle + cotangent.astype(F32)
-        grad_low = grad_middle.astype(LOW)
+        grad_middle, grad_low, gain_two_grad = norm_grads(
+            [after(back[0], grad_feed)], own, middle, feed_gain, cotangent, True
+        )
         done(grad_low)
         move_back = rows_start(grad_low)
         out_parts = [None] * chunks
@@ -1028,9 +1061,7 @@
             shard_feed = shard_feed.astype(F32)
             square_feed = jnp.sum(shard_feed * shard_feed)
         shard_up, shard_down = shard_feed[:, :2 * hidden_size], shard_feed[:, 2 * hidden_size:]
-        grad_one = spread_sum(back, own)
-        grad_inputs, gain_one_grad = norm_back(grad_one, inputs_f, scale_one, attn_gain)
-        input_grad = grad_inputs + grad_middle
+        input_grad, gain_one_grad = norm_grads(back, own, inputs, attn_gain, grad_middle, False)
         while ring_go.k < dp // 2:
             ring_go.step()
         shard_go = ring_go.all()
@@ -1043,7 +1074,7 @@
         bias_full = jnp.where(jnp.arange(tn)[:, None] == rank, bias_local_grad[None], 0.0).reshape(-1)
         square = square_feed + square_go + sum(jnp.sum(s * s) for s in (shard_qkv, shard_forget))
         pad = 128 - forget_bias.shape[0] - 1
-        packed = jnp.concatenate([gain_one_grad, gain_two_grad, bias_full, square[None], jnp.zeros((pad,), F32)])
+        packed = jnp.concatenate([gain_one_grad[0], gain_two_grad[0], bias_full, square[None], jnp.zeros((pad,), F32)])
         packed = sum_all(sum_all(packed.reshape(-1, 128), "tensor", tn), "dp", dp).reshape(-1)
         gain_one_sum, gain_two_sum = packed[:dims], packed[dims:2 * dims]
         bias_sum = packed[2 * dims:2 * dims + forget_bias.shape[0]]

time: 634 us -> 628 us (level)
  other arithmetic: 76.8 us -> 51.5 us
  local copies, waits for them, and re-layouts: 35.9 us -> 50.9 us
  Pallas kernels: 279 us -> 286 us
    unnamed x193 -> x213, local copies, waits for them, and re-layouts: 22 us -> 37.2 us
    pallas_call x12, Pallas kernels: 141 us -> 129 us  [call(): pl.pallas_call(kernel, grid_spec=pltpu.PrefetchScalarGridSpec(num_scalar_...]
    pallas_call x0 -> x2, Pallas kernels: none -> 9.89 us  [norm_grads(): pl.pallas_call(kernel, grid=(4,), in_specs=parts + [wide] * (m + 1) + [ro...]
    reduce_sum x2 -> x0, other arithmetic: 8.13 us -> none  [norm_back(): return (backward, jnp.sum(gradient * normed, axis=0))]
  transfers between devices with their start and end apart: 54 -> 54, of which waited for: 29 -> 27; matrix products, arithmetic and copies ran while one was open for 11% -> 7% of each run, Pallas kernels for 40% -> 42%
where the time goes in v5:
time: 628 us; the launch traced here: 624 us
  Pallas kernels  286 us (46%)
  waiting for transfers between devices  156 us (25%)
  starting transfers between devices  57.1 us (9%)
  other arithmetic  51.5 us (8%)
  local copies, waits for them, and re-layouts  50.9 us (8%)
  between operations  22.1 us (4%)
    pallas_call x12, Pallas kernels, call(): pl.pallas_call(kernel, grid_spec=pltpu.PrefetchScalarGridSpec(num_scalar_...  129 us
    ppermute x26, waiting for transfers between devices, swap(): return lax.ppermute(x, 'tensor', [(i, i ^ bit) for i in range(tn)])  72.4 us
    ppermute x21, waiting for transfers between devices, step(): lax.ppermute(x, self.axis, [(self.table[r], self.table[(r + way) % n]) fo...  68.4 us
    pallas_call x2, Pallas kernels, attend_back(): pl.pallas_call(functools.partial(attn_bwd_kernel, hb=hb), grid_spec=pltpu...  55.1 us
    ppermute x21, starting transfers between devices, step(): lax.ppermute(x, self.axis, [(self.table[r], self.table[(r + way) % n]) fo...  40.3 us
    pallas_call x2, Pallas kernels, weight_grads(): pl.pallas_call(kernel, grid_spec=pltpu.PrefetchScalarGridSpec(num_scalar_...  39.1 us
    unnamed x213, local copies, waits for them, and re-layouts  37.2 us
    pallas_call x2, Pallas kernels, attend(): pl.pallas_call(functools.partial(attn_fwd_kernel, hb=hb), grid_spec=pltpu...  33.8 us
  transfers between devices with their start and end apart: 54, of which 27 were waited for; matrix products, arithmetic and copies ran while one was open for 7% of the time, Pallas kernels for 42%

profile of v5, /device:TPU:0, one launch (start us, length us, event | category | flops | bytes accessed | tf_op | source)
XLA Modules:
  0.0 623.5 jit_solution(16417482776780666032)
XLA Ops:
  14.4 16.9 %collective-permute-done.2.refs_1_ = bf16[208,1920]{1,0:T(8,128)(2,1)S(1)} collective-permute-done((bf16[208,1920]{1,0:T(8,128)(2,1)S(1)}, bf16[208,1920]{1,0:T(8,128)(2,1)S(1)}, u32[]{:S(2)}, u32[]{:S(2)}) %collective-permute-start.2) | collective-permute-done | bytes 798752 | tf_op jit(solution)/shard_map/ppermute | solution.py:717
  37.2 16.1 %collective-permute-done = bf16[256,1536]{1,0:T(8,128)(2,1)} collective-permute-done((bf16[256,1536]{1,0:T(8,128)(2,1)S(1)}, bf16[256,1536]{1,0:T(8,128)(2,1)}, u32[]{:S(2)}, u32[]{:S(2)}) %collective-permute-start) | collective-permute-done | bytes 786464 | tf_op jit(solution)/shard_map/ppermute | solution.py:850
  56.7 13.8 %collective-permute-done.6.refs_3_ = bf16[208,1920]{1,0:T(8,128)(2,1)} collective-permute-done((bf16[208,1920]{1,0:T(8,128)(2,1)}, bf16[208,1920]{1,0:T(8,128)(2,1)}, u32[]{:S(2)}, u32[]{:S(2)}) %collective-permute-start.6) | collective-permute-done | bytes 798752 | tf_op jit(solution)/shard_map/ppermute | solution.py:717
  76.3 11.4 %collective-permute-done.1 = bf16[256,1536]{1,0:T(8,128)(2,1)S(1)} collective-permute-done((bf16[256,1536]{1,0:T(8,128)(2,1)}, bf16[256,1536]{1,0:T(8,128)(2,1)S(1)}, u32[]{:S(2)}, u32[]{:S(2)}) %collective-permute-start.1) | collective-permute-done | bytes 786464 | tf_op jit(solution)/shard_map/ppermute | solution.py:850
  92.3 13.7 %collective-permute-done.8.refs_4_ = bf16[208,1920]{1,0:T(8,128)(2,1)} collective-permute-done((bf16[208,1920]{1,0:T(8,128)(2,1)}, bf16[208,1920]{1,0:T(8,128)(2,1)}, u32[]{:S(2)}, u32[]{:S(2)}) %collective-permute-start.8) | collective-permute-done | bytes 798752 | tf_op jit(solution)/shard_map/ppermute | solution.py:717
  113.5 11.0 %project.2 = (bf16[1024,1152]{1,0:T(8,128)(2,1)}, f32[1024,384]{1,0:T(8,128)S(1)}, f32[3,8,1024]{2,1,0:T(8,128)S(1)}) custom-call(s32[2]{0:T(128)S(1)} %pad_add_fusion.half, bf16[512,1536]{1,0:T(8,128)(2,1)S(1)} %fusion.2.refs_0_, bf16[512,1536]{1,0:T(8,128)(2,1)} %collective-permute-done.9.refs_1_.refs_2_.refs_5_, bf16[1536,1920]{1,0:T(8,128)(2,1)} %copy-done.29, ...), custom_call_target="tpu_custom_call" | custom-call | flops 7247757312 | bytes 13148256 | tf_op jit(solution)/shard_map/project/pallas_call | solution.py:358
  125.6 10.9 %project.3 = (bf16[1024,1152]{1,0:T(8,128)(2,1)}, f32[1024,384]{1,0:T(8,128)S(1)}, f32[3,8,1024]{2,1,0:T(8,128)S(1)}) custom-call(s32[2]{0:T(128)S(1)} %pad_add_fusion.half, bf16[512,1536]{1,0:T(8,128)(2,1)} %constant_dynamic-update-slice_fusion.refs_0_.refs_4_.refs_10_, bf16[512,1536]{1,0:T(8,128)(2,1)} %collective-permute-done.10.refs_1_.refs_6_.refs_15_, ...), custom_call_target="tpu_custom_call" | custom-call | flops 7247757312 | bytes 13148256 | tf_op jit(solution)/shard_map/project/pallas_call | solution.py:358
  138.9 16.6 %attend.2 = (f32[1024,384]{1,0:T(8,128)S(1)}, f32[3,8,1024]{2,1,0:T(8,128)S(1)}) custom-call(s32[1]{0:T(128)} %get-tuple-element.307.start, s32[1]{0:T(128)} %get-tuple-element.302.size, bf16[1024,1152]{1,0:T(8,128)(2,1)S(1)} %copy-done.42, bf16[1024,1152]{1,0:T(8,128)(2,1)S(1)} %copy-done.42, bf16[1024,1152]{1,0:T(8,128)(2,1)S(1)} %copy-done.42, ...), custom_call_target="tpu_custom_call" | custom-call | flops 10066329600 | bytes 3932160 | tf_op jit(solution)/shard_map/attend/pallas_call | solution.py:253
  169.5 17.2 %attend.3 = (f32[1024,384]{1,0:T(8,128)S(1)}, f32[3,8,1024]{2,1,0:T(8,128)S(1)}) custom-call(s32[1]{0:T(128)} %get-tuple-element.306.start, s32[1]{0:T(128)} %get-tuple-element.303.size, bf16[1024,1152]{1,0:T(8,128)(2,1)S(1)} %copy-done.44, bf16[1024,1152]{1,0:T(8,128)(2,1)S(1)} %copy-done.44, bf16[1024,1152]{1,0:T(8,128)(2,1)S(1)} %copy-done.44, ...), custom_call_target="tpu_custom_call" | custom-call | flops 10066329600 | bytes 3932160 | tf_op jit(solution)/shard_map/attend/pallas_call | solution.py:253
  193.6 11.2 %collective-permute-done.12 = bf16[512,1536]{1,0:T(8,128)(2,1)S(1)} collective-permute-done((bf16[512,1536]{1,0:T(8,128)(2,1)S(1)}, bf16[512,1536]{1,0:T(8,128)(2,1)S(1)}, u32[]{:S(2)}, u32[]{:S(2)}) %collective-permute-start.12) | collective-permute-done | bytes 1572896 | tf_op jit(solution)/shard_map/ppermute | solution.py:850
  218.7 25.2 %feed.2 = (bf16[1024,1024]{1,0:T(8,128)(2,1)}, bf16[1024,2048]{1,0:T(8,128)(2,1)}, bf16[512,1536]{1,0:T(8,128)(2,1)S(1)}, bf16[512,1536]{1,0:T(8,128)(2,1)S(1)}) custom-call(s32[2]{0:T(128)S(1)} %pad_add_fusion.half, bf16[512,1536]{1,0:T(8,128)(2,1)} %multiply_convert_fusion.refs_0_, bf16[512,1536]{1,0:T(8,128)(2,1)} %collective-permute-done.17.refs_1_.refs_2_, ...), custom_call_target="tpu_custom_call" | custom-call | flops 24159191040 | bytes 25165824 | tf_op jit(solution)/shard_map/feed/pallas_call | solution.py:358
  256.2 25.0 %feed.3 = (bf16[1024,1024]{1,0:T(8,128)(2,1)}, bf16[1024,2048]{1,0:T(8,128)(2,1)}, bf16[512,1536]{1,0:T(8,128)(2,1)S(1)}, bf16[512,1536]{1,0:T(8,128)(2,1)S(1)}) custom-call(s32[2]{0:T(128)S(1)} %pad_add_fusion.half, bf16[512,1536]{1,0:T(8,128)(2,1)} %collective-permute-done.16.refs_0_.refs_4_, bf16[512,1536]{1,0:T(8,128)(2,1)} %copy-done.105, ...), custom_call_target="tpu_custom_call" | custom-call | flops 24159191040 | bytes 25165824 | tf_op jit(solution)/shard_map/feed/pallas_call | solution.py:358
  286.4 28.1 %grad_feed.1 = bf16[1536,3072]{1,0:T(8,128)(2,1)} custom-call(s32[2]{0:T(128)S(1)} %pad_add_fusion.half, bf16[512,1536]{1,0:T(8,128)(2,1)} %multiply_convert_fusion.refs_0_, bf16[1024,2048]{1,0:T(8,128)(2,1)} %get-tuple-element.176.refs_1_.refs_3_, bf16[512,1536]{1,0:T(8,128)(2,1)} %collective-permute-done.17.refs_1_.refs_2_, ...), custom_call_target="tpu_custom_call" | custom-call | flops 28991029248 | bytes 28311552 | tf_op jit(solution)/shard_map/grad_feed/pallas_call | solution.py:539
  314.5 8.3 %collective-permute-done.22.refs_0_ = bf16[512,1536]{1,0:T(8,128)(2,1)} collective-permute-done((bf16[512,1536]{1,0:T(8,128)(2,1)}, bf16[512,1536]{1,0:T(8,128)(2,1)}, u32[]{:S(2)}, u32[]{:S(2)}) %collective-permute-start.22) | collective-permute-done | bytes 1572896 | tf_op jit(solution)/shard_map/ppermute | solution.py:850
  332.4 7.8 %feed_out.2 = (bf16[512,1536]{1,0:T(8,128)(2,1)S(1)}, bf16[512,1536]{1,0:T(8,128)(2,1)}) custom-call(s32[2]{0:T(128)S(1)} %pad_add_fusion.half, bf16[1024,1024]{1,0:T(8,128)(2,1)S(1)} %copy-done.41, bf16[1536,3072]{1,0:T(8,128)(2,1)} %all-gather.2.cloned.1.call-done.refs_4_.w_ref), custom_call_target="tpu_custom_call" | custom-call | flops 4831838208 | bytes 14680064 | tf_op jit(solution)/shard_map/feed_out/pallas_call | solution.py:358
  347.5 29.3 %attend_back.2 = (bf16[1024,384]{1,0:T(8,128)(2,1)S(1)}, bf16[1024,384]{1,0:T(8,128)(2,1)S(1)}, bf16[1024,384]{1,0:T(8,128)(2,1)S(1)}, f32[3,8,1024]{2,1,0:T(8,128)S(1)}) custom-call(s32[1]{0:T(128)} %get-tuple-element.306.start, s32[1]{0:T(128)} %get-tuple-element.303.size, bf16[1024,1152]{1,0:T(8,128)(2,1)S(1)} %copy-done.45, ...), custom_call_target="tpu_custom_call" | custom-call | flops 16357785600 | bytes 7864320 | tf_op jit(solution)/shard_map/attend_back/pallas_call | solution.py:277
  384.1 6.8 %feed_out.3 = (bf16[512,1536]{1,0:T(8,128)(2,1)S(1)}, bf16[512,1536]{1,0:T(8,128)(2,1)S(1)}) custom-call(s32[2]{0:T(128)S(1)} %pad_add_fusion.half, bf16[1024,1024]{1,0:T(8,128)(2,1)S(1)} %copy-done.40, bf16[1536,3072]{1,0:T(8,128)(2,1)} %all-gather.2.cloned.1.call-done.refs_4_.w_ref), custom_call_target="tpu_custom_call" | custom-call | flops 4831838208 | bytes 14680064 | tf_op jit(solution)/shard_map/feed_out/pallas_call | solution.py:358
  398.6 11.0 %grad_gate_out.1 = bf16[1536,768]{1,0:T(8,128)(2,1)} custom-call(s32[2]{0:T(128)S(1)} %pad_add_fusion.half, bf16[512,1536]{1,0:T(8,128)(2,1)} %copy-done.5, bf16[1024,384]{1,0:T(8,128)(2,1)S(1)} %get-tuple-element.194.refs_1_.refs_3_, bf16[512,1536]{1,0:T(8,128)(2,1)} %collective-permute-done.9.refs_1_.refs_2_.refs_5_, ...), custom_call_target="tpu_custom_call" | custom-call | flops 7247757312 | bytes 7077888 | tf_op jit(solution)/shard_map/grad_gate_out/pallas_call | solution.py:539
  419.5 5.6 collective-permute-start.28
  425.1 25.8 %attend_back.3 = (bf16[1024,384]{1,0:T(8,128)(2,1)S(1)}, bf16[1024,384]{1,0:T(8,128)(2,1)S(1)}, bf16[1024,384]{1,0:T(8,128)(2,1)S(1)}, f32[3,8,1024]{2,1,0:T(8,128)S(1)}) custom-call(s32[1]{0:T(128)} %get-tuple-element.307.start, s32[1]{0:T(128)} %get-tuple-element.302.size, bf16[1024,1152]{1,0:T(8,128)(2,1)S(1)} %copy-done.43, ...), custom_call_target="tpu_custom_call" | custom-call | flops 16357785600 | bytes 7864320 | tf_op jit(solution)/shard_map/attend_back/pallas_call | solution.py:277
  452.2 10.8 %project_back.2 = (bf16[512,1536]{1,0:T(8,128)(2,1)S(1)}, bf16[512,1536]{1,0:T(8,128)(2,1)}) custom-call(s32[2]{0:T(128)S(1)} %pad_add_fusion.half, bf16[1024,384]{1,0:T(8,128)(2,1)S(1)} %get-tuple-element.204.refs_0_.refs_11_.refs_16_, bf16[1024,384]{1,0:T(8,128)(2,1)S(1)} %get-tuple-element.205.refs_1_.refs_12_.refs_17_, ...), custom_call_target="tpu_custom_call" | custom-call | flops 7247757312 | bytes 12361728 | tf_op jit(solution)/shard_map/project_back/pallas_call | solution.py:358
  473.8 15.1 %project_grads.1 = bf16[8,208,1152]{2,1,0:T(8,128)(2,1)} custom-call(s32[2]{0:T(128)S(1)} %pad_add_fusion.half, bf16[512,1536]{1,0:T(8,128)(2,1)} %copy-done.5, bf16[1024,384]{1,0:T(8,128)(2,1)S(1)} %copy-done.47, bf16[1024,384]{1,0:T(8,128)(2,1)S(1)} %copy-done.49, bf16[1024,384]{1,0:T(8,128)(2,1)S(1)} %copy-done.51, ...), custom_call_target="tpu_custom_call" | custom-call | flops 10871635968 | bytes 10616832 | tf_op jit(solution)/shard_map/project_grads/pallas_call | solution.py:603
  509.6 10.6 %project_back.3 = (bf16[512,1536]{1,0:T(8,128)(2,1)S(1)}, bf16[512,1536]{1,0:T(8,128)(2,1)}) custom-call(s32[2]{0:T(128)S(1)} %pad_add_fusion.half, bf16[1024,384]{1,0:T(8,128)(2,1)S(1)} %copy-done.47, bf16[1024,384]{1,0:T(8,128)(2,1)S(1)} %copy-done.49, bf16[1024,384]{1,0:T(8,128)(2,1)S(1)} %copy-done.51, bf16[1024,384]{1,0:T(8,128)(2,1)S(1)} %copy-done.35, ...), custom_call_target="tpu_custom_call" | custom-call | flops 7247757312 | bytes 12361728 | tf_op jit(solution)/shard_map/project_back/pallas_call | solution.py:358
  532.1 7.5 %collective-permute-done.42 = bf16[208,1152]{1,0:T(8,128)(2,1)S(1)} collective-permute-done((bf16[208,1152]{1,0:T(8,128)(2,1)S(1)}, bf16[208,1152]{1,0:T(8,128)(2,1)S(1)}, u32[]{:S(2)}, u32[]{:S(2)}) %collective-permute-start.42) | collective-permute-done | bytes 479264 | tf_op jit(solution)/shard_map/ppermute | solution.py:717
  (403 shorter events, 245.7 us)
Async XLA Ops:
  7.2 211.5 %all-gather.2.cloned.1.call-start = ((), (), s32[]{:S(2)}) async-start(), calls=%async_computation.1 | async-start | bytes 10616832 | tf_op jit(solution)/shard_map/all_gather | solution.py:938
  10.4 20.9 %collective-permute-start.2 = (bf16[208,1920]{1,0:T(8,128)(2,1)S(1)}, bf16[208,1920]{1,0:T(8,128)(2,1)S(1)}, u32[]{:S(2)}, u32[]{:S(2)}) collective-permute-start(bf16[208,1920]{1,0:T(8,128)(2,1)S(1)} %fusion.15.refs_0_), channel_id=1, source_target_pairs={{0,4},{8,0},{16,8},{24,16},{28,24},{20,28},{12,20},{4,12},{1,5},{9... | collective-permute-start | bytes 2396168 | tf_op jit(solution)/shard_map/ppermute | solution.py:717
  13.4 19.3 %collective-permute-start.3 = (bf16[208,1920]{1,0:T(8,128)(2,1)S(1)}, bf16[208,1920]{1,0:T(8,128)(2,1)S(1)}, u32[]{:S(2)}, u32[]{:S(2)}) collective-permute-start(bf16[208,1920]{1,0:T(8,128)(2,1)S(1)} %fusion.15.refs_0_), channel_id=1, source_target_pairs={{0,8},{8,16},{16,24},{24,28},{28,20},{20,12},{12,4},{4,0},{1,9},{9... | collective-permute-start | bytes 2396168 | tf_op jit(solution)/shard_map/ppermute | solution.py:717
  32.7 20.7 %collective-permute-start.4 = (bf16[208,1920]{1,0:T(8,128)(2,1)S(1)}, bf16[208,1920]{1,0:T(8,128)(2,1)}, u32[]{:S(2)}, u32[]{:S(2)}) collective-permute-start(bf16[208,1920]{1,0:T(8,128)(2,1)S(1)} %collective-permute-done.2.refs_1_), channel_id=1, source_target_pairs={{0,4},{8,0},{16,8},{24,16},{28,24},{20,28},{12,20},{4,12},{1,5},{9... | collective-permute-start | bytes 2396168 | tf_op jit(solution)/shard_map/ppermute | solution.py:717
  34.3 19.1 %collective-permute-start.5 = (bf16[208,1920]{1,0:T(8,128)(2,1)S(1)}, bf16[208,1920]{1,0:T(8,128)(2,1)}, u32[]{:S(2)}, u32[]{:S(2)}) collective-permute-start(bf16[208,1920]{1,0:T(8,128)(2,1)S(1)} %collective-permute-done.3.refs_7_), channel_id=1, source_target_pairs={{0,8},{8,16},{16,24},{24,28},{28,20},{20,12},{12,4},{4,0},{1,9},{9... | collective-permute-start | bytes 2396168 | tf_op jit(solution)/shard_map/ppermute | solution.py:717
  71.9 485.3 %reduce-scatter.2.cloned.1.call-start = ((), (), s32[]{:S(2)}) async-start(), calls=%async_computation.2 | async-start | bytes 10616832 | tf_op jit(solution)/shard_map/reduce_scatter | solution.py:990
  73.5 39.9 %collective-permute-start.9 = (bf16[512,1536]{1,0:T(8,128)(2,1)S(1)}, bf16[512,1536]{1,0:T(8,128)(2,1)}, u32[]{:S(2)}, u32[]{:S(2)}) collective-permute-start(bf16[512,1536]{1,0:T(8,128)(2,1)S(1)} %fusion.2.refs_0_), channel_id=1, source_target_pairs={{0,1},{1,0},{2,3},{3,2},{4,5},{5,4},{6,7},{7,6},{8,9},{9,8},{10,11... | collective-permute-start | bytes 4718600 | tf_op jit(solution)/shard_map/ppermute | solution.py:850
  73.5 32.4 %collective-permute-start.8 = (bf16[208,1920]{1,0:T(8,128)(2,1)}, bf16[208,1920]{1,0:T(8,128)(2,1)}, u32[]{:S(2)}, u32[]{:S(2)}) collective-permute-start(bf16[208,1920]{1,0:T(8,128)(2,1)} %collective-permute-done.7.refs_5_), channel_id=1, source_target_pairs={{0,8},{8,16},{16,24},{24,28},{28,20},{20,12},{12,4},{4,0},{1,9},{9... | collective-permute-start | bytes 2396168 | tf_op jit(solution)/shard_map/ppermute | solution.py:717
  88.6 37.0 %collective-permute-start.10 = (bf16[512,1536]{1,0:T(8,128)(2,1)}, bf16[512,1536]{1,0:T(8,128)(2,1)}, u32[]{:S(2)}, u32[]{:S(2)}) collective-permute-start(bf16[512,1536]{1,0:T(8,128)(2,1)} %constant_dynamic-update-slice_fusion.refs_0_.refs_4_.refs_10_), channel_id=1, source_target_pairs={{0,1},{1,0},{2,3},{3,2},{4,5},{5,4},{6,7},{7,6},{8,9},{9,8},{10,11... | collective-permute-start | bytes 4718600 | tf_op jit(solution)/shard_map/ppermute | solution.py:850
  90.7 72.4 %collective-permute-start.13 = (bf16[512,1536]{1,0:T(8,128)(2,1)}, bf16[512,1536]{1,0:T(8,128)(2,1)}, u32[]{:S(2)}, u32[]{:S(2)}) collective-permute-start(bf16[512,1536]{1,0:T(8,128)(2,1)} %refs_5_.1), channel_id=1, source_target_pairs={{0,2},{1,3},{2,0},{3,1},{4,6},{5,7},{6,4},{7,5},{8,10},{9,11},{10,... | collective-permute-start | bytes 4718600 | tf_op jit(solution)/shard_map/ppermute | solution.py:850
  168.3 36.5 %collective-permute-start.12 = (bf16[512,1536]{1,0:T(8,128)(2,1)S(1)}, bf16[512,1536]{1,0:T(8,128)(2,1)S(1)}, u32[]{:S(2)}, u32[]{:S(2)}) collective-permute-start(bf16[512,1536]{1,0:T(8,128)(2,1)S(1)} %add_convert_fusion.3), channel_id=1, source_target_pairs={{0,2},{1,3},{2,0},{3,1},{4,6},{5,7},{6,4},{7,5},{8,10},{9,11},{10,... | collective-permute-start | bytes 4718600 | tf_op jit(solution)/shard_map/ppermute | solution.py:850
  213.2 37.0 %collective-permute-start.16 = (bf16[512,1536]{1,0:T(8,128)(2,1)}, bf16[512,1536]{1,0:T(8,128)(2,1)}, u32[]{:S(2)}, u32[]{:S(2)}) collective-permute-start(bf16[512,1536]{1,0:T(8,128)(2,1)} %multiply_convert_fusion.refs_0_), channel_id=1, source_target_pairs={{0,2},{1,3},{2,0},{3,1},{4,6},{5,7},{6,4},{7,5},{8,10},{9,11},{10,... | collective-permute-start | bytes 4718600 | tf_op jit(solution)/shard_map/ppermute | solution.py:850
  286.1 36.8 %collective-permute-start.22 = (bf16[512,1536]{1,0:T(8,128)(2,1)}, bf16[512,1536]{1,0:T(8,128)(2,1)}, u32[]{:S(2)}, u32[]{:S(2)}) collective-permute-start(bf16[512,1536]{1,0:T(8,128)(2,1)} %add_convert_fusion.2), channel_id=1, source_target_pairs={{0,2},{1,3},{2,0},{3,1},{4,6},{5,7},{6,4},{7,5},{8,10},{9,11},{10,... | collective-permute-start | bytes 4718600 | tf_op jit(solution)/shard_map/ppermute | solution.py:850
  332.1 47.3 %collective-permute-start.24 = (bf16[512,1536]{1,0:T(8,128)(2,1)S(1)}, bf16[512,1536]{1,0:T(8,128)(2,1)}, u32[]{:S(2)}, u32[]{:S(2)}) collective-permute-start(bf16[512,1536]{1,0:T(8,128)(2,1)S(1)} %get-tuple-element.184.refs_0_.refs_8_), channel_id=1, source_target_pairs={{0,2},{1,3},{2,0},{3,1},{4,6},{5,7},{6,4},{7,5},{8,10},{9,11},{10,... | collective-permute-start | bytes 4718600 | tf_op jit(solution)/shard_map/ppermute | solution.py:850
  383.0 26.5 %collective-permute-start.26 = (bf16[512,1536]{1,0:T(8,128)(2,1)}, bf16[512,1536]{1,0:T(8,128)(2,1)}, u32[]{:S(2)}, u32[]{:S(2)}) collective-permute-start(bf16[512,1536]{1,0:T(8,128)(2,1)} %get-tuple-element.201), channel_id=1, source_target_pairs={{0,1},{1,0},{2,3},{3,2},{4,5},{5,4},{6,7},{7,6},{8,9},{9,8},{10,11... | collective-permute-start | bytes 4718600 | tf_op jit(solution)/shard_map/ppermute | solution.py:850
  411.5 39.4 %collective-permute-start.29 = (bf16[512,1536]{1,0:T(8,128)(2,1)S(1)}, bf16[512,1536]{1,0:T(8,128)(2,1)S(1)}, u32[]{:S(2)}, u32[]{:S(2)}) collective-permute-start(bf16[512,1536]{1,0:T(8,128)(2,1)S(1)} %add_convert_fusion.1), channel_id=1, source_target_pairs={{0,2},{1,3},{2,0},{3,1},{4,6},{5,7},{6,4},{7,5},{8,10},{9,11},{10,... | collective-permute-start | bytes 4718600 | tf_op jit(solution)/shard_map/ppermute | solution.py:850
  414.0 36.9 %collective-permute-start.27 = (bf16[192,768]{1,0:T(8,128)(2,1)S(1)}, bf16[192,768]{1,0:T(8,128)(2,1)S(1)}, u32[]{:S(2)}, u32[]{:S(2)}) collective-permute-start(bf16[192,768]{1,0:T(8,128)(2,1)S(1)} %get-tuple-element.282), channel_id=1, source_target_pairs={{0,8},{8,16},{16,24},{24,28},{28,20},{20,12},{12,4},{4,0},{1,9},{9... | collective-permute-start | bytes 884744 | tf_op jit(solution)/shard_map/ppermute | solution.py:717
  419.5 31.4 %collective-permute-start.28 = (bf16[192,768]{1,0:T(8,128)(2,1)S(1)}, bf16[192,768]{1,0:T(8,128)(2,1)S(1)}, u32[]{:S(2)}, u32[]{:S(2)}) collective-permute-start(bf16[192,768]{1,0:T(8,128)(2,1)S(1)} %get-tuple-element.281), channel_id=1, source_target_pairs={{0,4},{8,0},{16,8},{24,16},{28,24},{20,28},{12,20},{4,12},{1,5},{9... | collective-permute-start | bytes 884744 | tf_op jit(solution)/shard_map/ppermute | solution.py:717
  465.3 23.6 %collective-permute-start.32 = (bf16[192,768]{1,0:T(8,128)(2,1)}, bf16[192,768]{1,0:T(8,128)(2,1)S(1)}, u32[]{:S(2)}, u32[]{:S(2)}) collective-permute-start(bf16[192,768]{1,0:T(8,128)(2,1)} %get-tuple-element.280), channel_id=1, source_target_pairs={{0,8},{8,16},{16,24},{24,28},{28,20},{20,12},{12,4},{4,0},{1,9},{9... | collective-permute-start | bytes 884744 | tf_op jit(solution)/shard_map/ppermute | solution.py:717
  467.3 27.2 %collective-permute-start.33 = (bf16[192,768]{1,0:T(8,128)(2,1)}, bf16[192,768]{1,0:T(8,128)(2,1)S(1)}, u32[]{:S(2)}, u32[]{:S(2)}) collective-permute-start(bf16[192,768]{1,0:T(8,128)(2,1)} %get-tuple-element.279), channel_id=1, source_target_pairs={{0,4},{8,0},{16,8},{24,16},{28,24},{20,28},{12,20},{4,12},{1,5},{9... | collective-permute-start | bytes 884744 | tf_op jit(solution)/shard_map/ppermute | solution.py:717
  472.0 22.5 %collective-permute-start.31 = (bf16[256,1536]{1,0:T(8,128)(2,1)S(1)}, bf16[256,1536]{1,0:T(8,128)(2,1)S(1)}, u32[]{:S(2)}, u32[]{:S(2)}) collective-permute-start(bf16[256,1536]{1,0:T(8,128)(2,1)S(1)} %get-tuple-element.284), channel_id=1, source_target_pairs={{0,2},{1,3},{2,0},{3,1},{4,6},{5,7},{6,4},{7,5},{8,10},{9,11},{10,... | collective-permute-start | bytes 2359304 | tf_op jit(solution)/shard_map/ppermute | solution.py:850
  499.1 30.3 %collective-permute-start.34 = (bf16[512,1536]{1,0:T(8,128)(2,1)S(1)}, bf16[512,1536]{1,0:T(8,128)(2,1)S(1)}, u32[]{:S(2)}, u32[]{:S(2)}) collective-permute-start(bf16[512,1536]{1,0:T(8,128)(2,1)S(1)} %copy-done.33), channel_id=1, source_target_pairs={{0,1},{1,0},{2,3},{3,2},{4,5},{5,4},{6,7},{7,6},{8,9},{9,8},{10,11... | collective-permute-start | bytes 4718600 | tf_op jit(solution)/shard_map/ppermute | solution.py:850
  501.6 27.7 %collective-permute-start.35 = (bf16[256,1536]{1,0:T(8,128)(2,1)S(1)}, bf16[256,1536]{1,0:T(8,128)(2,1)S(1)}, u32[]{:S(2)}, u32[]{:S(2)}) collective-permute-start(bf16[256,1536]{1,0:T(8,128)(2,1)S(1)} %get-tuple-element.222), channel_id=1, source_target_pairs={{0,2},{1,3},{2,0},{3,1},{4,6},{5,7},{6,4},{7,5},{8,10},{9,11},{10,... | collective-permute-start | bytes 2359304 | tf_op jit(solution)/shard_map/ppermute | solution.py:850
  505.8 18.5 %collective-permute-start.40 = (bf16[208,1152]{1,0:T(8,128)(2,1)S(1)}, bf16[208,1152]{1,0:T(8,128)(2,1)}, u32[]{:S(2)}, u32[]{:S(2)}) collective-permute-start(bf16[208,1152]{1,0:T(8,128)(2,1)S(1)} %get-tuple-element.276), channel_id=1, source_target_pairs={{0,4},{8,0},{16,8},{24,16},{28,24},{20,28},{12,20},{4,12},{1,5},{9... | collective-permute-start | bytes 1437704 | tf_op jit(solution)/shard_map/ppermute | solution.py:717
  (136 other events, 1200.1 us)
Sparse Core Ops, SparseCore 0:
  72.0 146.7 all-gather.1
  323.0 181.0 reduce-scatter.1
